TPU v7x, 32 devices: a whole 2x2x4 slice. The times are simulated.
32 devices in a mesh: fsdp: 4 (over y, x), seq: 8 (over z, core).
Axes of the slice: x: 2, y: 2, z: 4, core: 2. Of those that a mesh axis runs over, the one named last changes fastest.
Arguments:
- layer_input: bfloat16 [8, 1024, 1024], P('fsdp', 'seq'), may hold values from -8 to 8
- documents: int32 [8, 1024], P('fsdp', 'seq'), may hold values from 0 to 5, as said below
- cotangent: bfloat16 [8, 1024, 1024], P('fsdp', 'seq'), may hold values from -6 to 6
- attend_weight: float32 [2, 3, 1024, 1024], P(None, None, ('fsdp', 'seq')), may hold values from -0.25 to 0.25
- attend_bias: float32 [2, 2, 1024], P(None, None, ('fsdp', 'seq')), may hold values from -3 to 3
- output_weight: float32 [2, 1024, 1024], P(None, ('fsdp', 'seq')), may hold values from -0.5 to 0.5
- output_bias: float32 [2, 1024], P(None, ('fsdp', 'seq')), may hold values from -3 to 3
- norm_gain: float32 [2, 2, 1024], P(None, None, ('fsdp', 'seq')), may hold values from 0.25 to 1.75
- norm_shift: float32 [2, 2, 1024], P(None, None, ('fsdp', 'seq')), may hold values from -1.75 to 1.75
- expand_weight: float32 [2, 1024, 4096], P(None, ('fsdp', 'seq')), may hold values from -0.1875 to 0.1875
- expand_bias: float32 [2, 4096], P(None, ('fsdp', 'seq')), may hold values from -3 to 3
- reduce_weight: float32 [2, 4096, 1024], P(None, ('fsdp', 'seq')), may hold values from -0.09375 to 0.09375
- reduce_bias: float32 [2, 1024], P(None, ('fsdp', 'seq')), may hold values from -3 to 3
Outputs:
- layer_output: bfloat16 [8, 1024, 1024], P('fsdp', 'seq')
- input_gradient: float32 [8, 1024, 1024], P('fsdp', 'seq')
- attend_weight_grad: float32 [2, 3, 1024, 1024], P(None, None, ('fsdp', 'seq'))
- attend_bias_grad: float32 [2, 2, 1024], P(None, None, ('fsdp', 'seq'))
- output_weight_grad: float32 [2, 1024, 1024], P(None, ('fsdp', 'seq'))
- output_bias_grad: float32 [2, 1024], P(None, ('fsdp', 'seq'))
- norm_gain_grad: float32 [2, 2, 1024], P(None, None, ('fsdp', 'seq'))
- norm_shift_grad: float32 [2, 2, 1024], P(None, None, ('fsdp', 'seq'))
- expand_weight_grad: float32 [2, 1024, 4096], P(None, ('fsdp', 'seq'))
- expand_bias_grad: float32 [2, 4096], P(None, ('fsdp', 'seq'))
- reduce_weight_grad: float32 [2, 4096, 1024], P(None, ('fsdp', 'seq'))
- reduce_bias_grad: float32 [2, 1024], P(None, ('fsdp', 'seq'))
Inputs may be any that keep to these rules, and one draw needn't show every extreme that they name: In each sequence the numbers start at 0 and rise by one at the start of each document. Of the 2 sequences on each index of fsdp, one has a first document of fewer than 128 tokens and a second that runs to the sequence's end, so that it has 897 to 1023 tokens and is not bounded by 1500; another is made of documents of exactly 200 tokens. Every other document has 200 to 1500 tokens, except that the last of a sequence is cut at the sequence's end.
All inputs are finite; a program needn't handle non-finite values.
Results may differ from a plain program's by a relative error of at most 0.035.
The roundings to bfloat16 on the way count: a program that leaves them out, or rounds other values in their place, can miss the bound.
Values may be sent and summed in bfloat16 or wider, within the bound.
No kernel may reach another device: no remote copies, remote signals or barrier semaphores. Data moves between devices by JAX's collectives and lax.ppermute only.
A program may use at most 320 MiB of HBM per device.

v0:
```python
import jax
import jax.numpy as jnp
from jax import lax
from jax.sharding import PartitionSpec as P

HEAD = 64


EPSILON = 1e-05
NEG_FILL = -1e30


def matmul(left_side, right_side):
    return jnp.dot(left_side, right_side, preferred_element_type=jnp.float32)


def layer_norm(token_rows, gain_row, shift_row):
    mean_row = jnp.mean(token_rows, axis=-1, keepdims=True)
    centred = token_rows - mean_row
    variance = jnp.mean(centred * centred, axis=-1, keepdims=True)
    return centred * lax.rsqrt(variance + EPSILON) * gain_row + shift_row


def gelu_exact(values_in):
    return jax.nn.gelu(values_in, approximate=False)


def gather_weights(shards):
    (
        attend_weight,
        attend_bias,
        output_weight,
        output_bias,
        norm_gain,
        norm_shift,
        expand_weight,
        expand_bias,
        reduce_weight,
        reduce_bias,
    ) = shards
    return (
        lax.all_gather(attend_weight, ("fsdp", "seq"), axis=1, tiled=True),
        lax.all_gather(attend_bias, ("fsdp", "seq"), axis=1, tiled=True),
        lax.all_gather(output_weight, ("fsdp", "seq"), axis=0, tiled=True),
        lax.all_gather(output_bias, ("fsdp", "seq"), axis=0, tiled=True),
        lax.all_gather(norm_gain, ("fsdp", "seq"), axis=1, tiled=True),
        lax.all_gather(norm_shift, ("fsdp", "seq"), axis=1, tiled=True),
        lax.all_gather(expand_weight, ("fsdp", "seq"), axis=0, tiled=True),
        lax.all_gather(expand_bias, ("fsdp", "seq"), axis=0, tiled=True),
        lax.all_gather(reduce_weight, ("fsdp", "seq"), axis=0, tiled=True),
        lax.all_gather(reduce_bias, ("fsdp", "seq"), axis=0, tiled=True),
    )


def gather_weights_again(shards):
    (
        attend_weight,
        attend_bias,
        output_weight,
        output_bias,
        norm_gain,
        norm_shift,
        expand_weight,
        expand_bias,
        reduce_weight,
        reduce_bias,
    ) = shards
    return (
        lax.all_gather(attend_weight, ("fsdp", "seq"), axis=1, tiled=True),
        lax.all_gather(attend_bias, ("fsdp", "seq"), axis=1, tiled=True),
        lax.all_gather(output_weight, ("fsdp", "seq"), axis=0, tiled=True),
        lax.all_gather(output_bias, ("fsdp", "seq"), axis=0, tiled=True),
        lax.all_gather(norm_gain, ("fsdp", "seq"), axis=1, tiled=True),
        lax.all_gather(norm_shift, ("fsdp", "seq"), axis=1, tiled=True),
        lax.all_gather(expand_weight, ("fsdp", "seq"), axis=0, tiled=True),
        lax.all_gather(expand_bias, ("fsdp", "seq"), axis=0, tiled=True),
        lax.all_gather(reduce_weight, ("fsdp", "seq"), axis=0, tiled=True),
        lax.all_gather(reduce_bias, ("fsdp", "seq"), axis=0, tiled=True),
    )


def scatter_stacked(gradients):
    (
        attend_weight,
        attend_bias,
        output_weight,
        output_bias,
        norm_gain,
        norm_shift,
        expand_weight,
        expand_bias,
        reduce_weight,
        reduce_bias,
    ) = gradients
    return (
        lax.psum_scatter(attend_weight, ("fsdp", "seq"), scatter_dimension=2, tiled=True),
        lax.psum_scatter(attend_bias, ("fsdp", "seq"), scatter_dimension=2, tiled=True),
        lax.psum_scatter(output_weight, ("fsdp", "seq"), scatter_dimension=1, tiled=True),
        lax.psum_scatter(output_bias, ("fsdp", "seq"), scatter_dimension=1, tiled=True),
        lax.psum_scatter(norm_gain, ("fsdp", "seq"), scatter_dimension=2, tiled=True),
        lax.psum_scatter(norm_shift, ("fsdp", "seq"), scatter_dimension=2, tiled=True),
        lax.psum_scatter(expand_weight, ("fsdp", "seq"), scatter_dimension=1, tiled=True),
        lax.psum_scatter(expand_bias, ("fsdp", "seq"), scatter_dimension=1, tiled=True),
        lax.psum_scatter(reduce_weight, ("fsdp", "seq"), scatter_dimension=1, tiled=True),
        lax.psum_scatter(reduce_bias, ("fsdp", "seq"), scatter_dimension=1, tiled=True),
    )


def attend_forward(query_heads, key_heads, value_heads, segments_full):
    seq_count, length, local_width = query_heads.shape
    heads_here = local_width // HEAD
    block_rows = min(512, length)
    block_count = length // block_rows
    scale_factor = HEAD ** (-0.5)

    def one_sequence(pieces):
        query_seq, key_seq, value_seq, segment_seq = pieces
        key_split = key_seq.reshape(length, heads_here, HEAD)
        value_split = value_seq.reshape(length, heads_here, HEAD)

        def one_block(block_pieces):
            query_part, segment_part = block_pieces
            scores = (
                jnp.einsum(
                    "qhd,khd->hqk", query_part, key_split, preferred_element_type=jnp.float32
                )
                * scale_factor
            )
            allowed = segment_part[:, None] == segment_seq[None, :]
            scores = jnp.where(allowed[None], scores, NEG_FILL)
            row_top = jnp.max(scores, axis=-1, keepdims=True)
            exponent = jnp.exp(scores - row_top)
            row_total = jnp.sum(exponent, axis=-1, keepdims=True)
            soft_low = (exponent / row_total).astype(jnp.bfloat16)
            context = jnp.einsum(
                "hqk,khd->qhd", soft_low, value_split, preferred_element_type=jnp.float32
            )
            return (context.astype(jnp.bfloat16), (row_top + jnp.log(row_total))[..., 0])

        contexts, log_totals = lax.map(
            one_block,
            (
                query_seq.reshape(block_count, block_rows, heads_here, HEAD),
                segment_seq.reshape(block_count, block_rows),
            ),
        )
        return (contexts.reshape(length, local_width), log_totals)

    return lax.map(one_sequence, (query_heads, key_heads, value_heads, segments_full))


def attend_backward(grad_heads, query_heads, key_heads, value_heads, log_totals, segments_full):
    seq_count, length, local_width = query_heads.shape
    heads_here = local_width // HEAD
    block_rows = min(512, length)
    block_count = length // block_rows
    scale_factor = HEAD ** (-0.5)

    def one_sequence(pieces):
        grad_seq, query_seq, key_seq, value_seq, log_seq, segment_seq = pieces
        key_split = key_seq.reshape(length, heads_here, HEAD)
        value_split = value_seq.reshape(length, heads_here, HEAD)

        def one_block(running, block_pieces):
            grad_key_sum, grad_value_sum = running
            query_part, grad_part, log_part, segment_part = block_pieces
            scores = (
                jnp.einsum(
                    "qhd,khd->hqk", query_part, key_split, preferred_element_type=jnp.float32
                )
                * scale_factor
            )
            allowed = segment_part[:, None] == segment_seq[None, :]
            scores = jnp.where(allowed[None], scores, NEG_FILL)
            soft_probs = jnp.exp(scores - log_part[..., None])
            soft_low = soft_probs.astype(jnp.bfloat16)
            grad_value_sum = grad_value_sum + jnp.einsum(
                "hqk,qhd->khd", soft_low, grad_part, preferred_element_type=jnp.float32
            )
            grad_soft = jnp.einsum(
                "qhd,khd->hqk", grad_part, value_split, preferred_element_type=jnp.float32
            )
            grad_scores = soft_probs * (
                grad_soft - jnp.sum(soft_probs * grad_soft, axis=-1, keepdims=True)
            )
            grad_low = grad_scores.astype(jnp.bfloat16)
            grad_query = (
                jnp.einsum("hqk,khd->qhd", grad_low, key_split, preferred_element_type=jnp.float32)
                * scale_factor
            )
            grad_key_sum = (
                grad_key_sum
                + jnp.einsum(
                    "hqk,qhd->khd", grad_low, query_part, preferred_element_type=jnp.float32
                )
                * scale_factor
            )
            return ((grad_key_sum, grad_value_sum), grad_query.astype(jnp.bfloat16))

        zeros_start = jnp.zeros((length, heads_here, HEAD), jnp.float32)
        (grad_key_sum, grad_value_sum), grad_queries = lax.scan(
            one_block,
            (zeros_start, zeros_start),
            (
                query_seq.reshape(block_count, block_rows, heads_here, HEAD),
                grad_seq.reshape(block_count, block_rows, heads_here, HEAD),
                log_seq,
                segment_seq.reshape(block_count, block_rows),
            ),
        )
        return (
            grad_queries.reshape(length, local_width),
            grad_key_sum.astype(jnp.bfloat16).reshape(length, local_width),
            grad_value_sum.astype(jnp.bfloat16).reshape(length, local_width),
        )

    return lax.map(
        one_sequence, (grad_heads, query_heads, key_heads, value_heads, log_totals, segments_full)
    )


def forward_layer(rows_in, rows_low, weights, segments_full):
    (
        attend_weight,
        attend_bias,
        output_weight,
        output_bias,
        norm_gain,
        norm_shift,
        expand_weight,
        expand_bias,
        reduce_weight,
        reduce_bias,
    ) = weights
    seq_count = segments_full.shape[0]
    token_count, model_width = rows_in.shape
    local_shape = (seq_count, token_count // seq_count, model_width)
    query_rows = (
        (matmul(rows_low, attend_weight[0]) + attend_bias[0])
        .astype(jnp.bfloat16)
        .reshape(local_shape)
    )
    key_rows = matmul(rows_low, attend_weight[1]).astype(jnp.bfloat16).reshape(local_shape)
    value_rows = (
        (matmul(rows_low, attend_weight[2]) + attend_bias[1])
        .astype(jnp.bfloat16)
        .reshape(local_shape)
    )
    query_heads, key_heads, value_heads = (
        lax.all_to_all(query_rows, "seq", split_axis=2, concat_axis=1, tiled=True),
        lax.all_to_all(key_rows, "seq", split_axis=2, concat_axis=1, tiled=True),
        lax.all_to_all(value_rows, "seq", split_axis=2, concat_axis=1, tiled=True),
    )
    context_heads, log_totals = attend_forward(query_heads, key_heads, value_heads, segments_full)
    context_rows = lax.all_to_all(
        context_heads, "seq", split_axis=1, concat_axis=2, tiled=True
    ).reshape(token_count, model_width)
    branch = matmul(context_rows, output_weight) + output_bias
    first_sum = rows_in + branch
    first_norm = layer_norm(first_sum, norm_gain[0], norm_shift[0])
    first_low = first_norm.astype(jnp.bfloat16)
    expanded = matmul(first_low, expand_weight) + expand_bias
    activated_low = gelu_exact(expanded).astype(jnp.bfloat16)
    second_sum = first_norm + (matmul(activated_low, reduce_weight) + reduce_bias)
    output_rows = layer_norm(second_sum, norm_gain[1], norm_shift[1])
    kept_state = (
        rows_low,
        query_heads,
        key_heads,
        value_heads,
        log_totals,
        context_rows,
        first_sum,
        first_low,
        expanded,
        activated_low,
        second_sum,
    )
    return (output_rows, kept_state)


def backward_layer(grad_output, kept_state, weights, segments_full):
    (
        rows_low,
        query_heads,
        key_heads,
        value_heads,
        log_totals,
        context_rows,
        first_sum,
        first_low,
        expanded,
        activated_low,
        second_sum,
    ) = kept_state
    (
        attend_weight,
        attend_bias,
        output_weight,
        output_bias,
        norm_gain,
        norm_shift,
        expand_weight,
        expand_bias,
        reduce_weight,
        reduce_bias,
    ) = weights
    seq_count = segments_full.shape[0]
    token_count, model_width = grad_output.shape
    local_shape = (seq_count, token_count // seq_count, model_width)
    gain_float = norm_gain.astype(jnp.float32)
    shift_float = norm_shift.astype(jnp.float32)
    second_pull = jax.vjp(layer_norm, second_sum, gain_float[1], shift_float[1])[1]
    grad_second, grad_gain_second, grad_shift_second = second_pull(grad_output)
    grad_reduced = grad_second.astype(jnp.bfloat16)
    grad_reduce_weight = jnp.einsum(
        "rf,rd->fd", activated_low, grad_reduced, preferred_element_type=jnp.float32
    )
    grad_reduce_bias = jnp.sum(grad_reduced, axis=0, dtype=jnp.float32)
    grad_activated = jnp.einsum(
        "rd,fd->rf", grad_reduced, reduce_weight, preferred_element_type=jnp.float32
    )
    gelu_pull = jax.vjp(gelu_exact, expanded)[1]
    grad_expanded = gelu_pull(grad_activated)[0].astype(jnp.bfloat16)
    grad_expand_weight = jnp.einsum(
        "rd,rf->df", first_low, grad_expanded, preferred_element_type=jnp.float32
    )
    grad_expand_bias = jnp.sum(grad_expanded, axis=0, dtype=jnp.float32)
    grad_first = grad_second + jnp.einsum(
        "rf,df->rd", grad_expanded, expand_weight, preferred_element_type=jnp.float32
    )
    first_pull = jax.vjp(layer_norm, first_sum, gain_float[0], shift_float[0])[1]
    grad_first_sum, grad_gain_first, grad_shift_first = first_pull(grad_first)
    grad_branch = grad_first_sum.astype(jnp.bfloat16)
    grad_output_weight = jnp.einsum(
        "rd,re->de", context_rows, grad_branch, preferred_element_type=jnp.float32
    )
    grad_output_bias = jnp.sum(grad_branch, axis=0, dtype=jnp.float32)
    grad_context = jnp.einsum(
        "re,de->rd", grad_branch, output_weight, preferred_element_type=jnp.float32
    )
    grad_context = grad_context.astype(jnp.bfloat16).reshape(local_shape)
    grad_heads = lax.all_to_all(grad_context, "seq", split_axis=2, concat_axis=1, tiled=True)
    grad_query_heads, grad_key_heads, grad_value_heads = attend_backward(
        grad_heads, query_heads, key_heads, value_heads, log_totals, segments_full
    )
    grad_query_rows, grad_key_rows, grad_value_rows = (
        lax.all_to_all(grad_query_heads, "seq", split_axis=1, concat_axis=2, tiled=True),
        lax.all_to_all(grad_key_heads, "seq", split_axis=1, concat_axis=2, tiled=True),
        lax.all_to_all(grad_value_heads, "seq", split_axis=1, concat_axis=2, tiled=True),
    )
    grad_projected = jnp.stack([grad_query_rows, grad_key_rows, grad_value_rows]).reshape(
        3, token_count, model_width
    )
    grad_attend_weight = jnp.einsum(
        "rd,tre->tde", rows_low, grad_projected, preferred_element_type=jnp.float32
    )
    grad_attend_bias = jnp.stack(
        [
            jnp.sum(grad_projected[0], axis=0, dtype=jnp.float32),
            jnp.sum(grad_projected[2], axis=0, dtype=jnp.float32),
        ]
    )
    grad_input = grad_first_sum + jnp.einsum(
        "tre,tde->rd", grad_projected, attend_weight, preferred_element_type=jnp.float32
    )
    grad_gains = jnp.stack([grad_gain_first, grad_gain_second])
    grad_shifts = jnp.stack([grad_shift_first, grad_shift_second])
    gradients = (
        grad_attend_weight,
        grad_attend_bias,
        grad_output_weight,
        grad_output_bias,
        grad_gains,
        grad_shifts,
        grad_expand_weight,
        grad_expand_bias,
        grad_reduce_weight,
        grad_reduce_bias,
    )
    return (grad_input, gradients)


def body(
    layer_input,
    documents,
    cotangent,
    attend_weight,
    attend_bias,
    output_weight,
    output_bias,
    norm_gain,
    norm_shift,
    expand_weight,
    expand_bias,
    reduce_weight,
    reduce_bias,
):
    params = (
        attend_weight,
        attend_bias,
        output_weight,
        output_bias,
        norm_gain,
        norm_shift,
        expand_weight,
        expand_bias,
        reduce_weight,
        reduce_bias,
    )
    layer_count = attend_weight.shape[0]
    seq_count, token_here, model_width = layer_input.shape
    segments_full = lax.all_gather(documents, "seq", axis=1, tiled=True)
    rows_low = layer_input.reshape(seq_count * token_here, model_width)
    rows_in = rows_low.astype(jnp.float32)
    kept_layers = []
    gathered_layers = []
    for layer_index in range(layer_count):
        weights = gather_weights(
            tuple((weight_item[layer_index].astype(jnp.bfloat16) for weight_item in params))
        )
        rows_in, kept_state = forward_layer(rows_in, rows_low, weights, segments_full)
        rows_low = rows_in.astype(jnp.bfloat16)
        kept_layers.append(kept_state)
        gathered_layers.append(weights)
    layer_output = rows_low.reshape(seq_count, token_here, model_width)
    grad_rows = cotangent.reshape(seq_count * token_here, model_width).astype(jnp.float32)
    gradient_store = ()
    for layer_index in reversed(range(layer_count)):
        weights = gather_weights_again(
            tuple((weight_item[layer_index].astype(jnp.bfloat16) for weight_item in params))
        )
        grad_rows, gradients = backward_layer(
            grad_rows, kept_layers[layer_index], weights, segments_full
        )
        if layer_index == layer_count - 1:
            gradient_store = tuple(
                (
                    jnp.zeros((layer_count,) + member_grad.shape, jnp.float32)
                    for member_grad in gradients
                )
            )
        gradient_store = tuple(
            (
                store_item.at[layer_index].set(member_grad)
                for store_item, member_grad in zip(gradient_store, gradients)
            )
        )
    result_grads = scatter_stacked(gradient_store)
    input_gradient = grad_rows.reshape(seq_count, token_here, model_width)
    return (layer_output, input_gradient) + tuple(result_grads)


def solution(mesh):
    placed = (
        P("fsdp", "seq", None),
        P("fsdp", "seq"),
        P("fsdp", "seq", None),
        P(None, None, ("fsdp", "seq"), None),
        P(None, None, ("fsdp", "seq")),
        P(None, ("fsdp", "seq"), None),
        P(None, ("fsdp", "seq")),
        P(None, None, ("fsdp", "seq")),
        P(None, None, ("fsdp", "seq")),
        P(None, ("fsdp", "seq"), None),
        P(None, ("fsdp", "seq")),
        P(None, ("fsdp", "seq"), None),
        P(None, ("fsdp", "seq")),
    )
    return jax.shard_map(
        body,
        mesh=mesh,
        in_specs=placed,
        out_specs=(
            P("fsdp", "seq", None),
            P("fsdp", "seq", None),
            P(None, None, ("fsdp", "seq"), None),
            P(None, None, ("fsdp", "seq")),
            P(None, ("fsdp", "seq"), None),
            P(None, ("fsdp", "seq")),
            P(None, None, ("fsdp", "seq")),
            P(None, None, ("fsdp", "seq")),
            P(None, ("fsdp", "seq"), None),
            P(None, ("fsdp", "seq")),
            P(None, ("fsdp", "seq"), None),
            P(None, ("fsdp", "seq")),
        ),
        check_vma=False,
    )
```

profile of v0, /device:TPU:0, one launch (start us, length us, event | category | flops | bytes accessed | tf_op | source)
XLA Modules:
  0.0 3141.0 jit_solution(8736066258796125641)
XLA Ops:
  16.1 46.6 %all-gather.1 = bf16[1,2,1024]{1,0,2:T(2,128)(2,1)S(1)} all-gather(bf16[1,2,32]{1,0,2:T(2,128)(2,1)S(1)} %get-tuple-element.1137), channel_id=3, replica_groups=mesh['fsdp'=4,'seq'=8] {'fsdp','seq'}, dimensions={2}, use_global_device_ids=true | all-gather | bytes 4224 | tf_op jit(solution)/shard_map/all_gather | solution.py:43
  135.2 40.2 %all-reduce.5 = (bf16[1024]{0:T(1024)(128)(2,1)S(1)}, bf16[1024]{0:T(1024)(128)(2,1)S(1)}, bf16[1024]{0:T(1024)(128)(2,1)}, bf16[1024]{0:T(1024)(128)(2,1)}) all-reduce(bf16[1024]{0:T(1024)(128)(2,1)S(1)} %dynamic-update-slice.60, bf16[1024]{0:T(1024)(128)(2,1)S(1)} %dynamic-update-slice.61, ...), channel_id=5, replica_groups=mesh['fsdp'=4,'seq'=8] {'fsdp','seq'}, use_global_device_ids=true, to_apply=%add | all-reduce | flops 4096 | bytes 16384
  176.5 41.1 %all-gather.7 = bf16[1,4096]{1,0:T(2,128)(2,1)S(1)} all-gather(bf16[1,128]{1,0:T(2,128)(2,1)S(1)} %get-tuple-element.1142), channel_id=9, replica_groups=mesh['fsdp'=4,'seq'=8] {'fsdp','seq'}, dimensions={1}, use_global_device_ids=true | all-gather | bytes 8448 | tf_op jit(solution)/shard_map/all_gather | solution.py:49
  220.3 42.8 %all-gather.5 = bf16[1,2,1024]{1,0,2:T(2,128)(2,1)} all-gather(bf16[1,2,32]{1,0,2:T(2,128)(2,1)S(1)} %get-tuple-element.1135), channel_id=7, replica_groups=mesh['fsdp'=4,'seq'=8] {'fsdp','seq'}, dimensions={2}, use_global_device_ids=true | all-gather | bytes 4224 | tf_op jit(solution)/shard_map/all_gather | solution.py:47
  275.4 22.1 while.127
  304.0 48.9 %all-gather.4 = bf16[1,2,1024]{1,0,2:T(2,128)(2,1)S(1)} all-gather(bf16[1,2,32]{1,0,2:T(2,128)(2,1)S(1)} %get-tuple-element.1133), channel_id=6, replica_groups=mesh['fsdp'=4,'seq'=8] {'fsdp','seq'}, dimensions={2}, use_global_device_ids=true | all-gather | bytes 4224 | tf_op jit(solution)/shard_map/all_gather | solution.py:46
  352.9 42.0 %all-gather.11 = bf16[1,2,1024]{1,0,2:T(2,128)(2,1)S(1)} all-gather(bf16[1,2,32]{1,0,2:T(2,128)(2,1)S(1)} %copy-done.73), channel_id=13, replica_groups=mesh['fsdp'=4,'seq'=8] {'fsdp','seq'}, dimensions={2}, use_global_device_ids=true | all-gather | bytes 4224 | tf_op jit(solution)/shard_map/all_gather | solution.py:43
  419.5 16.1 multiply_convert_fusion.3
  454.0 15.8 all-to-all-done.4
  477.5 16.7 all-to-all-done.5
  499.1 21.1 all-to-all-done.6
  520.8 20.8 while.129
  546.3 49.8 %all-gather.17 = bf16[1,4096]{1,0:T(2,128)(2,1)S(1)} all-gather(bf16[1,128]{1,0:T(2,128)(2,1)S(1)} %copy-done.124), channel_id=19, replica_groups=mesh['fsdp'=4,'seq'=8] {'fsdp','seq'}, dimensions={1}, use_global_device_ids=true | all-gather | bytes 8448 | tf_op jit(solution)/shard_map/all_gather | solution.py:49
  596.2 40.5 %all-gather.14 = bf16[1,2,1024]{1,0,2:T(2,128)(2,1)S(1)} all-gather(bf16[1,2,32]{1,0,2:T(2,128)(2,1)S(1)} %copy-done.74), channel_id=16, replica_groups=mesh['fsdp'=4,'seq'=8] {'fsdp','seq'}, dimensions={2}, use_global_device_ids=true | all-gather | bytes 4224 | tf_op jit(solution)/shard_map/all_gather | solution.py:46
  637.3 40.5 %all-gather.15 = bf16[1,2,1024]{1,0,2:T(2,128)(2,1)S(1)} all-gather(bf16[1,2,32]{1,0,2:T(2,128)(2,1)S(1)} %copy-done.72), channel_id=17, replica_groups=mesh['fsdp'=4,'seq'=8] {'fsdp','seq'}, dimensions={2}, use_global_device_ids=true | all-gather | bytes 4224 | tf_op jit(solution)/shard_map/all_gather | solution.py:47
  701.3 16.2 multiply_convert_fusion.2
  770.2 72.6 %while.131 = (s32[]{:T(128)}, bf16[2,1024,128]{1,2,0:T(8,128)(2,1)}, bf16[2,1024,128]{1,2,0:T(8,128)(2,1)}, bf16[2,1024,128]{1,2,0:T(8,128)(2,1)}, bf16[2,1024,1...) while((s32[]{:T(128)}, bf16[2,1024,128]{1,2,0:T(8,128)(2,1)}, ...), condition=%wide.region_28.29_spmd, body=%wide.region_24.28_spmd.sunk | while | flops 688389120 | bytes 81210144 | solution.py:217
  774.3 27.9 while.136
  810.7 27.9 while.136
  957.9 77.9 %while.133 = (s32[]{:T(128)}, bf16[2,1024,128]{1,2,0:T(8,128)(2,1)}, bf16[2,1024,128]{1,2,0:T(8,128)(2,1)}, bf16[2,1024,128]{1,2,0:T(8,128)(2,1)}, bf16[2,1024,1...) while((s32[]{:T(128)}, bf16[2,1024,128]{1,2,0:T(8,128)(2,1)}, ...), condition=%wide.region_37.38_spmd, body=%wide.region_33.37_spmd.sunk | while | flops 688389120 | bytes 68627040 | solution.py:217
  964.9 27.9 while.137
  1003.8 27.9 while.137
  1112.7 37.5 %copy.183 = f32[2,3,1024,1024]{3,0,1,2:T(2,128)} copy(f32[2,3,1024,1024]{2,3,1,0:T(8,128)} %pad_maximum_fusion.2) | data formatting | bytes 50331648 | tf_op jit(solution)/shard_map/scatter | solution.py:445
  1200.2 131.1 %reduce-scatter.38.cloned.1.call-done = f32[32,2]{1,0:T(8,128)} async-done(((f32[1024,2]{1,0:T(8,128)}), f32[32,2]{1,0:T(8,128)}) %reduce-scatter.38.cloned.1.call-update) | async-done | bytes 272
  1332.6 131.1 %reduce-scatter.32.cloned.1.call-done = f32[32,4]{1,0:T(8,128)} async-done(((f32[1024,4]{1,0:T(8,128)}), f32[32,4]{1,0:T(8,128)}) %reduce-scatter.32.cloned.1.call-update) | async-done | bytes 528
  1465.2 130.9 %reduce-scatter.34.cloned.1.call-done = f32[32,4]{1,0:T(8,128)} async-done(((f32[1024,4]{1,0:T(8,128)}), f32[32,4]{1,0:T(8,128)}) %reduce-scatter.34.cloned.1.call-update) | async-done | bytes 528
  1597.5 134.2 %reduce-scatter.36.cloned.1.call-done = f32[128,2]{1,0:T(8,128)} async-done(((f32[4096,2]{1,0:T(8,128)}), f32[128,2]{1,0:T(8,128)}) %reduce-scatter.36.cloned.1.call-update) | async-done | bytes 1040
  1741.6 123.2 %reduce-scatter.28.cloned.1.call-done = f32[32,4]{1,0:T(8,128)} async-done(((f32[1024,4]{1,0:T(8,128)}), f32[32,4]{1,0:T(8,128)}) %reduce-scatter.28.cloned.1.call-update) | async-done | bytes 528
  1866.3 391.3 %all-reduce.8.cloned.1.call-done = f32[2,3,1024,1024]{3,0,1,2:T(2,128)} async-done(((f32[2,3,1024,1024]{3,0,1,2:T(2,128)}), f32[2,3,1024,1024]{3,0,1,2:T(2,128)}) %all-reduce.8.cloned.1.call-update) | async-done | bytes 25165840
  2260.0 151.9 %reduce-scatter.22.cloned.1.call-done = f32[2,32,1024]{2,1,0:T(8,128)} async-done(((f32[2,1024,1024]{2,1,0:T(8,128)}), f32[2,32,1024]{2,1,0:T(8,128)}) %reduce-scatter.22.cloned.1.call-update) | async-done | bytes 262160 | tf_op jit(solution)/shard_map/reduce_scatter | solution.py:98
  2411.9 361.7 %reduce-scatter.24.cloned.1.call-done = f32[2,32,4096]{2,1,0:T(8,128)} async-done(((f32[2,1024,4096]{2,1,0:T(8,128)}), f32[2,32,4096]{2,1,0:T(8,128)}) %reduce-scatter.24.cloned.1.call-update) | async-done | bytes 1048592 | tf_op jit(solution)/shard_map/reduce_scatter | solution.py:102
  2773.6 360.4 %reduce-scatter.26.cloned.1.call-done = f32[2,128,1024]{2,1,0:T(8,128)} async-done(((f32[2,4096,1024]{2,1,0:T(8,128)}), f32[2,128,1024]{2,1,0:T(8,128)}) %reduce-scatter.26.cloned.1.call-update) | async-done | bytes 1048592 | tf_op jit(solution)/shard_map/reduce_scatter | solution.py:104
  (863 shorter events, 724.3 us)
Async XLA Ops:
  7.2 77.5 %all-gather.29.cloned.1.call-start = ((), (), s32[]{:S(2)}) async-start(), calls=%async_computation.28 | async-start | bytes 6488064 | tf_op jit(solution)/shard_map/all_gather | solution.py:42
  9.3 407.1 %all-gather.31.cloned.1.call-start = ((), (), s32[]{:S(2)}) async-start(), calls=%async_computation.29 | async-start | bytes 2162688 | tf_op jit(solution)/shard_map/all_gather | solution.py:44
  11.1 408.4 %all-gather.33.cloned.1.call-start = ((), (), s32[]{:S(2)}) async-start(), calls=%async_computation.30 | async-start | bytes 8650752 | tf_op jit(solution)/shard_map/all_gather | solution.py:48
  13.3 422.3 %all-gather.35.cloned.1.call-start = ((), (), s32[]{:S(2)}) async-start(), calls=%async_computation.31 | async-start | bytes 8650752 | tf_op jit(solution)/shard_map/all_gather | solution.py:50
  14.2 429.2 %all-gather.37.cloned.1.call-start = ((), (), s32[]{:S(2)}) async-start(), calls=%async_computation.32 | async-start | bytes 6488064 | tf_op jit(solution)/shard_map/all_gather | solution.py:42
  14.8 683.3 %all-gather.39.cloned.1.call-start = ((), (), s32[]{:S(2)}) async-start(), calls=%async_computation.33 | async-start | bytes 2162688 | tf_op jit(solution)/shard_map/all_gather | solution.py:44
  88.2 20.2 all-to-all-start
  108.4 21.5 all-to-all-start.1
  129.9 144.0 %all-to-all-start.2 = ((bf16[2,128,1024]{1,0,2:T(2,128)(2,1)}), bf16[2,128,1024]{1,0,2:T(2,128)(2,1)S(1)}, u32[]{:S(2)}, u32[]{:S(2)}) async-start(bf16[2,128,1024]{1,0,2:T(2,128)(2,1)} %copy.149), calls=%async_computation.2 | async-start | bytes 1048576 | tf_op jit(solution)/shard_map/all_to_all | solution.py:252
  133.4 567.9 %all-gather.41.cloned.1.call-start = ((), (), s32[]{:S(2)}) async-start(), calls=%async_computation.34 | async-start | bytes 8650752 | tf_op jit(solution)/shard_map/all_gather | solution.py:48
  299.8 114.4 %all-to-all-start.3 = ((bf16[2,1024,128]{2,0,1:T(2,128)(2,1)}), bf16[2,1024,128]{2,0,1:T(2,128)(2,1)S(1)}, u32[]{:S(2)}, u32[]{:S(2)}) async-start(bf16[2,1024,128]{2,0,1:T(2,128)(2,1)} %copy.151), calls=%async_computation.3 | async-start | bytes 1048576 | tf_op jit(solution)/shard_map/all_to_all | solution.py:255
  447.1 22.7 all-to-all-start.4
  469.8 24.4 all-to-all-start.5
  473.3 244.2 %all-gather.43.cloned.1.call-start = ((), (), s32[]{:S(2)}) async-start(), calls=%async_computation.35 | async-start | bytes 8650752 | tf_op jit(solution)/shard_map/all_gather | solution.py:50
  494.2 25.9 all-to-all-start.6
  542.8 154.9 %all-to-all-start.7 = ((bf16[2,1024,128]{2,0,1:T(2,128)(2,1)}), bf16[2,1024,128]{2,0,1:T(2,128)(2,1)S(1)}, u32[]{:S(2)}, u32[]{:S(2)}) async-start(bf16[2,1024,128]{2,0,1:T(2,128)(2,1)} %copy.161), calls=%async_computation.7 | async-start | bytes 1048576 | tf_op jit(solution)/shard_map/all_to_all | solution.py:255
  748.3 18.8 all-to-all-start.8
  863.7 18.9 all-to-all-start.10
  882.6 18.8 all-to-all-start.11
  935.6 19.2 all-to-all-start.12
  1056.8 19.0 all-to-all-start.13
  1060.3 138.6 %reduce-scatter.30.cloned.1.call-start = ((), (), s32[]{:S(2)}) async-start(), calls=%async_computation.37 | async-start | bytes 540672
  1061.5 269.7 %reduce-scatter.38.cloned.1.call-start = ((), (), s32[]{:S(2)}) async-start(), calls=%async_computation.41 | async-start | bytes 540672
  1062.7 401.0 %reduce-scatter.32.cloned.1.call-start = ((), (), s32[]{:S(2)}) async-start(), calls=%async_computation.38 | async-start | bytes 540672
  1064.8 531.2 %reduce-scatter.34.cloned.1.call-start = ((), (), s32[]{:S(2)}) async-start(), calls=%async_computation.39 | async-start | bytes 540672
  1075.8 20.0 all-to-all-start.14
  1080.0 651.8 %reduce-scatter.36.cloned.1.call-start = ((), (), s32[]{:S(2)}) async-start(), calls=%async_computation.40 | async-start | bytes 2162688
  1082.0 782.8 %reduce-scatter.28.cloned.1.call-start = ((), (), s32[]{:S(2)}) async-start(), calls=%async_computation.36 | async-start | bytes 540672
  1099.2 1158.5 %all-reduce.8.cloned.1.call-start = ((), (), s32[]{:S(2)}) async-start(), calls=%async_computation.42 | async-start | bytes 50331648
  1150.2 1261.7 %reduce-scatter.22.cloned.1.call-start = ((), (), s32[]{:S(2)}) async-start(), calls=%async_computation.25 | async-start | bytes 8650752 | tf_op jit(solution)/shard_map/reduce_scatter | solution.py:98
  1157.1 1616.4 %reduce-scatter.24.cloned.1.call-start = ((), (), s32[]{:S(2)}) async-start(), calls=%async_computation.26 | async-start | bytes 34603008 | tf_op jit(solution)/shard_map/reduce_scatter | solution.py:102
  1178.4 1955.6 %reduce-scatter.26.cloned.1.call-start = ((), (), s32[]{:S(2)}) async-start(), calls=%async_computation.27 | async-start | bytes 34603008 | tf_op jit(solution)/shard_map/reduce_scatter | solution.py:104
  (165 other events, 5589.4 us)
Sparse Core Ops, SparseCore 0:
  11.7 73.0 all-gather.28
  88.3 60.4 all-gather.30
  152.4 78.9 all-gather.32
  234.8 79.2 all-gather.34
  317.0 72.3 all-gather.36
  392.2 56.1 all-gather.38
  451.9 85.9 all-gather.40
  540.9 80.6 all-gather.42
  1063.3 135.4 reduce-scatter.29
  1201.0 130.1 reduce-scatter.37
  1333.5 130.1 reduce-scatter.31
  1465.9 130.1 reduce-scatter.33
  1598.3 133.3 reduce-scatter.35
  1734.5 130.3 reduce-scatter.27
  1871.1 386.5 all-reduce.7
  2260.4 151.4 reduce-scatter.21
  2414.6 358.9 reduce-scatter.23
  2776.3 357.5 reduce-scatter.25
where the time goes:
time: 3150 us; the launch traced here: 3140 us
  waiting for transfers between devices  2100 us (67%)
  blocking collectives  402 us (13%)
  matrix products  250 us (8%)
  local copies, waits for them, and re-layouts  190 us (6%)
  other arithmetic  121 us (4%)
  starting transfers between devices  58.5 us (2%)
    unnamed x25, waiting for transfers between devices  1050 us
    reduce_scatter x1, waiting for transfers between devices, scatter_stacked(): lax.psum_scatter(expand_weight, ('fsdp', 'seq'), scatter_dimension=1, til...  362 us
    reduce_scatter x1, waiting for transfers between devices, scatter_stacked(): lax.psum_scatter(reduce_weight, ('fsdp', 'seq'), scatter_dimension=1, til...  360 us
    reduce_scatter x1, waiting for transfers between devices, scatter_stacked(): lax.psum_scatter(output_weight, ('fsdp', 'seq'), scatter_dimension=1, til...  152 us
    all_gather x2, blocking collectives, gather_weights(): lax.all_gather(expand_bias, ('fsdp', 'seq'), axis=0, tiled=True)  91 us
    all_gather x2, blocking collectives, gather_weights(): lax.all_gather(norm_gain, ('fsdp', 'seq'), axis=1, tiled=True)  89.4 us
    all_gather x2, blocking collectives, gather_weights(): lax.all_gather(attend_bias, ('fsdp', 'seq'), axis=1, tiled=True)  88.6 us
    all_gather x2, blocking collectives, gather_weights(): lax.all_gather(norm_shift, ('fsdp', 'seq'), axis=1, tiled=True)  83.3 us
  transfers between devices with their start and end apart: 34, of which 24 were waited for; matrix products, arithmetic and copies ran while one was open for 10% of the time, Pallas kernels for 0%

commit v1 on v0

v1 whole, which is shorter than its diff:
```python
import jax
import jax.numpy as jnp
from jax import lax
from jax.sharding import Mesh, PartitionSpec as P

HEAD = 64
WIDE = 1024
SMALL_ROWS = 16
EPSILON = 1e-05
NEG_FILL = -1e30
BF = jnp.bfloat16
F32 = jnp.float32


def shift_perm(count, step):
    return [(i, (i + step) % count) for i in range(count)]


def swap_core(value):
    return lax.ppermute(value, "c", [(0, 1), (1, 0)])


def gather_shift(value, axes, count):
    place = lax.axis_index(axes)
    pieces = [value] + [
        lax.ppermute(value, axes, shift_perm(count, step)) for step in range(1, count)
    ]
    out = jnp.zeros((count,) + value.shape, value.dtype)
    for step, piece in enumerate(pieces):
        out = lax.dynamic_update_index_in_dim(out, piece, (place - step) % count, 0)
    return out


def scatter_shift(value, axes, count, dim=0):
    place = lax.axis_index(axes)

    def piece(step):
        return lax.dynamic_index_in_dim(value, (place + step) % count, dim, keepdims=False)

    got = [lax.ppermute(piece(step), axes, shift_perm(count, step)) for step in range(1, count)]
    total = piece(0).astype(F32)
    for part in got:
        total = total + part.astype(F32)
    return total


def both_cores(value):
    return jnp.concatenate([value, swap_core(value)], axis=0)


def sum_cores(partial):
    half = partial.shape[0] // 2
    return partial[:half] + swap_core(partial[half:].astype(BF)).astype(F32)


def matmul(left, right):
    return jnp.dot(left, right, preferred_element_type=F32)


def matmul_tn(left, right):
    return lax.dot_general(left, right, (((0,), (0,)), ((), ())), preferred_element_type=F32)


def matmul_nt(left, right):
    return lax.dot_general(left, right, (((1,), (1,)), ((), ())), preferred_element_type=F32)


def layer_norm(rows, gain, shift):
    mean = jnp.mean(rows, axis=-1, keepdims=True)
    centred = rows - mean
    variance = jnp.mean(centred * centred, axis=-1, keepdims=True)
    return centred * lax.rsqrt(variance + EPSILON) * gain + shift


def layer_norm_back(grad, rows, gain):
    mean = jnp.mean(rows, axis=-1, keepdims=True)
    centred = rows - mean
    variance = jnp.mean(centred * centred, axis=-1, keepdims=True)
    inverse = lax.rsqrt(variance + EPSILON)
    hat = centred * inverse
    grad_hat = grad * gain
    grad_rows = inverse * (
        grad_hat
        - jnp.mean(grad_hat, axis=-1, keepdims=True)
        - hat * jnp.mean(grad_hat * hat, axis=-1, keepdims=True)
    )
    return grad_rows, jnp.sum(grad * hat, axis=0), jnp.sum(grad, axis=0)


def attend_forward(query, key_value, docs_query, docs_key):
    rows, width = query.shape
    heads = width // HEAD
    query_heads = query.reshape(rows, heads, HEAD)
    key_heads = key_value[:, :width].reshape(-1, heads, HEAD)
    value_heads = key_value[:, width:].reshape(-1, heads, HEAD)
    scores = jnp.einsum("qhd,khd->hqk", query_heads, key_heads, preferred_element_type=F32)
    scores = scores * HEAD ** (-0.5)
    allowed = docs_query[:, None] == docs_key[None, :]
    scores = jnp.where(allowed[None], scores, NEG_FILL)
    top = jnp.max(scores, axis=-1, keepdims=True)
    raised = jnp.exp(scores - top)
    total = jnp.sum(raised, axis=-1, keepdims=True)
    soft = (raised / total).astype(BF)
    context = jnp.einsum("hqk,khd->qhd", soft, value_heads, preferred_element_type=F32)
    return context.astype(BF).reshape(rows, width), (top + jnp.log(total))[..., 0]


def attend_backward(grad, query, key_value, log_total, docs_query, docs_key):
    rows, width = query.shape
    heads = width // HEAD
    scale = HEAD ** (-0.5)
    grad_heads = grad.reshape(rows, heads, HEAD)
    query_heads = query.reshape(rows, heads, HEAD)
    key_heads = key_value[:, :width].reshape(-1, heads, HEAD)
    value_heads = key_value[:, width:].reshape(-1, heads, HEAD)
    scores = jnp.einsum("qhd,khd->hqk", query_heads, key_heads, preferred_element_type=F32)
    allowed = docs_query[:, None] == docs_key[None, :]
    scores = jnp.where(allowed[None], scores * scale, NEG_FILL)
    soft = jnp.exp(scores - log_total[..., None])
    grad_value = jnp.einsum("hqk,qhd->khd", soft.astype(BF), grad_heads, preferred_element_type=F32)
    grad_soft = jnp.einsum("qhd,khd->hqk", grad_heads, value_heads, preferred_element_type=F32)
    low = soft * (grad_soft - jnp.sum(soft * grad_soft, axis=-1, keepdims=True))
    low = low.astype(BF)
    grad_query = jnp.einsum("hqk,khd->qhd", low, key_heads, preferred_element_type=F32) * scale
    grad_key = jnp.einsum("hqk,qhd->khd", low, query_heads, preferred_element_type=F32) * scale
    keys = key_value.shape[0]
    return (
        grad_query.astype(BF).reshape(rows, width),
        grad_key.reshape(keys, width),
        grad_value.reshape(keys, width),
    )


def ffn_forward(rows_low, packed, bias, rows1):
    first = packed[:, :rows1].reshape(WIDE, WIDE)
    second = packed[:, rows1 : 2 * rows1].reshape(WIDE, WIDE)
    reduce = packed[:, 2 * rows1 :].reshape(2 * WIDE, WIDE)
    expanded = jnp.concatenate([matmul(rows_low, first), matmul(rows_low, second)], axis=1) + bias
    active = jax.nn.gelu(expanded, approximate=False).astype(BF)
    return matmul(active, reduce), expanded


def ffn_backward(grad_low, rows_low, expanded, packed, rows1):
    chips = packed.shape[0]
    first = packed[:, :rows1].reshape(WIDE, WIDE)
    second = packed[:, rows1 : 2 * rows1].reshape(WIDE, WIDE)
    reduce = packed[:, 2 * rows1 :].reshape(2 * WIDE, WIDE)
    active, pull = jax.vjp(lambda v: jax.nn.gelu(v, approximate=False), expanded)
    grad_reduce = matmul_tn(active.astype(BF), grad_low).astype(BF)
    grad_expanded = pull(matmul_nt(grad_low, reduce))[0].astype(BF)
    left, right = grad_expanded[:, :WIDE], grad_expanded[:, WIDE:]
    grad_first = matmul_tn(rows_low, left).astype(BF)
    grad_second = matmul_tn(rows_low, right).astype(BF)
    grad_rows = matmul_nt(left, first) + matmul_nt(right, second)
    grads = jnp.concatenate(
        [
            grad_first.reshape(chips, rows1, WIDE),
            grad_second.reshape(chips, rows1, WIDE),
            grad_reduce.reshape(chips, -1, WIDE),
        ],
        axis=1,
    )
    return grads, grad_rows, jnp.sum(grad_expanded, axis=0, dtype=F32)


def make_body(n_fa, n_fb, n_h, n_m):
    n_f, n_z = n_fa * n_fb, n_h * n_m
    n_chip = n_f * n_z
    z_axes = ("h", "m")

    def body(
        layer_input,
        documents,
        cotangent,
        attend_weight,
        attend_bias,
        output_weight,
        output_bias,
        norm_gain,
        norm_shift,
        expand_weight,
        expand_bias,
        reduce_weight,
        reduce_bias,
    ):
        core, half = lax.axis_index("c"), lax.axis_index("h")
        layers = attend_weight.shape[0]
        tokens = layer_input.shape[1]
        rows0 = attend_weight.shape[2]
        rows1 = 2 * rows0
        units = reduce_weight.shape[1]
        width = WIDE // 2
        own_tokens = 2 * tokens

        def by_core(own, other, axis):
            return jnp.where(
                core == 0,
                jnp.concatenate([own, other], axis=axis),
                jnp.concatenate([other, own], axis=axis),
            )

        def to_halves(pair):
            keep = jnp.where(half == 0, pair[0], pair[1])
            give = jnp.where(half == 0, pair[1], pair[0])
            got = lax.ppermute(give, "h", [(0, 1), (1, 0)])
            first = jnp.where(half == 0, keep, got)
            last = jnp.where(half == 0, got, keep)
            return jnp.concatenate([first, last], axis=0)

        def from_halves(rows):
            first, last = rows[:tokens], rows[tokens:]
            keep = jnp.where(half == 0, first, last)
            give = jnp.where(half == 0, last, first)
            got = lax.ppermute(give, "h", [(0, 1), (1, 0)])
            return jnp.where(half == 0, jnp.stack([keep, got]), jnp.stack([got, keep]))

        def smalls_of(layer):
            return jnp.concatenate(
                [
                    attend_bias[layer].reshape(-1),
                    output_bias[layer],
                    norm_gain[layer].reshape(-1),
                    norm_shift[layer].reshape(-1),
                    expand_bias[layer],
                    reduce_bias[layer],
                ]
            )

        small_row = jnp.concatenate([smalls_of(layer) for layer in range(layers)])
        small_len = small_row.shape[0] // layers
        small_row = jnp.pad(small_row.astype(BF), (0, WIDE - layers * small_len))[None]
        small_row = by_core(small_row, swap_core(small_row), 0)
        small_shard = jnp.pad(small_row, ((0, SMALL_ROWS - 2), (0, 0)))

        def shards_of(layer):
            wa = attend_weight[layer].astype(BF)
            wo = output_weight[layer].astype(BF)
            w1 = expand_weight[layer].astype(BF).reshape(rows0, -1, 2, units)
            wa_own = jnp.where(core == 0, wa[..., :width], wa[..., width:])
            wa_give = jnp.where(core == 0, wa[..., width:], wa[..., :width])
            wo_own = jnp.where(core == 0, wo[:, :width], wo[:, width:])
            wo_give = jnp.where(core == 0, wo[:, width:], wo[:, :width])
            w1_own = jnp.where(core == 0, w1[:, :, 0], w1[:, :, 1]).reshape(rows0, 2 * WIDE)
            w1_give = jnp.where(core == 0, w1[:, :, 1], w1[:, :, 0]).reshape(rows0, 2 * WIDE)

            def attn_pack(a, o):
                return jnp.stack(
                    [
                        jnp.concatenate([a[0], a[1]], axis=1),
                        jnp.concatenate([a[2], o], axis=1),
                    ]
                )

            def ffn_pack(w):
                return jnp.stack([w[:, :WIDE], w[:, WIDE:]])

            attn_own, attn_give = attn_pack(wa_own, wo_own), attn_pack(wa_give, wo_give)
            ffn_own, ffn_give = ffn_pack(w1_own), ffn_pack(w1_give)
            got = swap_core(jnp.concatenate([attn_give, ffn_give], axis=0))
            attn = by_core(attn_own, got[:2], 1)
            ffn = by_core(ffn_own, got[2:], 1).reshape(2 * rows1, WIDE)
            ffn = jnp.concatenate([ffn, reduce_weight[layer].astype(BF)], axis=0)
            return attn, ffn

        def gather_attn(attn, extra=None):
            parts = [attn[0], attn[1]]
            if extra is not None:
                parts.append(extra)
            column = gather_shift(jnp.concatenate(parts, axis=0), z_axes, n_z)
            first = column[:, :rows1]
            second = column[:, rows1:]
            first = gather_shift(gather_shift(first, "fb", n_fb), "fa", n_fa)
            second = gather_shift(gather_shift(second, "fa", n_fa), "fb", n_fb)
            second = jnp.swapaxes(second, 0, 1)
            first = first.reshape(n_chip, -1, WIDE)
            second = second.reshape(n_chip, -1, WIDE)
            small = second[:, rows1:]
            query_key = first.reshape(WIDE, WIDE)
            value_out = second[:, :rows1].reshape(WIDE, WIDE)
            out_cols = value_out[:, width:]
            give = jnp.where(core == 0, out_cols[width:], out_cols[:width])
            mine = jnp.where(core == 0, out_cols[:width], out_cols[width:])
            out_rows = by_core(mine, swap_core(give), 1)
            return (query_key, value_out[:, :width], out_rows), small

        def gather_ffn(ffn):
            column = gather_shift(ffn, z_axes, n_z)
            whole = lax.all_gather(column, ("fa", "fb"), axis=0, tiled=True)
            return whole

        attn_w, ffn_w = [], []
        shards = [shards_of(layer) for layer in range(layers)]
        for layer in range(layers):
            if layer == 0:
                got, small = gather_attn(shards[layer][0], small_shard)
            else:
                got, _ = gather_attn(shards[layer][0])
            attn_w.append(got)
            ffn_w.append(gather_ffn(shards[layer][1]))

        small = small[:, :2].reshape(2 * n_chip, WIDE)[:, : layers * small_len].astype(F32)
        small = small.reshape(2 * n_chip, layers, small_len)

        def small_params(layer):
            part = small[:, layer]

            def vector(index):
                return part[:, index * rows0 : (index + 1) * rows0].reshape(-1)

            bias1 = part[:, 7 * rows0 : 7 * rows0 + units].reshape(n_chip, 2, units)
            bias1 = jnp.where(core == 0, bias1[:, 0], bias1[:, 1]).reshape(-1)
            bias2 = part[:, 7 * rows0 + units :].reshape(-1)
            return [vector(index) for index in range(7)] + [bias1, bias2]

        vectors = [small_params(layer) for layer in range(layers)]

        rows_low = to_halves(layer_input)
        docs_own = to_halves(documents)
        docs_chip = both_cores(docs_own)
        docs_all = jnp.concatenate(
            [docs_chip]
            + [lax.ppermute(docs_chip, "m", shift_perm(n_m, step)) for step in range(1, n_m)]
        )
        grad_rows = to_halves(cotangent).astype(F32)

        def core_half(vector):
            return jnp.where(core == 0, vector[:width], vector[width:])

        kept = []
        rows_in = rows_low.astype(F32)
        for layer in range(layers):
            (query_key, value_w, out_w), ffn = attn_w[layer], ffn_w[layer]
            bq, bv, bo, gain0, gain1, shift0, shift1, bias1, bias2 = vectors[layer]
            chip_rows = both_cores(rows_low)
            qk = matmul(chip_rows, query_key)
            query = (qk[:, :width] + core_half(bq)).astype(BF)
            key = qk[:, width:].astype(BF)
            value = (matmul(chip_rows, value_w) + core_half(bv)).astype(BF)
            kv = jnp.concatenate([key, value], axis=1)
            kv = jnp.concatenate(
                [kv]
                + [lax.ppermute(kv, "m", shift_perm(n_m, step)) for step in range(1, n_m)],
                axis=0,
            )
            context, log_total = attend_forward(query, kv, docs_chip, docs_all)
            branch = sum_cores(matmul(context, out_w)) + bo
            first_sum = rows_in + branch
            first_norm = layer_norm(first_sum, gain0, shift0)
            chip_norm = both_cores(first_norm.astype(BF))
            reduced, expanded = ffn_forward(chip_norm, ffn, bias1, rows1)
            second_sum = first_norm + (sum_cores(reduced) + bias2)
            rows_in = layer_norm(second_sum, gain1, shift1)
            kept.append((chip_rows, query, kv, context, log_total, first_sum, chip_norm, expanded, second_sum))
            rows_low = rows_in.astype(BF)
        layer_output = from_halves(rows_low)

        ffn_grads, attn_grads, small_grads = [None] * layers, [None] * layers, [None] * layers
        for layer in reversed(range(layers)):
            chip_rows, query, kv, context, log_total, first_sum, chip_norm, expanded, second_sum = kept[layer]
            (query_key, value_w, out_w), ffn = attn_w[layer], ffn_w[layer]
            gain0, gain1 = vectors[layer][3], vectors[layer][4]
            grad_second, dgain1, dshift1 = layer_norm_back(grad_rows, second_sum, gain1)
            grad_low = grad_second.astype(BF)
            dbias2 = jnp.sum(grad_low, axis=0, dtype=F32)
            packed, grad_norm, dbias1 = ffn_backward(both_cores(grad_low), chip_norm, expanded, ffn, rows1)
            ffn_grads[layer] = packed
            grad_first = grad_second + sum_cores(grad_norm)
            grad_sum, dgain0, dshift0 = layer_norm_back(grad_first, first_sum, gain0)
            grad_low = grad_sum.astype(BF)
            dbo = jnp.sum(grad_low, axis=0, dtype=F32)
            chip_low = both_cores(grad_low)
            grad_context = matmul_nt(chip_low, out_w).astype(BF)
            grad_out = matmul_tn(context, chip_low).astype(BF)
            give = jnp.where(core == 0, grad_out[:, width:], grad_out[:, :width])
            mine = jnp.where(core == 0, grad_out[:, :width], grad_out[:, width:])
            grad_out = by_core(mine, swap_core(give), 0)
            dq, dk, dv = attend_backward(grad_context, query, kv, log_total, docs_chip, docs_all)
            dkv = jnp.concatenate([dk, dv], axis=1)
            chip_tokens = 2 * own_tokens
            total = dkv[:chip_tokens]
            for step in range(1, n_m):
                part = dkv[step * chip_tokens : (step + 1) * chip_tokens].astype(BF)
                total = total + lax.ppermute(part, "m", shift_perm(n_m, -step)).astype(F32)
            dkv = total.astype(BF)
            dk, dv = dkv[:, :width], dkv[:, width:]
            dqk = jnp.concatenate([dq, dk], axis=1)
            grad_qk = matmul_tn(chip_rows, dqk).astype(BF)
            grad_v = matmul_tn(chip_rows, dv).astype(BF)
            attn_grads[layer] = (grad_qk, jnp.concatenate([grad_v, grad_out], axis=1))
            dbq = jnp.sum(dq, axis=0, dtype=F32)
            dbv = jnp.sum(dv, axis=0, dtype=F32)
            grad_rows = grad_sum + sum_cores(matmul_nt(dqk, query_key) + matmul_nt(dv, value_w))

            def spread(vector):
                blank = jnp.zeros_like(vector)
                return by_core(vector, blank, 0)

            dbias1 = dbias1.reshape(n_chip, 1, units)
            dbias1 = by_core(dbias1, jnp.zeros_like(dbias1), 1).reshape(2 * n_chip, units)
            small_grads[layer] = jnp.concatenate(
                [
                    vector.reshape(2 * n_chip, rows0)
                    for vector in (spread(dbq), spread(dbv), dbo, dgain0, dgain1, dshift0, dshift1)
                ]
                + [dbias1, dbias2.reshape(2 * n_chip, rows0)],
                axis=1,
            )
        input_gradient = from_halves(grad_rows)

        small_all = jnp.concatenate(small_grads, axis=1)
        small_all = jnp.pad(small_all, ((0, 0), (0, WIDE - layers * small_len)))
        small_all = small_all.reshape(n_chip, 2, WIDE).astype(BF)
        small_all = jnp.pad(small_all, ((0, 0), (0, SMALL_ROWS - 2), (0, 0)))

        def scatter_attn(first, second, extra=None):
            first = first.reshape(n_fa, n_fb, n_z, rows1, WIDE)
            second = second.reshape(n_chip, rows1, WIDE)
            if extra is not None:
                second = jnp.concatenate([second, extra], axis=1)
            second = second.reshape(n_fa, n_fb, n_z, -1, WIDE)
            first = scatter_shift(first, "fa", n_fa).astype(BF)
            second = scatter_shift(second, "fb", n_fb, 1).astype(BF)
            first = scatter_shift(first, "fb", n_fb)
            second = scatter_shift(second, "fa", n_fa)
            both = jnp.concatenate([first, second], axis=1).astype(BF)
            return scatter_shift(both, z_axes, n_z)

        def core_rows(value, axis):
            count = value.shape[axis] // 2
            low = lax.slice_in_dim(value, 0, count, axis=axis)
            high = lax.slice_in_dim(value, count, 2 * count, axis=axis)
            return jnp.where(core == 0, low, high), jnp.where(core == 0, high, low)

        wa_out, wo_out, w1_out, w2_out = [None] * layers, [None] * layers, [None] * layers, [None] * layers
        for layer in reversed(range(layers)):
            column = lax.psum_scatter(ffn_grads[layer], ("fa", "fb"), scatter_dimension=0, tiled=True)
            mine = scatter_shift(column, z_axes, n_z)
            w2_out[layer] = mine[2 * rows1 :]
            keep, give = core_rows(mine[: 2 * rows1].reshape(2, rows1, WIDE), 1)
            got = swap_core(give)
            keep = jnp.swapaxes(keep, 0, 1).reshape(rows0, -1, 1, units)
            got = jnp.swapaxes(got, 0, 1).reshape(rows0, -1, 1, units)
            w1_out[layer] = by_core(keep, got, 2).reshape(rows0, -1)

            extra = small_all if layer == 0 else None
            mine = scatter_attn(*attn_grads[layer], extra)
            keep, give = core_rows(mine[: 2 * rows1].reshape(2, rows1, 2, width), 1)
            got = swap_core(give)
            full = by_core(keep[:, :, None], got[:, :, None], 2)
            wa_out[layer] = jnp.stack(
                [
                    full[0, :, :, 0].reshape(rows0, WIDE),
                    full[0, :, :, 1].reshape(rows0, WIDE),
                    full[1, :, :, 0].reshape(rows0, WIDE),
                ]
            )
            wo_out[layer] = full[1, :, :, 1].reshape(rows0, WIDE)
            if layer == 0:
                keep, give = core_rows(mine[2 * rows1 : 2 * rows1 + 2], 0)
                row = (keep + swap_core(give))[0, : layers * small_len].reshape(layers, small_len)
        cut = [row[:, index * rows0 : (index + 1) * rows0] for index in range(7)]
        return (
            layer_output,
            input_gradient,
            jnp.stack(wa_out),
            jnp.stack([cut[0], cut[1]], axis=1),
            jnp.stack(wo_out),
            cut[2],
            jnp.stack([cut[3], cut[4]], axis=1),
            jnp.stack([cut[5], cut[6]], axis=1),
            jnp.stack(w1_out),
            row[:, 7 * rows0 : 7 * rows0 + units],
            jnp.stack(w2_out),
            row[:, 7 * rows0 + units :],
        )

    return body


def solution(mesh):
    n_f, n_s = mesh.shape["fsdp"], mesh.shape["seq"]
    sizes = (2, n_f // 2, 2, n_s // 4, 2)
    grid = Mesh(mesh.devices.reshape(sizes), ("fa", "fb", "h", "m", "c"))
    fsdp, seq = ("fa", "fb"), ("h", "m", "c")
    both = fsdp + seq
    tokens = P(fsdp, seq, None)
    third, second = P(None, None, both), P(None, both)
    params = (
        P(None, None, both, None),
        third,
        P(None, both, None),
        second,
        third,
        third,
        P(None, both, None),
        second,
        P(None, both, None),
        second,
    )
    return jax.shard_map(
        make_body(sizes[0], sizes[1], sizes[2], sizes[3]),
        mesh=grid,
        in_specs=(tokens, P(fsdp, seq), tokens) + params,
        out_specs=(tokens, tokens) + params,
        check_vma=False,
    )
```

time: 3150 us -> 928 us (0.29)
  waiting for transfers between devices: 2100 us -> 366 us
  blocking collectives: 402 us -> 0 us
  matrix products: 250 us -> 138 us
  starting transfers between devices: 58.5 us -> 131 us
  local copies, waits for them, and re-layouts: 190 us -> 133 us
    unnamed x25 -> x4, waiting for transfers between devices: 1050 us -> 0.07 us
    reduce_scatter x3 -> x2, waiting for transfers between devices: 874 us -> 0.01 us  [body(): lax.psum_scatter(ffn_grads[layer], ('fa', 'fb'), scatter_dimension=0, til...]
    ppermute x0 -> x79, waiting for transfers between devices: none -> 366 us  [the longest x20 138 us: scatter_shift(): lax.ppermute(piece(step), axes, shift_perm(count, step))]
    all_gather x9 -> x0, blocking collectives: 362 us -> none  [the longest x2 91 us: gather_weights(): lax.all_gather(expand_bias, ('fsdp', 'seq'), axis=0, tiled=True)]
    all_to_all x16 -> x0, waiting for transfers between devices: 166 us -> none  [the longest x2 31.3 us: forward_layer(): lax.all_to_all(key_rows, 'seq', split_axis=2, concat_axis=1, tiled=True)]
    ppermute x0 -> x79, starting transfers between devices: none -> 130 us  [the longest x20 44.6 us: scatter_shift(): lax.ppermute(piece(step), axes, shift_perm(count, step))]
    dot_general x84 -> x48, matrix products: 250 us -> 138 us  [the longest x2 30.8 us: attend_backward(): jnp.einsum('qhd,khd->hqk', grad_heads, value_heads, preferred_element_typ...]
    all_to_all x16 -> x0, starting transfers between devices: 57.4 us -> none  [the longest x2 7.82 us: backward_layer(): lax.all_to_all(grad_key_heads, 'seq', split_axis=1, concat_axis=2, tiled=...]
  transfers between devices with their start and end apart: 34 -> 83, of which waited for: 24 -> 40; matrix products, arithmetic and copies ran while one was open for 10% -> 36% of each run, Pallas kernels for 0% -> 0%
where the time goes in v1:
time: 928 us; the launch traced here: 918 us
  waiting for transfers between devices  366 us (39%)
  matrix products  138 us (15%)
  local copies, waits for them, and re-layouts  133 us (14%)
  other arithmetic  133 us (14%)
  starting transfers between devices  131 us (14%)
  between operations  18.1 us (2%)
    ppermute x20, waiting for transfers between devices, scatter_shift(): lax.ppermute(piece(step), axes, shift_perm(count, step))  138 us
    ppermute x20, waiting for transfers between devices, gather_shift(): lax.ppermute(value, axes, shift_perm(count, step))  123 us
    ppermute x20, starting transfers between devices, scatter_shift(): lax.ppermute(piece(step), axes, shift_perm(count, step))  44.6 us
    unnamed x365, local copies, waits for them, and re-layouts  39.7 us
    ppermute x20, starting transfers between devices, gather_shift(): lax.ppermute(value, axes, shift_perm(count, step))  37.3 us
    ppermute x2, waiting for transfers between devices, body(): total = total + lax.ppermute(part, 'm', shift_perm(n_m, -step)).astype(F32)  32.2 us
    dot_general x2, matrix products, attend_backward(): jnp.einsum('qhd,khd->hqk', grad_heads, value_heads, preferred_element_typ...  30.8 us
    ppermute x2, waiting for transfers between devices, body(): lax.ppermute(kv, 'm', shift_perm(n_m, step))  30.4 us
  transfers between devices with their start and end apart: 83, of which 40 were waited for; matrix products, arithmetic and copies ran while one was open for 36% of the time, Pallas kernels for 0%

profile of v1, /device:TPU:0, one launch (start us, length us, event | category | flops | bytes accessed | tf_op | source)
XLA Modules:
  0.0 918.5 jit_solution(12357589308869176527)
XLA Ops:
  25.0 12.4 %collective-permute-done.18 = bf16[256,1024]{1,0:T(8,128)(2,1)} collective-permute-done((bf16[256,1024]{1,0:T(8,128)(2,1)}, bf16[256,1024]{1,0:T(8,128)(2,1)}, u32[]{:S(2)}, u32[]{:S(2)}) %collective-permute-start.18) | collective-permute-done | bytes 524320 | tf_op jit(solution)/shard_map/ppermute | solution.py:26
  38.4 20.6 %collective-permute-done.19 = bf16[256,1024]{1,0:T(8,128)(2,1)} collective-permute-done((bf16[256,1024]{1,0:T(8,128)(2,1)}, bf16[256,1024]{1,0:T(8,128)(2,1)}, u32[]{:S(2)}, u32[]{:S(2)}) %collective-permute-start.19) | collective-permute-done | bytes 524320 | tf_op jit(solution)/shard_map/ppermute | solution.py:26
  61.6 9.7 %collective-permute-start = (bf16[128,1024]{1,0:T(8,128)(2,1)S(1)}, bf16[128,1024]{1,0:T(8,128)(2,1)S(1)}, u32[]{:S(2)}, u32[]{:S(2)}) collective-permute-start(bf16[128,1024]{1,0:T(8,128)(2,1)S(1)} %select_bitcast_fusion.7), channel_id=1, source_target_pairs={{0,4},{4,0},{1,5},{5,1},{2,6},{6,2},{3,7},{7,3},{8,12},{12,8},{9,1... | collective-permute-start | bytes 786440 | tf_op jit(solution)/shard_map/ppermute | solution.py:205
  99.2 14.3 %collective-permute-done.25 = bf16[128,1024]{1,0:T(8,128)(2,1)S(1)} collective-permute-done((bf16[128,1024]{1,0:T(8,128)(2,1)S(1)}, bf16[128,1024]{1,0:T(8,128)(2,1)S(1)}, u32[]{:S(2)}, u32[]{:S(2)}) %collective-permute-start.25) | collective-permute-done | bytes 262176 | tf_op jit(solution)/shard_map/ppermute | solution.py:26
  113.5 7.8 collective-permute-start.36
  134.8 18.4 %collective-permute-done.35 = bf16[256,1024]{1,0:T(8,128)(2,1)S(1)} collective-permute-done((bf16[256,1024]{1,0:T(8,128)(2,1)}, bf16[256,1024]{1,0:T(8,128)(2,1)S(1)}, u32[]{:S(2)}, u32[]{:S(2)}) %collective-permute-start.35) | collective-permute-done | bytes 524320 | tf_op jit(solution)/shard_map/ppermute | solution.py:26
  168.7 25.9 %collective-permute-done.8 = bf16[2,4,64,1024]{3,2,1,0:T(8,128)(2,1)S(1)} collective-permute-done((bf16[2,4,64,1024]{3,2,1,0:T(8,128)(2,1)S(1)}, bf16[2,4,64,1024]{3,2,1,0:T(8,128)(2,1)S(1)}, u32[]{:S(2)}, u32[]{:S(2)}) %collective-permute-start.8) | collective-permute-done | bytes 1048608 | tf_op jit(solution)/shard_map/ppermute | solution.py:26
  197.4 11.2 %collective-permute-done.10 = bf16[2,4,80,1024]{3,2,1,0:T(8,128)(2,1)S(1)} collective-permute-done((bf16[2,4,80,1024]{3,2,1,0:T(8,128)(2,1)S(1)}, bf16[2,4,80,1024]{3,2,1,0:T(8,128)(2,1)S(1)}, u32[]{:S(2)}, u32[]{:S(2)}) %collective-permute-start.10) | collective-permute-done | bytes 1310752 | tf_op jit(solution)/shard_map/ppermute | solution.py:26
  215.7 11.8 %collective-permute-start.11 = (bf16[512,1024]{1,0:T(8,128)(2,1)}, bf16[512,1024]{1,0:T(8,128)(2,1)}, u32[]{:S(2)}, u32[]{:S(2)}) collective-permute-start(bf16[512,1024]{1,0:T(8,128)(2,1)} %pad_maximum_fusion.9), channel_id=1, source_target_pairs={{0,2},{2,0},{1,3},{3,1},{4,6},{6,4},{5,7},{7,5},{8,10},{10,8},{9,1... | collective-permute-start | bytes 3145736 | tf_op jit(solution)/shard_map/ppermute | solution.py:342
  238.3 12.5 %collective-permute-done.11 = bf16[512,1024]{1,0:T(8,128)(2,1)} collective-permute-done((bf16[512,1024]{1,0:T(8,128)(2,1)}, bf16[512,1024]{1,0:T(8,128)(2,1)}, u32[]{:S(2)}, u32[]{:S(2)}) %collective-permute-start.11) | collective-permute-done | bytes 1048608 | tf_op jit(solution)/shard_map/ppermute | solution.py:342
  289.5 10.2 %multiply_convert_fusion.3 = (bf16[512,2048]{1,0:T(8,128)(2,1)S(1)}, f32[512,2048]{1,0:T(8,128)}) fusion(f32[512,1024]{1,0:T(8,128)S(1)} %fusion.145, f32[512,1024]{1,0:T(8,128)S(1)} %fusion.146, f32[2048]{0:T(1024)S(1)} %bitcast.558), kind=kLoop, calls=%fused_computation.51 | loop fusion | flops 70254592 | bytes 10493952 | tf_op jit(solution)/shard_map/convert_element_type | solution.py:139
  312.7 10.2 %collective-permute-done.30 = bf16[2,4,64,1024]{3,2,1,0:T(8,128)(2,1)} collective-permute-done((bf16[2,4,64,1024]{3,2,1,0:T(8,128)(2,1)}, bf16[2,4,64,1024]{3,2,1,0:T(8,128)(2,1)}, u32[]{:S(2)}, u32[]{:S(2)}) %collective-permute-start.30) | collective-permute-done | bytes 1048608 | tf_op jit(solution)/shard_map/ppermute | solution.py:26
  342.7 17.9 %collective-permute-done.31 = bf16[512,1024]{1,0:T(8,128)(2,1)} collective-permute-done((bf16[512,1024]{1,0:T(8,128)(2,1)}, bf16[512,1024]{1,0:T(8,128)(2,1)}, u32[]{:S(2)}, u32[]{:S(2)}) %collective-permute-start.31) | collective-permute-done | bytes 1048608 | tf_op jit(solution)/shard_map/ppermute | solution.py:342
  398.1 10.4 %multiply_convert_fusion.2 = (bf16[512,2048]{1,0:T(8,128)(2,1)S(1)}, f32[512,2048]{1,0:T(8,128)}) fusion(f32[512,1024]{1,0:T(8,128)S(1)} %fusion.142, f32[512,1024]{1,0:T(8,128)S(1)} %fusion.143, f32[2048]{0:T(1024)S(1)} %bitcast.560), kind=kLoop, calls=%fused_computation.38 | loop fusion | flops 70254592 | bytes 10493952 | tf_op jit(solution)/shard_map/convert_element_type | solution.py:139
  414.9 12.2 %collective-permute-done.40 = bf16[128,1024]{1,0:T(8,128)(2,1)S(1)} collective-permute-done((bf16[128,1024]{1,0:T(8,128)(2,1)S(1)}, bf16[128,1024]{1,0:T(8,128)(2,1)S(1)}, u32[]{:S(2)}, u32[]{:S(2)}) %collective-permute-start.40) | collective-permute-done | bytes 262176 | tf_op jit(solution)/shard_map/ppermute | solution.py:205
  436.2 6.2 convert_reduce_fusion
  470.8 14.9 %multiply_reduce_fusion.1 = (f32[8,512]{1,0:T(8,128)S(1)}, f32[8,512,1024]{2,1,0:T(8,128)}) fusion(f32[8,512,1024]{2,1,0:T(8,128)} %copy-done.1, f32[8,512]{1,0:T(8,128)S(1)} %log_add_fusion.1, bf16[512,8,64]{0,2,1:T(8,128)(2,1)} %bitcast.508, bf16[1024,8,64]{0,2,1:T(8,128)(2,1)S(1)} %bitcast.497), kind=kOutput, calls=%fused_computation.4 | convolution fusion | flops 549449728 | bytes 35160064 | tf_op jit(solution)/shard_map/qhd,khd->hqk/dot_general | solution.py:121
  488.4 8.2 multiply_convert_fusion.1
  519.1 16.9 %collective-permute-done.44 = bf16[512,1024]{0,1:T(8,128)(2,1)} collective-permute-done((bf16[512,1024]{0,1:T(8,128)(2,1)S(1)}, bf16[512,1024]{0,1:T(8,128)(2,1)}, u32[]{:S(2)}, u32[]{:S(2)}) %collective-permute-start.44) | collective-permute-done | bytes 1048608 | tf_op jit(solution)/shard_map/ppermute | solution.py:383
  596.1 15.6 %collective-permute-done.62 = bf16[4,64,1024]{2,1,0:T(8,128)(2,1)S(1)} collective-permute-done((bf16[4,64,1024]{2,1,0:T(8,128)(2,1)S(1)}, bf16[4,64,1024]{2,1,0:T(8,128)(2,1)S(1)}, u32[]{:S(2)}, u32[]{:S(2)}) %collective-permute-start.62) | collective-permute-done | bytes 524320 | tf_op jit(solution)/shard_map/ppermute | solution.py:40
  629.9 6.5 collective-permute-done.67
  640.3 15.9 %multiply_reduce_fusion = (f32[8,512]{1,0:T(8,128)S(1)}, f32[8,512,1024]{2,1,0:T(8,128)}) fusion(f32[8,512,1024]{2,1,0:T(8,128)} %copy-done, f32[8,512]{1,0:T(8,128)S(1)} %log_add_fusion, bf16[512,8,64]{0,2,1:T(8,128)(2,1)S(1)} %bitcast.510, bf16[1024,8,64]{0,2,1:T(8,128)(2,1)S(1)} %bitcast.495), kind=kOutput, calls=%fused_computation.1 | convolution fusion | flops 549449728 | bytes 35160064 | tf_op jit(solution)/shard_map/qhd,khd->hqk/dot_general | solution.py:121
  656.8 8.2 multiply_convert_fusion
  676.4 6.8 collective-permute-start.49
  692.0 15.2 %collective-permute-done.49 = bf16[512,1024]{0,1:T(8,128)(2,1)} collective-permute-done((bf16[512,1024]{0,1:T(8,128)(2,1)}, bf16[512,1024]{0,1:T(8,128)(2,1)}, u32[]{:S(2)}, u32[]{:S(2)}) %collective-permute-start.49) | collective-permute-done | bytes 1048608 | tf_op jit(solution)/shard_map/ppermute | solution.py:383
  730.0 14.6 %collective-permute-done.52 = bf16[2,4,64,1024]{3,2,1,0:T(8,128)(2,1)S(1)} collective-permute-done((bf16[2,4,64,1024]{3,2,1,0:T(8,128)(2,1)S(1)}, bf16[2,4,64,1024]{3,2,1,0:T(8,128)(2,1)S(1)}, u32[]{:S(2)}, u32[]{:S(2)}) %collective-permute-start.52) | collective-permute-done | bytes 1048608 | tf_op jit(solution)/shard_map/ppermute | solution.py:40
  747.1 6.1 collective-permute-done.55
  755.8 7.6 collective-permute-done.53
  777.1 14.7 %collective-permute-done.51 = f32[128,1024]{1,0:T(8,128)S(1)} collective-permute-done((f32[128,1024]{1,0:T(8,128)S(1)}, f32[128,1024]{1,0:T(8,128)S(1)}, u32[]{:S(2)}, u32[]{:S(2)}) %collective-permute-start.51) | collective-permute-done | bytes 524320 | tf_op jit(solution)/shard_map/ppermute | solution.py:214
  824.2 12.5 %collective-permute-start.72 = (bf16[256,1024]{1,0:T(8,128)(2,1)}, bf16[256,1024]{1,0:T(8,128)(2,1)}, u32[]{:S(2)}, u32[]{:S(2)}) collective-permute-start(bf16[256,1024]{1,0:T(8,128)(2,1)} %get-tuple-element.111), channel_id=1, source_target_pairs={{0,4},{2,6},{4,0},{6,2},{1,5},{3,7},{5,1},{7,3},{8,12},{10,14},{12... | collective-permute-start | bytes 1572872 | tf_op jit(solution)/shard_map/ppermute | solution.py:40
  839.7 29.5 %collective-permute-done.76 = bf16[256,1024]{1,0:T(8,128)(2,1)} collective-permute-done((bf16[256,1024]{1,0:T(8,128)(2,1)S(1)}, bf16[256,1024]{1,0:T(8,128)(2,1)}, u32[]{:S(2)}, u32[]{:S(2)}) %collective-permute-start.76) | collective-permute-done | bytes 524320 | tf_op jit(solution)/shard_map/ppermute | solution.py:40
  869.3 33.2 %collective-permute-done.72 = bf16[256,1024]{1,0:T(8,128)(2,1)} collective-permute-done((bf16[256,1024]{1,0:T(8,128)(2,1)}, bf16[256,1024]{1,0:T(8,128)(2,1)}, u32[]{:S(2)}, u32[]{:S(2)}) %collective-permute-start.72) | collective-permute-done | bytes 524320 | tf_op jit(solution)/shard_map/ppermute | solution.py:40
  (918 shorter events, 462.3 us)
Async XLA Ops:
  7.2 274.7 %all-gather.3.cloned.1.call-start = ((), (), s32[]{:S(2)}) async-start(), calls=%async_computation.2 | async-start | bytes 10485760 | tf_op jit(solution)/shard_map/all_gather | solution.py:288
  8.0 64.6 %collective-permute-start.12 = (s32[128]{0:T(128)S(1)}, s32[128]{0:T(128)S(1)}, u32[]{:S(2)}, u32[]{:S(2)}) collective-permute-start(s32[128]{0:T(128)S(1)} %fusion.127), channel_id=1, source_target_pairs={{0,4},{4,0},{1,5},{5,1},{2,6},{6,2},{3,7},{7,3},{8,12},{12,8},{9,1... | collective-permute-start | bytes 1544 | tf_op jit(solution)/shard_map/ppermute | solution.py:205
  21.9 37.1 %collective-permute-start.19 = (bf16[256,1024]{1,0:T(8,128)(2,1)}, bf16[256,1024]{1,0:T(8,128)(2,1)}, u32[]{:S(2)}, u32[]{:S(2)}) collective-permute-start(bf16[256,1024]{1,0:T(8,128)(2,1)} %pad_maximum_fusion.40), channel_id=1, source_target_pairs={{0,4},{2,6},{4,0},{6,2},{1,5},{3,7},{5,1},{7,3},{8,12},{10,14},{12... | collective-permute-start | bytes 1572872 | tf_op jit(solution)/shard_map/ppermute | solution.py:26
  22.3 54.0 %collective-permute-start.3 = (bf16[1,1024]{1,0:T(2,128)(2,1)S(1)}, bf16[1,1024]{1,0:T(2,128)(2,1)S(1)}, u32[]{:S(2)}, u32[]{:S(2)}) collective-permute-start(bf16[1,1024]{1,0:T(2,128)(2,1)S(1)} %broadcast_in_dim.201), channel_id=1, source_target_pairs={{0,1},{1,0},{2,3},{3,2},{4,5},{5,4},{6,7},{7,6},{8,9},{9,8},{10,11... | collective-permute-start | bytes 6152 | tf_op jit(solution)/shard_map/ppermute | solution.py:20
  22.5 37.6 %collective-permute-start.20 = (bf16[256,1024]{1,0:T(8,128)(2,1)}, bf16[256,1024]{1,0:T(8,128)(2,1)S(1)}, u32[]{:S(2)}, u32[]{:S(2)}) collective-permute-start(bf16[256,1024]{1,0:T(8,128)(2,1)} %pad_maximum_fusion.40), channel_id=1, source_target_pairs={{0,6},{2,0},{4,2},{6,4},{1,7},{3,1},{5,3},{7,5},{8,14},{10,8},{12,... | collective-permute-start | bytes 1572872 | tf_op jit(solution)/shard_map/ppermute | solution.py:26
  61.5 327.5 %all-gather.5.cloned.1.call-start = ((), (), s32[]{:S(2)}) async-start(), calls=%async_computation.3 | async-start | bytes 10485760 | tf_op jit(solution)/shard_map/all_gather | solution.py:288
  61.6 33.2 %collective-permute-start = (bf16[128,1024]{1,0:T(8,128)(2,1)S(1)}, bf16[128,1024]{1,0:T(8,128)(2,1)S(1)}, u32[]{:S(2)}, u32[]{:S(2)}) collective-permute-start(bf16[128,1024]{1,0:T(8,128)(2,1)S(1)} %select_bitcast_fusion.7), channel_id=1, source_target_pairs={{0,4},{4,0},{1,5},{5,1},{2,6},{6,2},{3,7},{7,3},{8,12},{12,8},{9,1... | collective-permute-start | bytes 786440 | tf_op jit(solution)/shard_map/ppermute | solution.py:205
  78.5 35.1 %collective-permute-start.25 = (bf16[128,1024]{1,0:T(8,128)(2,1)S(1)}, bf16[128,1024]{1,0:T(8,128)(2,1)S(1)}, u32[]{:S(2)}, u32[]{:S(2)}) collective-permute-start(bf16[128,1024]{1,0:T(8,128)(2,1)S(1)} %pad_maximum_fusion.45), channel_id=1, source_target_pairs={{0,4},{2,6},{4,0},{6,2},{1,5},{3,7},{5,1},{7,3},{8,12},{10,14},{12... | collective-permute-start | bytes 786440 | tf_op jit(solution)/shard_map/ppermute | solution.py:26
  82.0 39.4 %collective-permute-start.26 = (bf16[128,1024]{1,0:T(8,128)(2,1)S(1)}, bf16[128,1024]{1,0:T(8,128)(2,1)S(1)}, u32[]{:S(2)}, u32[]{:S(2)}) collective-permute-start(bf16[128,1024]{1,0:T(8,128)(2,1)S(1)} %pad_maximum_fusion.45), channel_id=1, source_target_pairs={{0,6},{2,0},{4,2},{6,4},{1,7},{3,1},{5,3},{7,5},{8,14},{10,8},{12,... | collective-permute-start | bytes 786440 | tf_op jit(solution)/shard_map/ppermute | solution.py:26
  85.9 44.3 %collective-permute-start.5 = (bf16[144,1024]{1,0:T(8,128)(2,1)S(1)}, bf16[144,1024]{1,0:T(8,128)(2,1)S(1)}, u32[]{:S(2)}, u32[]{:S(2)}) collective-permute-start(bf16[144,1024]{1,0:T(8,128)(2,1)S(1)} %fusion.105), channel_id=1, source_target_pairs={{0,4},{2,6},{4,0},{6,2},{1,5},{3,7},{5,1},{7,3},{8,12},{10,14},{12... | collective-permute-start | bytes 884744 | tf_op jit(solution)/shard_map/ppermute | solution.py:26
  94.8 33.6 %collective-permute-start.4 = (bf16[144,1024]{1,0:T(8,128)(2,1)S(1)}, bf16[144,1024]{1,0:T(8,128)(2,1)S(1)}, u32[]{:S(2)}, u32[]{:S(2)}) collective-permute-start(bf16[144,1024]{1,0:T(8,128)(2,1)S(1)} %fusion.105), channel_id=1, source_target_pairs={{0,2},{2,4},{4,6},{6,0},{1,3},{3,5},{5,7},{7,1},{8,10},{10,12},{12... | collective-permute-start | bytes 884744 | tf_op jit(solution)/shard_map/ppermute | solution.py:26
  95.9 35.3 %collective-permute-start.6 = (bf16[144,1024]{1,0:T(8,128)(2,1)S(1)}, bf16[144,1024]{1,0:T(8,128)(2,1)S(1)}, u32[]{:S(2)}, u32[]{:S(2)}) collective-permute-start(bf16[144,1024]{1,0:T(8,128)(2,1)S(1)} %fusion.105), channel_id=1, source_target_pairs={{0,6},{2,0},{4,2},{6,4},{1,7},{3,1},{5,3},{7,5},{8,14},{10,8},{12,... | collective-permute-start | bytes 884744 | tf_op jit(solution)/shard_map/ppermute | solution.py:26
  113.5 52.1 %collective-permute-start.36 = (bf16[256,1024]{1,0:T(8,128)(2,1)}, bf16[256,1024]{1,0:T(8,128)(2,1)S(1)}, u32[]{:S(2)}, u32[]{:S(2)}) collective-permute-start(bf16[256,1024]{1,0:T(8,128)(2,1)} %pad_maximum_fusion.41), channel_id=1, source_target_pairs={{0,4},{2,6},{4,0},{6,2},{1,5},{3,7},{5,1},{7,3},{8,12},{10,14},{12... | collective-permute-start | bytes 1572872 | tf_op jit(solution)/shard_map/ppermute | solution.py:26
  128.4 99.0 %collective-permute-start.37 = (bf16[256,1024]{1,0:T(8,128)(2,1)}, bf16[256,1024]{1,0:T(8,128)(2,1)}, u32[]{:S(2)}, u32[]{:S(2)}) collective-permute-start(bf16[256,1024]{1,0:T(8,128)(2,1)} %pad_maximum_fusion.41), channel_id=1, source_target_pairs={{0,6},{2,0},{4,2},{6,4},{1,7},{3,1},{5,3},{7,5},{8,14},{10,8},{12,... | collective-permute-start | bytes 1572872 | tf_op jit(solution)/shard_map/ppermute | solution.py:26
  153.1 41.9 %collective-permute-start.1 = (bf16[256,1024]{1,0:T(8,128)(2,1)S(1)}, bf16[256,1024]{1,0:T(8,128)(2,1)S(1)}, u32[]{:S(2)}, u32[]{:S(2)}) collective-permute-start(bf16[256,1024]{1,0:T(8,128)(2,1)S(1)} %pad_maximum_fusion.39), channel_id=1, source_target_pairs={{0,1},{1,0},{2,3},{3,2},{4,5},{5,4},{6,7},{7,6},{8,9},{9,8},{10,11... | collective-permute-start | bytes 1572872 | tf_op jit(solution)/shard_map/ppermute | solution.py:20
  157.1 118.7 %collective-permute-start.27 = (bf16[4,64,1024]{2,1,0:T(8,128)(2,1)}, bf16[4,64,1024]{2,1,0:T(8,128)(2,1)}, u32[]{:S(2)}, u32[]{:S(2)}) collective-permute-start(bf16[4,64,1024]{2,1,0:T(8,128)(2,1)} %get-tuple-element.142), channel_id=1, source_target_pairs={{0,8},{8,0},{1,9},{9,1},{2,10},{10,2},{3,11},{11,3},{4,12},{12,4},... | collective-permute-start | bytes 1572872 | tf_op jit(solution)/shard_map/ppermute | solution.py:26
  165.7 42.9 %collective-permute-start.10 = (bf16[2,4,80,1024]{3,2,1,0:T(8,128)(2,1)S(1)}, bf16[2,4,80,1024]{3,2,1,0:T(8,128)(2,1)S(1)}, u32[]{:S(2)}, u32[]{:S(2)}) collective-permute-start(bf16[2,4,80,1024]{3,2,1,0:T(8,128)(2,1)S(1)} %bitcast_dynamic-update-slice_fusion.8), channel_id=1, source_target_pairs={{0,8},{8,0},{1,9},{9,1},{2,10},{10,2},{3,11},{11,3},{4,12},{12,4},... | collective-permute-start | bytes 3932168 | tf_op jit(solution)/shard_map/ppermute | solution.py:26
  194.6 77.7 %collective-permute-start.29 = (bf16[4,64,1024]{2,1,0:T(8,128)(2,1)}, bf16[4,64,1024]{2,1,0:T(8,128)(2,1)}, u32[]{:S(2)}, u32[]{:S(2)}) collective-permute-start(bf16[4,64,1024]{2,1,0:T(8,128)(2,1)} %get-tuple-element.143), channel_id=1, source_target_pairs={{0,16},{16,0},{1,17},{17,1},{2,18},{18,2},{3,19},{19,3},{4,20},{20... | collective-permute-start | bytes 1572872 | tf_op jit(solution)/shard_map/ppermute | solution.py:26
  215.7 35.1 %collective-permute-start.11 = (bf16[512,1024]{1,0:T(8,128)(2,1)}, bf16[512,1024]{1,0:T(8,128)(2,1)}, u32[]{:S(2)}, u32[]{:S(2)}) collective-permute-start(bf16[512,1024]{1,0:T(8,128)(2,1)} %pad_maximum_fusion.9), channel_id=1, source_target_pairs={{0,2},{2,0},{1,3},{3,1},{4,6},{6,4},{5,7},{7,5},{8,10},{10,8},{9,1... | collective-permute-start | bytes 3145736 | tf_op jit(solution)/shard_map/ppermute | solution.py:342
  229.4 572.6 %reduce-scatter.5.cloned.1.call-start = ((), (), s32[]{:S(2)}) async-start(), calls=%async_computation.5 | async-start | bytes 10485760 | tf_op jit(solution)/shard_map/reduce_scatter | solution.py:436
  274.3 48.6 %collective-permute-start.30 = (bf16[2,4,64,1024]{3,2,1,0:T(8,128)(2,1)}, bf16[2,4,64,1024]{3,2,1,0:T(8,128)(2,1)}, u32[]{:S(2)}, u32[]{:S(2)}) collective-permute-start(bf16[2,4,64,1024]{3,2,1,0:T(8,128)(2,1)} %bitcast_dynamic-update-slice_fusion.14), channel_id=1, source_target_pairs={{0,8},{8,0},{1,9},{9,1},{2,10},{10,2},{3,11},{11,3},{4,12},{12,4},... | collective-permute-start | bytes 3145736 | tf_op jit(solution)/shard_map/ppermute | solution.py:26
  277.7 48.5 %collective-permute-start.28 = (bf16[2,4,64,1024]{3,2,1,0:T(8,128)(2,1)}, bf16[2,4,64,1024]{3,2,1,0:T(8,128)(2,1)}, u32[]{:S(2)}, u32[]{:S(2)}) collective-permute-start(bf16[2,4,64,1024]{3,2,1,0:T(8,128)(2,1)} %bitcast_dynamic-update-slice_fusion.16), channel_id=1, source_target_pairs={{0,16},{16,0},{1,17},{17,1},{2,18},{18,2},{3,19},{19,3},{4,20},{20... | collective-permute-start | bytes 3145736 | tf_op jit(solution)/shard_map/ppermute | solution.py:26
  341.0 39.9 %collective-permute-start.32 = (bf16[512,512]{0,1:T(8,128)(2,1)}, bf16[512,512]{0,1:T(8,128)(2,1)}, u32[]{:S(2)}, u32[]{:S(2)}) collective-permute-start(bf16[512,512]{0,1:T(8,128)(2,1)} %get-tuple-element.141), channel_id=1, source_target_pairs={{0,1},{1,0},{2,3},{3,2},{4,5},{5,4},{6,7},{7,6},{8,9},{9,8},{10,11... | collective-permute-start | bytes 1572872 | tf_op jit(solution)/shard_map/ppermute | solution.py:20
  448.7 367.7 %reduce-scatter.3.cloned.1.call-start = ((), (), s32[]{:S(2)}) async-start(), calls=%async_computation.4 | async-start | bytes 10485760 | tf_op jit(solution)/shard_map/reduce_scatter | solution.py:436
  467.1 256.5 %collective-permute-start.39 = (bf16[128,1024]{1,0:T(8,128)(2,1)}, bf16[128,1024]{1,0:T(8,128)(2,1)}, u32[]{:S(2)}, u32[]{:S(2)}) collective-permute-start(bf16[128,1024]{1,0:T(8,128)(2,1)} %get-tuple-element.174), channel_id=1, source_target_pairs={{0,4},{4,0},{1,5},{5,1},{2,6},{6,2},{3,7},{7,3},{8,12},{12,8},{9,1... | collective-permute-start | bytes 786440 | tf_op jit(solution)/shard_map/ppermute | solution.py:214
  638.0 87.5 %collective-permute-start.69 = (f32[2,32,2,512]{3,2,1,0:T(2,128)}, f32[2,32,2,512]{3,2,1,0:T(2,128)}, u32[]{:S(2)}, u32[]{:S(2)}) collective-permute-start(f32[2,32,2,512]{3,2,1,0:T(2,128)} %get-tuple-element.172), channel_id=1, source_target_pairs={{0,1},{1,0},{2,3},{3,2},{4,5},{5,4},{6,7},{7,6},{8,9},{9,8},{10,11... | collective-permute-start | bytes 786440 | tf_op jit(solution)/shard_map/ppermute | solution.py:20
  721.6 31.7 %collective-permute-start.55 = (bf16[2,4,80,1024]{3,2,1,0:T(8,128)(2,1)S(1)}, bf16[2,4,80,1024]{3,2,1,0:T(8,128)(2,1)S(1)}, u32[]{:S(2)}, u32[]{:S(2)}) collective-permute-start(bf16[2,4,80,1024]{3,2,1,0:T(8,128)(2,1)S(1)} %fusion.40), channel_id=1, source_target_pairs={{0,8},{8,0},{1,9},{9,1},{2,10},{10,2},{3,11},{11,3},{4,12},{12,4},... | collective-permute-start | bytes 3932168 | tf_op jit(solution)/shard_map/ppermute | solution.py:40
  754.8 36.9 %collective-permute-start.51 = (f32[128,1024]{1,0:T(8,128)S(1)}, f32[128,1024]{1,0:T(8,128)S(1)}, u32[]{:S(2)}, u32[]{:S(2)}) collective-permute-start(f32[128,1024]{1,0:T(8,128)S(1)} %get-tuple-element.139), channel_id=1, source_target_pairs={{0,4},{4,0},{1,5},{5,1},{2,6},{6,2},{3,7},{7,3},{8,12},{12,8},{9,1... | collective-permute-start | bytes 1572872 | tf_op jit(solution)/shard_map/ppermute | solution.py:214
  815.8 53.5 %collective-permute-start.76 = (bf16[256,1024]{1,0:T(8,128)(2,1)S(1)}, bf16[256,1024]{1,0:T(8,128)(2,1)}, u32[]{:S(2)}, u32[]{:S(2)}) collective-permute-start(bf16[256,1024]{1,0:T(8,128)(2,1)S(1)} %get-tuple-element.114), channel_id=1, source_target_pairs={{0,4},{2,6},{4,0},{6,2},{1,5},{3,7},{5,1},{7,3},{8,12},{10,14},{12... | collective-permute-start | bytes 1572872 | tf_op jit(solution)/shard_map/ppermute | solution.py:40
  819.0 50.3 %collective-permute-start.71 = (bf16[256,1024]{1,0:T(8,128)(2,1)}, bf16[256,1024]{1,0:T(8,128)(2,1)}, u32[]{:S(2)}, u32[]{:S(2)}) collective-permute-start(bf16[256,1024]{1,0:T(8,128)(2,1)} %get-tuple-element.109), channel_id=1, source_target_pairs={{0,2},{2,4},{4,6},{6,0},{1,3},{3,5},{5,7},{7,1},{8,10},{10,12},{12... | collective-permute-start | bytes 1572872 | tf_op jit(solution)/shard_map/ppermute | solution.py:40
  820.9 48.3 %collective-permute-start.73 = (bf16[256,1024]{1,0:T(8,128)(2,1)}, bf16[256,1024]{1,0:T(8,128)(2,1)}, u32[]{:S(2)}, u32[]{:S(2)}) collective-permute-start(bf16[256,1024]{1,0:T(8,128)(2,1)} %get-tuple-element.110), channel_id=1, source_target_pairs={{0,6},{2,0},{4,2},{6,4},{1,7},{3,1},{5,3},{7,5},{8,14},{10,8},{12,... | collective-permute-start | bytes 1572872 | tf_op jit(solution)/shard_map/ppermute | solution.py:40
  824.2 78.3 %collective-permute-start.72 = (bf16[256,1024]{1,0:T(8,128)(2,1)}, bf16[256,1024]{1,0:T(8,128)(2,1)}, u32[]{:S(2)}, u32[]{:S(2)}) collective-permute-start(bf16[256,1024]{1,0:T(8,128)(2,1)} %get-tuple-element.111), channel_id=1, source_target_pairs={{0,4},{2,6},{4,0},{6,2},{1,5},{3,7},{5,1},{7,3},{8,12},{10,14},{12... | collective-permute-start | bytes 1572872 | tf_op jit(solution)/shard_map/ppermute | solution.py:40
  (227 other events, 2595.6 us)
Sparse Core Ops, SparseCore 0:
  61.6 117.7 all-gather.2
  229.5 110.9 all-gather.4
  448.8 86.4 reduce-scatter.4
  577.3 97.2 reduce-scatter.2

commit v2 on v1

v2 whole, which is shorter than its diff:
```python
import jax
import jax.numpy as jnp
from jax import lax
from jax.experimental import pallas as pl
from jax.experimental.pallas import tpu as pltpu
from jax.sharding import Mesh, PartitionSpec as P

HEAD = 64
PAIR = 2 * HEAD
BLOCK = 256
WIDE = 1024
EPSILON = 1e-05
NEG_FILL = -1e30
ROOT_HALF = 0.7071067811865476
ROOT_TWO_PI = 0.3989422804014327
BF = jnp.bfloat16
F32 = jnp.float32
VMEM_BYTES = 56 * 1024 * 1024

def matmul(left, right):
    return jnp.dot(left, right, preferred_element_type=F32)


def matmul_tn(left, right):
    return lax.dot_general(left, right, (((0,), (0,)), ((), ())), preferred_element_type=F32)


def matmul_nt(left, right):
    return lax.dot_general(left, right, (((1,), (1,)), ((), ())), preferred_element_type=F32)


def params(*semantics):
    return pltpu.CompilerParams(dimension_semantics=semantics, vmem_limit_bytes=VMEM_BYTES)


def one_head(value, lane, head):
    mine = lane < HEAD if head == 0 else lane >= HEAD
    return jnp.where(mine, value, jnp.zeros_like(value))


def attend_forward_kernel(q_ref, k_ref, v_ref, col_ref, row_ref, c_ref, log_ref):
    lane = lax.broadcasted_iota(jnp.int32, (BLOCK, PAIR), 1)

    def block(index, carry):
        at = pl.ds(pl.multiple_of(index * BLOCK, BLOCK), BLOCK)
        query = q_ref[at, :]
        allowed = col_ref[at, :] == row_ref[...]
        found, logs = [], []
        for head in (0, 1):
            scores = matmul_nt(one_head(query, lane, head), k_ref[...])
            scores = jnp.where(allowed, scores, NEG_FILL)
            top = jnp.max(scores, axis=1, keepdims=True)
            raised = jnp.exp(scores - top)
            total = jnp.sum(raised, axis=1, keepdims=True)
            found.append(matmul(raised.astype(BF), v_ref[...]) * (1.0 / total))
            logs.append(top + jnp.log(total))
        c_ref[at, :] = jnp.where(lane < HEAD, found[0], found[1]).astype(BF)
        log_ref[:, at] = jnp.where(lane < 1, logs[0], logs[1]).T[:8]
        return carry

    lax.fori_loop(0, q_ref.shape[0] // BLOCK, block, 0)


def pair_specs(tokens):
    return [
        pl.BlockSpec((tokens, PAIR), lambda p: (0, 2 * p)),
        pl.BlockSpec((tokens, PAIR), lambda p: (0, 2 * p + 1)),
        pl.BlockSpec((tokens, PAIR), lambda p: (0, p)),
    ]


def docs_specs(tokens):
    return [
        pl.BlockSpec((tokens, 1), lambda p: (0, 0)),
        pl.BlockSpec((1, tokens), lambda p: (0, 0)),
    ]


def attend_forward(query_key, value, docs):
    tokens, width = value.shape
    pairs = width // PAIR
    return pl.pallas_call(
        attend_forward_kernel,
        grid=(pairs,),
        in_specs=pair_specs(tokens) + docs_specs(tokens),
        out_specs=[
            pl.BlockSpec((tokens, PAIR), lambda p: (0, p)),
            pl.BlockSpec((8, tokens), lambda p: (p, 0)),
        ],
        out_shape=[
            jax.ShapeDtypeStruct((tokens, width), BF),
            jax.ShapeDtypeStruct((8 * pairs, tokens), F32),
        ],
        compiler_params=params("arbitrary"),
        cost_estimate=pl.CostEstimate(
            flops=16 * tokens * tokens * width,
            bytes_accessed=10 * tokens * width,
            transcendentals=tokens * tokens * width // HEAD,
        ),
    )(query_key, query_key, value, docs[:, None], docs[None])


def attend_backward_kernel(
    q_ref, k_ref, v_ref, g_ref, col_ref, row_ref, log_ref, dqk_ref, dv_ref, kt_ref, key_ref, value_ref
):
    lane = lax.broadcasted_iota(jnp.int32, (BLOCK, PAIR), 1)
    down = lax.broadcasted_iota(jnp.int32, (PAIR, BLOCK), 0)
    kt_ref[...] = k_ref[...].T
    key_ref[...] = jnp.zeros_like(key_ref)
    value_ref[...] = jnp.zeros_like(value_ref)

    def block(index, carry):
        at = pl.ds(pl.multiple_of(index * BLOCK, BLOCK), BLOCK)
        query, grad = q_ref[at, :], g_ref[at, :]
        allowed = col_ref[...] == row_ref[:, at]
        found = []
        for head in (0, 1):
            query_one, grad_one = one_head(query, lane, head), one_head(grad, lane, head)
            scores = matmul_nt(k_ref[...], query_one)
            soft = jnp.exp(jnp.where(allowed, scores, NEG_FILL) - log_ref[head : head + 1, at])
            grad_soft = matmul_nt(v_ref[...], grad_one)
            delta = jnp.sum(soft * grad_soft, axis=0, keepdims=True)
            low = (soft * (grad_soft - delta)).astype(BF)
            value_ref[...] += matmul(soft.astype(BF), grad_one)
            key_ref[...] += matmul(low, query_one)
            found.append(matmul(kt_ref[...], low))
        dq = jnp.where(down < HEAD, found[0], found[1]) * HEAD ** (-0.5)
        dqk_ref[at, :PAIR] = dq.T.astype(BF)
        return carry

    lax.fori_loop(0, q_ref.shape[0] // BLOCK, block, 0)
    dqk_ref[:, PAIR:] = key_ref[...].astype(BF)
    dv_ref[...] = value_ref[...].astype(BF)


def attend_backward(grad, query_key, value, logs, docs):
    tokens, width = grad.shape
    pairs = width // PAIR
    return pl.pallas_call(
        attend_backward_kernel,
        grid=(pairs,),
        in_specs=pair_specs(tokens)
        + [pl.BlockSpec((tokens, PAIR), lambda p: (0, p))]
        + docs_specs(tokens)
        + [pl.BlockSpec((8, tokens), lambda p: (p, 0))],
        out_specs=[
            pl.BlockSpec((tokens, 2 * PAIR), lambda p: (0, p)),
            pl.BlockSpec((tokens, PAIR), lambda p: (0, p)),
        ],
        out_shape=[
            jax.ShapeDtypeStruct((tokens, 2 * width), BF),
            jax.ShapeDtypeStruct((tokens, width), BF),
        ],
        scratch_shapes=[
            pltpu.VMEM((PAIR, tokens), BF),
            pltpu.VMEM((tokens, PAIR), F32),
            pltpu.VMEM((tokens, PAIR), F32),
        ],
        compiler_params=params("arbitrary"),
        cost_estimate=pl.CostEstimate(
            flops=40 * tokens * tokens * width,
            bytes_accessed=18 * tokens * width,
            transcendentals=tokens * tokens * width // HEAD,
        ),
    )(query_key, query_key, value, grad, docs[:, None], docs[None], logs)


def join(ref, first, second):
    half = first.shape[0]
    ref[:half, :] = first[...]
    ref[half:, :] = second[...]


def ffn_forward_kernel(
    x0_ref, x1_ref, w1_ref, w2_ref, b_ref, own_ref, give_ref, u_ref, x_ref, total_ref
):
    step = pl.program_id(0)
    tile = b_ref.shape[1]

    @pl.when(step == 0)
    def _():
        join(x_ref, x0_ref, x1_ref)

    expanded = matmul(x_ref[...], w1_ref[...].reshape(WIDE, tile)) + b_ref[...]
    u_ref[...] = expanded
    active = (expanded * (0.5 + 0.5 * lax.erf(expanded * ROOT_HALF))).astype(BF)
    part = matmul(active, w2_ref[...].reshape(tile, WIDE))

    @pl.when(step == 0)
    def _():
        total_ref[...] = part

    @pl.when(step > 0)
    def _():
        total_ref[...] += part

    @pl.when(step == pl.num_programs(0) - 1)
    def _():
        half = own_ref.shape[0]
        own_ref[...] = total_ref[:half, :]
        give_ref[...] = total_ref[half:, :].astype(BF)


def ffn_specs(packed, tile):
    chips, rows = packed.shape[0], packed.shape[1]
    per_half = WIDE // tile
    return [
        pl.BlockSpec((chips, rows // 4, tile), lambda t: (0, t // per_half, t % per_half)),
        pl.BlockSpec((tile * chips // (2 * WIDE), rows // 2, WIDE), lambda t: (t, 1, 0)),
    ]


def ffn_forward(rows_low, packed, bias):
    tokens, tile = 2 * rows_low[0].shape[0], 512
    half = pl.BlockSpec((tokens // 2, WIDE), lambda t: (0, 0))
    return pl.pallas_call(
        ffn_forward_kernel,
        grid=(2 * WIDE // tile,),
        in_specs=[half, half]
        + ffn_specs(packed, tile)
        + [pl.BlockSpec((1, tile), lambda t: (0, t))],
        out_specs=[
            pl.BlockSpec((tokens // 2, WIDE), lambda t: (0, 0)),
            pl.BlockSpec((tokens // 2, WIDE), lambda t: (0, 0)),
            pl.BlockSpec((tokens, tile), lambda t: (0, t)),
        ],
        out_shape=[
            jax.ShapeDtypeStruct((tokens // 2, WIDE), F32),
            jax.ShapeDtypeStruct((tokens // 2, WIDE), BF),
            jax.ShapeDtypeStruct((tokens, 2 * WIDE), F32),
        ],
        scratch_shapes=[pltpu.VMEM((tokens, WIDE), BF), pltpu.VMEM((tokens, WIDE), F32)],
        compiler_params=params("arbitrary"),
        cost_estimate=pl.CostEstimate(
            flops=8 * tokens * WIDE * WIDE,
            bytes_accessed=16 * WIDE * WIDE + 16 * tokens * WIDE,
            transcendentals=2 * tokens * WIDE,
        ),
    )(*rows_low, packed, packed, bias[None])


def ffn_backward_kernel(
    g0_ref,
    g1_ref,
    x0_ref,
    x1_ref,
    u_ref,
    w1_ref,
    w2_ref,
    own_ref,
    give_ref,
    db_ref,
    dw_ref,
    g_ref,
    xt_ref,
    total_ref,
):
    step = pl.program_id(0)
    tile = u_ref.shape[1]
    chips, rows = dw_ref.shape[0], dw_ref.shape[1]
    quarter = rows // 4
    per_half = WIDE // tile
    group = tile * chips // (2 * WIDE)

    @pl.when(step == 0)
    def _():
        join(g_ref, g0_ref, g1_ref)
        half = x0_ref.shape[0]
        xt_ref[:, :half] = x0_ref[...].T
        xt_ref[:, half:] = x1_ref[...].T
        total_ref[...] = jnp.zeros_like(total_ref)

    grad = g_ref[...]
    expanded = u_ref[...]
    normal = 0.5 + 0.5 * lax.erf(expanded * ROOT_HALF)
    active = (expanded * normal).astype(BF)
    slope = normal + expanded * (ROOT_TWO_PI * jnp.exp(-0.5 * expanded * expanded))
    dw2 = matmul_tn(active, grad)
    dw_ref[pl.ds(step * group, group), 2 * quarter :, :] = dw2.astype(BF).reshape(group, 2 * quarter, WIDE)
    low = (matmul_nt(grad, w2_ref[...].reshape(tile, WIDE)) * slope).astype(BF)
    db_ref[...] = jnp.sum(low.astype(F32), axis=0, keepdims=True)
    dw1 = matmul(xt_ref[...], low).astype(BF).reshape(chips, quarter, tile)
    dw_ref[:, pl.ds(pl.multiple_of((step // per_half) * quarter, quarter), quarter),
           pl.ds(pl.multiple_of((step % per_half) * tile, tile), tile)] = dw1
    total_ref[...] += matmul_nt(low, w1_ref[...].reshape(WIDE, tile))

    @pl.when(step == pl.num_programs(0) - 1)
    def _():
        half = own_ref.shape[0]
        own_ref[...] = total_ref[:half, :]
        give_ref[...] = total_ref[half:, :].astype(BF)


def ffn_backward(grad_low, rows_low, expanded, packed):
    tokens, tile = 2 * rows_low[0].shape[0], 256
    half = pl.BlockSpec((tokens // 2, WIDE), lambda t: (0, 0))
    return pl.pallas_call(
        ffn_backward_kernel,
        grid=(2 * WIDE // tile,),
        in_specs=[half] * 4
        + [pl.BlockSpec((tokens, tile), lambda t: (0, t))]
        + ffn_specs(packed, tile),
        out_specs=[
            pl.BlockSpec((tokens // 2, WIDE), lambda t: (0, 0)),
            pl.BlockSpec((tokens // 2, WIDE), lambda t: (0, 0)),
            pl.BlockSpec((1, tile), lambda t: (0, t)),
            pl.BlockSpec(packed.shape, lambda t: (0, 0, 0)),
        ],
        out_shape=[
            jax.ShapeDtypeStruct((tokens // 2, WIDE), F32),
            jax.ShapeDtypeStruct((tokens // 2, WIDE), BF),
            jax.ShapeDtypeStruct((1, 2 * WIDE), F32),
            jax.ShapeDtypeStruct(packed.shape, BF),
        ],
        scratch_shapes=[
            pltpu.VMEM((tokens, WIDE), BF),
            pltpu.VMEM((WIDE, tokens), BF),
            pltpu.VMEM((tokens, WIDE), F32),
        ],
        compiler_params=params("arbitrary"),
        cost_estimate=pl.CostEstimate(
            flops=16 * tokens * WIDE * WIDE,
            bytes_accessed=16 * WIDE * WIDE + 20 * tokens * WIDE,
            transcendentals=4 * tokens * WIDE,
        ),
    )(*grad_low, *rows_low, expanded, packed, packed)


def shift_perm(count, step):
    return [(i, (i + step) % count) for i in range(count)]


def swap_core(value):
    return lax.ppermute(value, "c", [(0, 1), (1, 0)])


def gather_shift(value, axis, count, dim):
    place = lax.axis_index(axis)
    out = jnp.zeros(value.shape[:dim] + (count,) + value.shape[dim:], value.dtype)
    for step in range(count):
        piece = lax.ppermute(value, axis, shift_perm(count, step)) if step else value
        out = lax.dynamic_update_index_in_dim(out, piece, (place - step) % count, dim)
    return out


def scatter_shift(value, axis, count, dim):
    place = lax.axis_index(axis)

    def piece(step):
        return lax.dynamic_index_in_dim(value, (place + step) % count, dim, keepdims=False)

    got = [lax.ppermute(piece(step), axis, shift_perm(count, step)) for step in range(1, count)]
    total = piece(0).astype(F32)
    for part in got:
        total = total + part.astype(F32)
    return total


def together(*values):
    return lax.optimization_barrier(values)


def layer_norm(rows, gain, shift):
    mean = jnp.mean(rows, axis=-1, keepdims=True)
    centred = rows - mean
    variance = jnp.mean(centred * centred, axis=-1, keepdims=True)
    return centred * lax.rsqrt(variance + EPSILON) * gain + shift


def layer_norm_back(grad, rows, gain):
    mean = jnp.mean(rows, axis=-1, keepdims=True)
    centred = rows - mean
    variance = jnp.mean(centred * centred, axis=-1, keepdims=True)
    inverse = lax.rsqrt(variance + EPSILON)
    hat = centred * inverse
    grad_hat = grad * gain
    grad_rows = inverse * (
        grad_hat
        - jnp.mean(grad_hat, axis=-1, keepdims=True)
        - hat * jnp.mean(grad_hat * hat, axis=-1, keepdims=True)
    )
    return grad_rows, jnp.sum(grad * hat, axis=0), jnp.sum(grad, axis=0)


def make_body(n_fa, n_fb, n_h, n_m):
    n_f, n_z = n_fa * n_fb, n_h * n_m
    n_chip, n_s = n_f * n_z, 2 * n_z
    team = 2 * n_m
    width = WIDE // team
    pairs = width // PAIR
    extra = PAIR

    def both_cores(value):
        return jnp.concatenate([value, swap_core(value)], axis=0)

    def team_rows(value):
        parts = [value] + [
            lax.ppermute(value, "m", shift_perm(n_m, step)) for step in range(1, n_m)
        ]
        return [both_cores(part) for part in parts]

    def team_sum(make):
        total = 0.0
        for step in reversed(range(n_m)):
            part = make(step)
            half = part.shape[0] // 2
            part = part[:half] + swap_core(part[half:].astype(BF)).astype(F32)
            if step:
                part = lax.ppermute(part.astype(BF), "m", shift_perm(n_m, -step)).astype(F32)
            total = total + part
        return total

    def pair_up(first, second):
        shape = first.shape[:-1]
        first = first.reshape(shape + (pairs, 1, PAIR))
        second = second.reshape(shape + (pairs, 1, PAIR))
        return jnp.concatenate([first, second], axis=-2).reshape(shape + (2 * width,))

    def body(
        layer_input,
        documents,
        cotangent,
        attend_weight,
        attend_bias,
        output_weight,
        output_bias,
        norm_gain,
        norm_shift,
        expand_weight,
        expand_bias,
        reduce_weight,
        reduce_bias,
    ):
        core, half = lax.axis_index("c"), lax.axis_index("h")
        rank = lax.axis_index(("m", "c"))
        layers = attend_weight.shape[0]
        tokens = layer_input.shape[1]
        rows0 = attend_weight.shape[2]
        rows1 = 2 * rows0
        units = reduce_weight.shape[1]
        lots = units // rows0
        lanes_of = 8 + lots

        def by_core(own, other, axis):
            return jnp.where(
                core == 0,
                jnp.concatenate([own, other], axis=axis),
                jnp.concatenate([other, own], axis=axis),
            )

        def to_halves(pair):
            keep = jnp.where(half == 0, pair[0], pair[1])
            give = jnp.where(half == 0, pair[1], pair[0])
            got = lax.ppermute(give, "h", [(0, 1), (1, 0)])
            first = jnp.where(half == 0, keep, got)
            last = jnp.where(half == 0, got, keep)
            return jnp.concatenate([first, last], axis=0)

        def from_halves(rows):
            first, last = rows[:tokens], rows[tokens:]
            keep = jnp.where(half == 0, first, last)
            give = jnp.where(half == 0, last, first)
            got = lax.ppermute(give, "h", [(0, 1), (1, 0)])
            return jnp.where(half == 0, jnp.stack([keep, got]), jnp.stack([got, keep]))

        def small_lanes(layer):
            return jnp.concatenate(
                [
                    attend_bias[layer],
                    output_bias[layer][None],
                    norm_gain[layer],
                    norm_shift[layer],
                    reduce_bias[layer][None],
                    expand_bias[layer].reshape(lots, rows0),
                ],
                axis=0,
            )

        small = jnp.concatenate([small_lanes(layer) for layer in range(layers)], axis=0)
        small = jnp.pad(small.astype(BF).T, ((0, 0), (0, extra - layers * lanes_of)))

        def attn_shard(layer):
            wa = attend_weight[layer].astype(BF).reshape(3, rows0, team, width)
            wo = output_weight[layer].astype(BF).reshape(rows0, team, width)
            packed = jnp.concatenate([pair_up(wa[0], wa[1]), wa[2], wo], axis=-1)
            packed = jnp.swapaxes(packed, 0, 1)
            if layer == 0:
                more = jnp.broadcast_to(small[None], (team,) + small.shape)
                packed = jnp.concatenate([packed, more], axis=-1)
            return jnp.broadcast_to(packed[None], (n_h,) + packed.shape).reshape((n_s,) + packed.shape[1:])

        def column_attn(shard):
            column = lax.all_to_all(shard, ("h", "m", "c"), 0, 0, tiled=True)
            return column.reshape(n_s * rows0, -1)

        def gather_attn(column):
            first, second = column[:, : 2 * width], column[:, 2 * width :]
            first = gather_shift(gather_shift(first, "fb", n_fb, 0), "fa", n_fa, 0)
            second = gather_shift(gather_shift(second, "fa", n_fa, 0), "fb", n_fb, 1)
            first, second = first.reshape(WIDE, -1), second.reshape(WIDE, -1)
            out = second[:, width : 2 * width].reshape(team, width, width)
            out = lax.all_to_all(out, ("m", "c"), 0, 0, tiled=True)
            out = jnp.swapaxes(out, 0, 1).reshape(width, WIDE)
            return (first, second[:, :width], out), second[:, 2 * width :]

        def ffn_shard(layer):
            w1 = expand_weight[layer].astype(BF).reshape(rows0, -1, 2, units)
            own = jnp.where(core == 0, w1[:, :, 0], w1[:, :, 1]).reshape(rows0, 2, WIDE)
            give = jnp.where(core == 0, w1[:, :, 1], w1[:, :, 0]).reshape(rows0, 2, WIDE)
            own, give = jnp.swapaxes(own, 0, 1), jnp.swapaxes(give, 0, 1)
            w1 = by_core(own, swap_core(give), 1).reshape(2 * rows1, WIDE)
            shard = jnp.concatenate([w1, reduce_weight[layer].astype(BF)], axis=0)
            return shard

        def column_ffn(shard):
            return gather_shift(shard, ("h", "m"), n_z, 0)

        def gather_ffn(column):
            return lax.all_gather(column, ("fa", "fb"), axis=0, tiled=True)

        attn_w, ffn_w = [None] * layers, [None] * layers
        attn_column = column_attn(attn_shard(0))
        rows_low = to_halves(layer_input)
        parts = team_rows(rows_low)
        parts, attn_column, ffn_part = together(parts, attn_column, ffn_shard(0))
        ffn_column = column_ffn(ffn_part)
        attn_w[0], small_all = gather_attn(attn_column)

        small_all = small_all.T.astype(F32)

        def small_params(layer):
            part = small_all[layer * lanes_of : (layer + 1) * lanes_of]
            bias1 = jnp.swapaxes(part[8:].reshape(lots, n_chip, 2, rows0), 0, 1)
            bias1 = jnp.swapaxes(bias1, 1, 2)
            bias1 = jnp.where(core == 0, bias1[:, 0], bias1[:, 1]).reshape(-1)
            return [part[index] for index in range(8)] + [bias1]

        vectors = [small_params(layer) for layer in range(layers)]

        def own_width(vector):
            return lax.dynamic_slice_in_dim(vector, rank * width, width)

        docs = jnp.concatenate(team_rows(to_halves(documents)))
        scale = pair_up(jnp.full((width,), HEAD ** (-0.5), F32), jnp.ones((width,), F32))

        kept = []
        rows_in = rows_low.astype(F32)
        for layer in range(layers):
            qk_w, v_w, out_w = attn_w[layer]
            bq, bv, bo, gain0, gain1, shift0, shift1, bias2, bias1 = vectors[layer]
            bias_qk = pair_up(own_width(bq), jnp.zeros((width,), F32))
            bias_v = own_width(bv)
            if layer:
                parts = team_rows(rows_low)
            qk = jnp.concatenate([((matmul(p, qk_w) + bias_qk) * scale).astype(BF) for p in parts])
            value = jnp.concatenate([(matmul(p, v_w) + bias_v).astype(BF) for p in parts])
            if layer == 0:
                qk, value, ffn_column = together(qk, value, ffn_column)
                ffn_w[0] = gather_ffn(ffn_column)
                qk, out_w, attn_part, ffn_part, cotangent = together(
                    qk, out_w, attn_shard(1), ffn_shard(1), cotangent
                )
                attn_w[1] = gather_attn(column_attn(attn_part))[0]
                ffn_column = column_ffn(ffn_part)
                grad_rows = to_halves(cotangent).astype(F32)
            context, logs = attend_forward(qk, value, docs)
            chip_rows = parts[0].shape[0]
            first_sum = rows_in + bo + team_sum(
                lambda step: matmul(context[step * chip_rows : (step + 1) * chip_rows], out_w)
            )
            first_norm = layer_norm(first_sum, gain0, shift0)
            norm_low = first_norm.astype(BF)
            chip_norm = (norm_low, swap_core(norm_low))
            if layer == 0:
                chip_norm, attn_w[1], ffn_column = together(chip_norm, attn_w[1], ffn_column)
                ffn_w[1] = gather_ffn(ffn_column)
            reduced, give, expanded = ffn_forward(chip_norm, ffn_w[layer], bias1)
            second_sum = first_norm + (reduced + swap_core(give).astype(F32) + bias2)
            rows_in = layer_norm(second_sum, gain1, shift1)
            kept.append((parts, qk, value, context, logs, first_sum, chip_norm, expanded, second_sum))
            rows_low = rows_in.astype(BF)
        layer_output = from_halves(rows_low)

        def own_ffn(mine):
            w1 = mine[:, : 2 * rows1].reshape(layers, 2, rows1, WIDE)
            keep = jnp.where(core == 0, w1[:, :, :rows0], w1[:, :, rows0:])
            give = jnp.where(core == 0, w1[:, :, rows0:], w1[:, :, :rows0])
            got = swap_core(give)
            keep = jnp.swapaxes(keep, 1, 2).reshape(layers, rows0, -1, 1, units)
            got = jnp.swapaxes(got, 1, 2).reshape(layers, rows0, -1, 1, units)
            return by_core(keep, got, 3).reshape(layers, rows0, -1), mine[:, 2 * rows1 :]

        def scatter_attn(first, second):
            first = first.reshape(n_fa, n_fb, n_s * rows0, -1)
            second = second.reshape(n_fa, n_fb, n_s * rows0, -1)
            first = scatter_shift(first, "fa", n_fa, 0).astype(BF)
            second = scatter_shift(second, "fb", n_fb, 1).astype(BF)
            return first, second

        def finish_attn(first, second):
            first = scatter_shift(first, "fb", n_fb, 0)
            second = scatter_shift(second, "fa", n_fa, 0)
            column = jnp.concatenate([first, second], axis=1).astype(BF)
            return column.reshape(n_s, rows0, -1)

        def own_attn(columns):
            column = jnp.concatenate(columns, axis=-1)
            pieces = lax.all_to_all(column, ("h", "m", "c"), 0, 0, tiled=True)
            pieces = jnp.sum(pieces.reshape((n_h, team, rows0, -1)).astype(F32), axis=0)
            fours = pieces[..., : 4 * width * layers].reshape(team, rows0, layers, 4 * width)
            qk = fours[..., : 2 * width].reshape(team, rows0, layers, pairs, 2, PAIR)
            query = qk[..., 0, :].reshape(team, rows0, layers, width)
            key = qk[..., 1, :].reshape(team, rows0, layers, width)
            value, out = fours[..., 2 * width : 3 * width], fours[..., 3 * width :]

            def whole(four):
                return jnp.transpose(four, (2, 1, 0, 3)).reshape(layers, rows0, WIDE)

            wa = jnp.stack([whole(query), whole(key), whole(value)], axis=1)
            return wa, whole(out), jnp.sum(pieces[..., 4 * width * layers :], axis=0)

        attn_columns, ffn_mine = [None] * layers, [None] * layers
        small_grads = [None] * layers
        for layer in reversed(range(layers)):
            parts, qk, value, context, logs, first_sum, chip_norm, expanded, second_sum = kept[layer]
            (qk_w, v_w, out_w), ffn = attn_w[layer], ffn_w[layer]
            gain0, gain1 = vectors[layer][3], vectors[layer][4]
            grad_second, dgain1, dshift1 = layer_norm_back(grad_rows, second_sum, gain1)
            grad_low = grad_second.astype(BF)
            dbias2 = jnp.sum(grad_low, axis=0, dtype=F32)
            chip_low = (grad_low, swap_core(grad_low))
            if layer + 1 < layers:
                chip_low, attn_half = together(chip_low, attn_half)
            reduced, give, dbias1, packed = ffn_backward(chip_low, chip_norm, expanded, ffn)
            if layer + 1 < layers:
                attn_columns[layer + 1] = finish_attn(*attn_half)
                ffn_last = ffn_column
            ffn_column = lax.psum_scatter(packed, ("fa", "fb"), scatter_dimension=0, tiled=True)
            grad_first = grad_second + (reduced + swap_core(give).astype(F32))
            grad_sum, dgain0, dshift0 = layer_norm_back(grad_first, first_sum, gain0)
            grad_low = grad_sum.astype(BF)
            dbo = jnp.sum(grad_low, axis=0, dtype=F32)
            grads = team_rows(grad_low)
            if layer + 1 < layers:
                grads, ffn_last = together(grads, ffn_last)
                ffn_mine[layer + 1] = scatter_shift(ffn_last, ("h", "m"), n_z, 0)
            grad_context = jnp.concatenate([matmul_nt(g, out_w).astype(BF) for g in grads])
            chip_rows = grads[0].shape[0]

            def piece(rows, step):
                return rows[step * chip_rows : (step + 1) * chip_rows]

            grad_out = sum(matmul_tn(piece(context, step), g) for step, g in enumerate(grads))
            grad_out = jnp.swapaxes(grad_out.astype(BF).reshape(width, team, width), 0, 1)
            grad_out = lax.all_to_all(grad_out, ("m", "c"), 0, 0, tiled=True).reshape(WIDE, width)
            if layer + 1 == layers:
                grad_context, layer_output = together(grad_context, layer_output)
            dqk, dv = attend_backward(grad_context, qk, value, logs, docs)
            if layer + 1 < layers:
                dqk, ffn_mine[layer + 1], attn_columns[layer + 1] = together(
                    dqk, ffn_mine[layer + 1], attn_columns[layer + 1]
                )
            grad_qk = sum(matmul_tn(p, piece(dqk, step)) for step, p in enumerate(parts)).astype(BF)
            grad_v = sum(matmul_tn(p, piece(dv, step)) for step, p in enumerate(parts)).astype(BF)
            dqk, dv, grad_qk, grad_v = together(dqk, dv, grad_qk, grad_v)
            grad_rows = grad_sum + team_sum(
                lambda step: matmul_nt(piece(dqk, step), qk_w) + matmul_nt(piece(dv, step), v_w)
            )
            dbq = jnp.sum(dqk.reshape(-1, pairs, 2, PAIR)[:, :, 0], axis=0, dtype=F32)
            dbv = jnp.sum(dv, axis=0, dtype=F32)

            def spread(vector):
                blank = jnp.zeros((WIDE,), F32)
                return lax.dynamic_update_slice_in_dim(blank, vector.reshape(-1), rank * width, 0)

            dbias1 = dbias1.reshape(n_chip, 1, lots, rows0)
            dbias1 = by_core(dbias1, jnp.zeros_like(dbias1), 1).reshape(2 * n_chip, lots, rows0)
            dbias1 = jnp.swapaxes(dbias1, 0, 1).reshape(lots, WIDE)
            small_grads[layer] = jnp.concatenate(
                [
                    jnp.stack(
                        [spread(dbq), spread(dbv), dbo, dgain0, dgain1, dshift0, dshift1, dbias2]
                    ),
                    dbias1,
                ]
            )
            second = [grad_v, grad_out]
            if layer == 0:
                lanes = jnp.concatenate(small_grads, axis=0).T.astype(BF)
                second.append(jnp.pad(lanes, ((0, 0), (0, extra - layers * lanes_of))))
            attn_half = scatter_attn(grad_qk, jnp.concatenate(second, axis=1))
        ffn_mine[0] = scatter_shift(ffn_column, ("h", "m"), n_z, 0)
        attn_columns[0] = finish_attn(*attn_half)
        attn_columns[0], ffn_mine[0] = together(attn_columns[0], ffn_mine[0])
        wa_out, wo_out, more = own_attn(attn_columns[::-1])
        w1_out, w2_out = own_ffn(jnp.stack(ffn_mine))
        input_gradient = from_halves(grad_rows.astype(BF)).astype(F32)

        more = more[:, : layers * lanes_of].T.reshape(layers, lanes_of, rows0)
        return (
            layer_output,
            input_gradient,
            wa_out[::-1],
            more[:, :2],
            wo_out[::-1],
            more[:, 2],
            more[:, 3:5],
            more[:, 5:7],
            w1_out,
            more[:, 8:].reshape(layers, units),
            w2_out,
            more[:, 7],
        )

    return body


def solution(mesh):
    n_f, n_s = mesh.shape["fsdp"], mesh.shape["seq"]
    sizes = (2, n_f // 2, 2, n_s // 4, 2)
    grid = Mesh(mesh.devices.reshape(sizes), ("fa", "fb", "h", "m", "c"))
    fsdp, seq = ("fa", "fb"), ("h", "m", "c")
    both = fsdp + seq
    tokens = P(fsdp, seq, None)
    third, second = P(None, None, both), P(None, both)
    weights = (
        P(None, None, both, None),
        third,
        P(None, both, None),
        second,
        third,
        third,
        P(None, both, None),
        second,
        P(None, both, None),
        second,
    )
    return jax.shard_map(
        make_body(*sizes[:4]),
        mesh=grid,
        in_specs=(tokens, P(fsdp, seq), tokens) + weights,
        out_specs=(tokens, tokens) + weights,
        check_vma=False,
    )
```

time: 928 us -> 742 us (0.80)
  Pallas kernels: 0 us -> 127 us
  matrix products: 138 us -> 35.1 us
  waiting for transfers between devices: 366 us -> 266 us
  other arithmetic: 133 us -> 71.6 us
  local copies, waits for them, and re-layouts: 133 us -> 93.8 us
    ppermute x45 -> x37, waiting for transfers between devices: 326 us -> 157 us  [the longest x14 55.8 us: scatter_shift(): lax.ppermute(piece(step), axis, shift_perm(count, step))]
    pallas_call x0 -> x8, Pallas kernels: none -> 127 us  [the longest x2 44.6 us: ffn_backward(): pl.pallas_call(ffn_backward_kernel, grid=(2 * WIDE // tile,), in_specs=[h...]
    dot_general x12 -> x0, matrix products: 64.6 us -> none  [the longest x2 30.8 us: attend_backward(): jnp.einsum('qhd,khd->hqk', grad_heads, value_heads, preferred_element_typ...]
    ppermute x45 -> x37, starting transfers between devices: 108 us -> 61.4 us  [the longest x14 26.3 us: scatter_shift(): lax.ppermute(piece(step), axis, shift_perm(count, step))]
    all_to_all x0 -> x7, starting transfers between devices: none -> 38 us  [the longest x1 12.6 us: own_attn(): pieces = lax.all_to_all(column, ('h', 'm', 'c'), 0, 0, tiled=True)]
    convert_element_type x12 -> x11, other arithmetic: 47.2 us -> 12.5 us  [the longest x4 4.06 us: team_sum(): part.astype(BF)]
    ppermute x2, waiting for transfers between devices: 14.7 us -> 45.5 us  [from_halves(): got = lax.ppermute(give, 'h', [(0, 1), (1, 0)])]
    unnamed x365 -> x165, local copies, waits for them, and re-layouts: 39.7 us -> 10.6 us
  transfers between devices with their start and end apart: 83 -> 82, of which waited for: 40 -> 37; matrix products, arithmetic and copies ran while one was open for 36% -> 22% of each run, Pallas kernels for 0% -> 13%
where the time goes in v2:
time: 742 us; the launch traced here: 736 us
  waiting for transfers between devices  266 us (36%)
  Pallas kernels  127 us (17%)
  starting transfers between devices  126 us (17%)
  local copies, waits for them, and re-layouts  93.8 us (13%)
  other arithmetic  71.6 us (10%)
  matrix products  35.1 us (5%)
  between operations  16.4 us (2%)
    ppermute x14, waiting for transfers between devices, scatter_shift(): lax.ppermute(piece(step), axis, shift_perm(count, step))  55.8 us
    ppermute x5, waiting for transfers between devices, team_rows(): lax.ppermute(value, 'm', shift_perm(n_m, step))  46.8 us
    ppermute x2, waiting for transfers between devices, from_halves(): got = lax.ppermute(give, 'h', [(0, 1), (1, 0)])  45.5 us
    pallas_call x2, Pallas kernels, ffn_backward(): pl.pallas_call(ffn_backward_kernel, grid=(2 * WIDE // tile,), in_specs=[h...  44.6 us
    pallas_call x2, Pallas kernels, attend_backward(): pl.pallas_call(attend_backward_kernel, grid=(pairs,), in_specs=pair_specs...  37.2 us
    ppermute x14, waiting for transfers between devices, gather_shift(): lax.ppermute(value, axis, shift_perm(count, step))  34 us
    ppermute x14, starting transfers between devices, scatter_shift(): lax.ppermute(piece(step), axis, shift_perm(count, step))  26.3 us
    pallas_call x2, Pallas kernels, attend_forward(): pl.pallas_call(attend_forward_kernel, grid=(pairs,), in_specs=pair_specs(...  24.2 us
  transfers between devices with their start and end apart: 82, of which 37 were waited for; matrix products, arithmetic and copies ran while one was open for 22% of the time, Pallas kernels for 13%

profile of v2, /device:TPU:0, one launch (start us, length us, event | category | flops | bytes accessed | tf_op | source)
XLA Modules:
  0.0 735.9 jit_solution(2247927424291111424)
XLA Ops:
  30.4 18.4 %collective-permute-done.2 = bf16[256,1024]{1,0:T(8,128)(2,1)} collective-permute-done((bf16[256,1024]{1,0:T(8,128)(2,1)S(1)}, bf16[256,1024]{1,0:T(8,128)(2,1)}, u32[]{:S(2)}, u32[]{:S(2)}) %collective-permute-start.2) | collective-permute-done | bytes 524320 | tf_op jit(solution)/shard_map/ppermute | solution.py:398
  78.3 14.0 %collective-permute-done.10 = bf16[256,1024]{1,0:T(8,128)(2,1)S(1)} collective-permute-done((bf16[256,1024]{1,0:T(8,128)(2,1)S(1)}, bf16[256,1024]{1,0:T(8,128)(2,1)S(1)}, u32[]{:S(2)}, u32[]{:S(2)}) %collective-permute-start.10) | collective-permute-done | bytes 524320 | tf_op jit(solution)/shard_map/ppermute | solution.py:341
  97.8 5.2 fusion.123
  110.8 9.3 %collective-permute-start.13 = (s32[128]{0:T(128)S(1)}, s32[128]{0:T(128)S(1)}, u32[]{:S(2)}, u32[]{:S(2)}) collective-permute-start(s32[128]{0:T(128)S(1)} %fusion.102), channel_id=1, source_target_pairs={{0,4},{4,0},{1,5},{5,1},{2,6},{6,2},{3,7},{7,3},{8,12},{12,8},{9,1... | collective-permute-start | bytes 1544 | tf_op jit(solution)/shard_map/ppermute | solution.py:454
  123.6 5.4 all-to-all-start.1
  131.5 6.4 collective-permute-done.15
  151.7 12.1 %shard_map.220 = (bf16[1024,256]{1,0:T(8,128)(2,1)}, f32[16,1024]{1,0:T(8,128)}) custom-call(bf16[1024,512]{1,0:T(8,128)(2,1)} %pad_maximum_fusion.5.q_ref.k_ref, bf16[1024,512]{1,0:T(8,128)(2,1)} %pad_maximum_fusion.5.q_ref.k_ref, bf16[1024,256]{1,0:T(8,128)(2,1)} %pad_maximum_fusion.17.v_ref, s32[1024,1]{1,0:T(8,128)} %copy.186.col_ref, s32[1,1024]{1,0:T(1,128)} %bitcast.396), custom_call_target="tpu_custom_call" | custom-call | flops 4294967296 | bytes 2621440 | tf_op jit(solution)/shard_map/pallas_call | solution.py:82
  175.9 5.3 collective-permute-done.26
  183.1 19.2 %all-to-all-done.2 = bf16[8,32,1024]{2,1,0:T(8,128)(2,1)S(1)} async-done(((bf16[8,32,1024]{2,1,0:T(8,128)(2,1)}), bf16[8,32,1024]{2,1,0:T(8,128)(2,1)S(1)}, u32[]{:S(2)}, u32[]{:S(2)}) %all-to-all-start.2) | async-done | bytes 524320 | tf_op jit(solution)/shard_map/all_to_all | solution.py:493
  216.6 10.6 %collective-permute-done.24 = bf16[2,256,512]{2,1,0:T(8,128)(2,1)S(1)} collective-permute-done((bf16[2,256,512]{2,1,0:T(8,128)(2,1)S(1)}, bf16[2,256,512]{2,1,0:T(8,128)(2,1)S(1)}, u32[]{:S(2)}, u32[]{:S(2)}) %collective-permute-start.24) | collective-permute-done | bytes 524320 | tf_op jit(solution)/shard_map/ppermute | solution.py:341
  245.6 10.4 %shard_map.221 = (f32[256,1024]{1,0:T(8,128)}, bf16[256,1024]{1,0:T(8,128)(2,1)}, f32[512,2048]{1,0:T(8,128)}) custom-call(bf16[256,1024]{1,0:T(8,128)(2,1)} %copy-done.39, bf16[256,1024]{1,0:T(8,128)(2,1)} %collective-permute-done.20.x1_ref, bf16[16,256,1024]{2,1,0:T(8,128)(2,1)} %all-gather.3.cloned.1.call-done.w1_ref.w2_ref, ...), custom_call_target="tpu_custom_call" | custom-call | flops 4294967296 | bytes 25165824 | tf_op jit(solution)/shard_map/pallas_call | solution.py:216
  262.9 11.5 %collective-permute-done.30 = bf16[256,1024]{1,0:T(8,128)(2,1)S(1)} collective-permute-done((bf16[256,1024]{1,0:T(8,128)(2,1)S(1)}, bf16[256,1024]{1,0:T(8,128)(2,1)S(1)}, u32[]{:S(2)}, u32[]{:S(2)}) %collective-permute-start.30) | collective-permute-done | bytes 524320 | tf_op jit(solution)/shard_map/ppermute | solution.py:398
  279.3 12.1 %shard_map.222 = (bf16[1024,256]{1,0:T(8,128)(2,1)}, f32[16,1024]{1,0:T(8,128)}) custom-call(bf16[1024,512]{1,0:T(8,128)(2,1)} %pad_maximum_fusion.7.q_ref.k_ref, bf16[1024,512]{1,0:T(8,128)(2,1)} %pad_maximum_fusion.7.q_ref.k_ref, bf16[1024,256]{1,0:T(8,128)(2,1)} %pad_maximum_fusion.19.v_ref, s32[1024,1]{1,0:T(8,128)} %copy.186.col_ref, s32[1,1024]{1,0:T(1,128)} %bitcast.397), custom_call_target="tpu_custom_call" | custom-call | flops 4294967296 | bytes 2621440 | tf_op jit(solution)/shard_map/pallas_call | solution.py:82
  295.8 13.4 %collective-permute-done.33 = bf16[256,1024]{1,0:T(8,128)(2,1)S(1)} collective-permute-done((bf16[256,1024]{1,0:T(8,128)(2,1)S(1)}, bf16[256,1024]{1,0:T(8,128)(2,1)S(1)}, u32[]{:S(2)}, u32[]{:S(2)}) %collective-permute-start.33) | collective-permute-done | bytes 524320 | tf_op jit(solution)/shard_map/ppermute | solution.py:409
  313.3 16.9 %all-gather.5.cloned.1.call-done.w1_ref.w2_ref = bf16[16,256,1024]{2,1,0:T(8,128)(2,1)} async-done(((bf16[4,256,1024]{2,1,0:T(8,128)(2,1)}), bf16[16,256,1024]{2,1,0:T(8,128)(2,1)}) %all-gather.5.cloned.1.call-update) | async-done | bytes 8388624 | tf_op jit(solution)/shard_map/all_gather | solution.py:519
  330.3 10.1 %shard_map.223 = (f32[256,1024]{1,0:T(8,128)}, bf16[256,1024]{1,0:T(8,128)(2,1)}, f32[512,2048]{1,0:T(8,128)}) custom-call(bf16[256,1024]{1,0:T(8,128)(2,1)} %fusion.49.x0_ref, bf16[256,1024]{1,0:T(8,128)(2,1)} %collective-permute-done.35.x1_ref, bf16[16,256,1024]{2,1,0:T(8,128)(2,1)} %all-gather.5.cloned.1.call-done.w1_ref.w2_ref, ...), custom_call_target="tpu_custom_call" | custom-call | flops 4294967296 | bytes 25165824 | tf_op jit(solution)/shard_map/pallas_call | solution.py:216
  343.0 12.8 %collective-permute-done.37 = bf16[128,1024]{1,0:T(8,128)(2,1)S(1)} collective-permute-done((bf16[128,1024]{1,0:T(8,128)(2,1)S(1)}, bf16[128,1024]{1,0:T(8,128)(2,1)S(1)}, u32[]{:S(2)}, u32[]{:S(2)}) %collective-permute-start.37) | collective-permute-done | bytes 262176 | tf_op jit(solution)/shard_map/ppermute | solution.py:454
  361.3 22.4 %shard_map.224 = (f32[256,1024]{1,0:T(8,128)}, bf16[256,1024]{1,0:T(8,128)(2,1)}, f32[1,2048]{1,0:T(1,128)}, bf16[16,256,1024]{2,1,0:T(8,128)(2,1)}) custom-call(bf16[256,1024]{1,0:T(8,128)(2,1)} %copy-done.59, bf16[256,1024]{1,0:T(8,128)(2,1)} %copy-done.77, bf16[256,1024]{1,0:T(8,128)(2,1)} %fusion.49.x0_ref, ...), custom_call_target="tpu_custom_call" | custom-call | flops 8589934592 | bytes 27262976 | tf_op jit(solution)/shard_map/pallas_call | solution.py:297
  394.1 13.9 %collective-permute-done.43 = bf16[128,1024]{1,0:T(8,128)(2,1)S(1)} collective-permute-done((bf16[128,1024]{1,0:T(8,128)(2,1)S(1)}, bf16[128,1024]{1,0:T(8,128)(2,1)S(1)}, u32[]{:S(2)}, u32[]{:S(2)}) %collective-permute-start.43) | collective-permute-done | bytes 262176 | tf_op jit(solution)/shard_map/ppermute | solution.py:463
  414.1 4.3 all-to-all-start.4
  421.0 18.7 %shard_map.225 = (bf16[1024,512]{1,0:T(8,128)(2,1)}, bf16[1024,256]{1,0:T(8,128)(2,1)}) custom-call(bf16[1024,512]{1,0:T(8,128)(2,1)} %pad_maximum_fusion.7.q_ref.k_ref, bf16[1024,512]{1,0:T(8,128)(2,1)} %pad_maximum_fusion.7.q_ref.k_ref, bf16[1024,256]{1,0:T(8,128)(2,1)} %pad_maximum_fusion.19.v_ref, bf16[1024,256]{1,0:T(8,128)(2,1)} %pad_maximum_fusion.21.g_ref, ...), custom_call_target="tpu_custom_call" | custom-call | flops 10737418240 | bytes 4718592 | tf_op jit(solution)/shard_map/pallas_call | solution.py:139
  460.5 7.4 %collective-permute-done.45 = bf16[256,1024]{1,0:T(8,128)(2,1)} collective-permute-done((bf16[256,1024]{1,0:T(8,128)(2,1)}, bf16[256,1024]{1,0:T(8,128)(2,1)}, u32[]{:S(2)}, u32[]{:S(2)}) %collective-permute-start.45) | collective-permute-done | bytes 524320 | tf_op jit(solution)/shard_map/ppermute | solution.py:409
  471.5 8.5 %collective-permute-done.48 = bf16[2,256,512]{2,1,0:T(8,128)(2,1)} collective-permute-done((bf16[2,256,512]{2,1,0:T(8,128)(2,1)}, bf16[2,256,512]{2,1,0:T(8,128)(2,1)}, u32[]{:S(2)}, u32[]{:S(2)}) %collective-permute-start.48) | collective-permute-done | bytes 524320 | tf_op jit(solution)/shard_map/ppermute | solution.py:352
  484.7 22.2 %shard_map.226 = (f32[256,1024]{1,0:T(8,128)}, bf16[256,1024]{1,0:T(8,128)(2,1)}, f32[1,2048]{1,0:T(1,128)}, bf16[16,256,1024]{2,1,0:T(8,128)(2,1)}) custom-call(bf16[256,1024]{1,0:T(8,128)(2,1)} %copy-done.58, bf16[256,1024]{1,0:T(8,128)(2,1)} %copy-done.76, bf16[256,1024]{1,0:T(8,128)(2,1)} %copy-done.39, ...), custom_call_target="tpu_custom_call" | custom-call | flops 8589934592 | bytes 27262976 | tf_op jit(solution)/shard_map/pallas_call | solution.py:297
  522.0 9.4 %collective-permute-done.52 = bf16[256,1024]{1,0:T(8,128)(2,1)S(1)} collective-permute-done((bf16[256,1024]{1,0:T(8,128)(2,1)S(1)}, bf16[256,1024]{1,0:T(8,128)(2,1)S(1)}, u32[]{:S(2)}, u32[]{:S(2)}) %collective-permute-start.52) | collective-permute-done | bytes 524320 | tf_op jit(solution)/shard_map/ppermute | solution.py:398
  551.7 18.5 %shard_map.227 = (bf16[1024,512]{1,0:T(8,128)(2,1)}, bf16[1024,256]{1,0:T(8,128)(2,1)}) custom-call(bf16[1024,512]{1,0:T(8,128)(2,1)} %pad_maximum_fusion.5.q_ref.k_ref, bf16[1024,512]{1,0:T(8,128)(2,1)} %pad_maximum_fusion.5.q_ref.k_ref, bf16[1024,256]{1,0:T(8,128)(2,1)} %pad_maximum_fusion.17.v_ref, bf16[1024,256]{1,0:T(8,128)(2,1)} %pad_maximum_fusion.22.g_ref, ...), custom_call_target="tpu_custom_call" | custom-call | flops 10737418240 | bytes 4718592 | tf_op jit(solution)/shard_map/pallas_call | solution.py:139
  596.9 10.5 %collective-permute-done.63 = bf16[2,256,512]{2,1,0:T(8,128)(2,1)} collective-permute-done((bf16[2,256,512]{2,1,0:T(8,128)(2,1)}, bf16[2,256,512]{2,1,0:T(8,128)(2,1)}, u32[]{:S(2)}, u32[]{:S(2)}) %collective-permute-start.63) | collective-permute-done | bytes 524320 | tf_op jit(solution)/shard_map/ppermute | solution.py:352
  615.3 9.8 %collective-permute-start.67 = (bf16[256,1024]{1,0:T(8,128)(2,1)S(1)}, bf16[256,1024]{1,0:T(8,128)(2,1)S(1)}, u32[]{:S(2)}, u32[]{:S(2)}) collective-permute-start(bf16[256,1024]{1,0:T(8,128)(2,1)S(1)} %get-tuple-element.235), channel_id=1, source_target_pairs={{0,2},{2,4},{4,6},{6,0},{1,3},{3,5},{5,7},{7,1},{8,10},{10,12},{12... | collective-permute-start | bytes 1572872 | tf_op jit(solution)/shard_map/ppermute | solution.py:352
  630.4 9.1 %collective-permute-done.67 = bf16[256,1024]{1,0:T(8,128)(2,1)S(1)} collective-permute-done((bf16[256,1024]{1,0:T(8,128)(2,1)S(1)}, bf16[256,1024]{1,0:T(8,128)(2,1)S(1)}, u32[]{:S(2)}, u32[]{:S(2)}) %collective-permute-start.67) | collective-permute-done | bytes 524320 | tf_op jit(solution)/shard_map/ppermute | solution.py:352
  639.5 19.7 %collective-permute-done.68 = bf16[256,1024]{1,0:T(8,128)(2,1)S(1)} collective-permute-done((bf16[256,1024]{1,0:T(8,128)(2,1)S(1)}, bf16[256,1024]{1,0:T(8,128)(2,1)S(1)}, u32[]{:S(2)}, u32[]{:S(2)}) %collective-permute-start.68) | collective-permute-done | bytes 524320 | tf_op jit(solution)/shard_map/ppermute | solution.py:352
  663.5 12.6 %all-to-all-start.6 = ((bf16[8,32,2176]{2,1,0:T(8,128)(2,1)}), bf16[8,32,2176]{2,1,0:T(8,128)(2,1)S(1)}, u32[]{:S(2)}, u32[]{:S(2)}) async-start(bf16[8,32,2176]{2,1,0:T(8,128)(2,1)} %pad_maximum_fusion.1), calls=%async_computation.8 | async-start | bytes 2228224 | tf_op jit(solution)/shard_map/all_to_all | solution.py:608
  683.6 31.7 %collective-permute-done.62 = bf16[128,1024]{1,0:T(8,128)(2,1)S(1)} collective-permute-done((bf16[128,1024]{1,0:T(8,128)(2,1)S(1)}, bf16[128,1024]{1,0:T(8,128)(2,1)S(1)}, u32[]{:S(2)}, u32[]{:S(2)}) %collective-permute-start.62) | collective-permute-done | bytes 262176 | tf_op jit(solution)/shard_map/ppermute | solution.py:463
  (646 shorter events, 307.7 us)
Async XLA Ops:
  21.3 32.4 %all-to-all-start = ((bf16[8,32,1152]{2,1,0:T(8,128)(2,1)}), bf16[8,32,1152]{2,1,0:T(8,128)(2,1)S(1)}, u32[]{:S(2)}, u32[]{:S(2)}) async-start(bf16[8,32,1152]{2,1,0:T(8,128)(2,1)} %bitcast.10), calls=%async_computation | async-start | bytes 1179648 | tf_op jit(solution)/shard_map/all_to_all | solution.py:493
  24.8 220.8 %all-gather.3.cloned.1.call-start = ((), (), s32[]{:S(2)}) async-start(), calls=%async_computation.9 | async-start | bytes 10485760 | tf_op jit(solution)/shard_map/all_gather | solution.py:519
  25.1 23.7 %collective-permute-start.2 = (bf16[256,1024]{1,0:T(8,128)(2,1)S(1)}, bf16[256,1024]{1,0:T(8,128)(2,1)}, u32[]{:S(2)}, u32[]{:S(2)}) collective-permute-start(bf16[256,1024]{1,0:T(8,128)(2,1)S(1)} %pad_maximum_fusion.15), channel_id=1, source_target_pairs={{0,2},{2,0},{1,3},{3,1},{4,6},{6,4},{5,7},{7,5},{8,10},{10,8},{9,1... | collective-permute-start | bytes 1572872 | tf_op jit(solution)/shard_map/ppermute | solution.py:398
  53.7 23.7 %collective-permute-start.9 = (bf16[256,1024]{1,0:T(8,128)(2,1)S(1)}, bf16[256,1024]{1,0:T(8,128)(2,1)S(1)}, u32[]{:S(2)}, u32[]{:S(2)}) collective-permute-start(bf16[256,1024]{1,0:T(8,128)(2,1)S(1)} %copy-done.46), channel_id=1, source_target_pairs={{0,2},{2,4},{4,6},{6,0},{1,3},{3,5},{5,7},{7,1},{8,10},{10,12},{12... | collective-permute-start | bytes 1572872 | tf_op jit(solution)/shard_map/ppermute | solution.py:341
  54.2 38.2 %collective-permute-start.10 = (bf16[256,1024]{1,0:T(8,128)(2,1)S(1)}, bf16[256,1024]{1,0:T(8,128)(2,1)S(1)}, u32[]{:S(2)}, u32[]{:S(2)}) collective-permute-start(bf16[256,1024]{1,0:T(8,128)(2,1)S(1)} %copy-done.46), channel_id=1, source_target_pairs={{0,4},{2,6},{4,0},{6,2},{1,5},{3,7},{5,1},{7,3},{8,12},{10,14},{12... | collective-permute-start | bytes 1572872 | tf_op jit(solution)/shard_map/ppermute | solution.py:341
  56.7 36.5 %collective-permute-start.11 = (bf16[256,1024]{1,0:T(8,128)(2,1)S(1)}, bf16[256,1024]{1,0:T(8,128)(2,1)S(1)}, u32[]{:S(2)}, u32[]{:S(2)}) collective-permute-start(bf16[256,1024]{1,0:T(8,128)(2,1)S(1)} %copy-done.46), channel_id=1, source_target_pairs={{0,6},{2,0},{4,2},{6,4},{1,7},{3,1},{5,3},{7,5},{8,14},{10,8},{12,... | collective-permute-start | bytes 1572872 | tf_op jit(solution)/shard_map/ppermute | solution.py:341
  69.3 24.8 %collective-permute-start.8 = (bf16[2,256,512]{2,1,0:T(8,128)(2,1)}, bf16[2,256,512]{2,1,0:T(8,128)(2,1)S(1)}, u32[]{:S(2)}, u32[]{:S(2)}) collective-permute-start(bf16[2,256,512]{2,1,0:T(8,128)(2,1)} %bitcast_dynamic-update-slice_fusion.22), channel_id=1, source_target_pairs={{0,16},{16,0},{1,17},{17,1},{2,18},{18,2},{3,19},{19,3},{4,20},{20... | collective-permute-start | bytes 1572872 | tf_op jit(solution)/shard_map/ppermute | solution.py:341
  110.7 29.4 %collective-permute-start.12 = (bf16[2,32,1024]{2,0,1:T(2,128)(2,1)S(1)}, bf16[2,32,1024]{2,0,1:T(2,128)(2,1)S(1)}, u32[]{:S(2)}, u32[]{:S(2)}) collective-permute-start(bf16[2,32,1024]{2,0,1:T(2,128)(2,1)S(1)} %bitcast.393), channel_id=1, source_target_pairs={{0,1},{1,0},{2,3},{3,2},{4,5},{5,4},{6,7},{7,6},{8,9},{9,8},{10,11... | collective-permute-start | bytes 393224 | tf_op jit(solution)/shard_map/ppermute | solution.py:334
  141.9 32.1 %collective-permute-start.25 = (bf16[256,1024]{1,0:T(8,128)(2,1)S(1)}, bf16[256,1024]{1,0:T(8,128)(2,1)}, u32[]{:S(2)}, u32[]{:S(2)}) collective-permute-start(bf16[256,1024]{1,0:T(8,128)(2,1)S(1)} %pad_maximum_fusion.18), channel_id=1, source_target_pairs={{0,2},{2,4},{4,6},{6,0},{1,3},{3,5},{5,7},{7,1},{8,10},{10,12},{12... | collective-permute-start | bytes 1572872 | tf_op jit(solution)/shard_map/ppermute | solution.py:341
  142.3 38.9 %collective-permute-start.26 = (bf16[256,1024]{1,0:T(8,128)(2,1)S(1)}, bf16[256,1024]{1,0:T(8,128)(2,1)}, u32[]{:S(2)}, u32[]{:S(2)}) collective-permute-start(bf16[256,1024]{1,0:T(8,128)(2,1)S(1)} %pad_maximum_fusion.18), channel_id=1, source_target_pairs={{0,4},{2,6},{4,0},{6,2},{1,5},{3,7},{5,1},{7,3},{8,12},{10,14},{12... | collective-permute-start | bytes 1572872 | tf_op jit(solution)/shard_map/ppermute | solution.py:341
  145.2 87.9 %collective-permute-start.27 = (bf16[256,1024]{1,0:T(8,128)(2,1)S(1)}, bf16[256,1024]{1,0:T(8,128)(2,1)}, u32[]{:S(2)}, u32[]{:S(2)}) collective-permute-start(bf16[256,1024]{1,0:T(8,128)(2,1)S(1)} %pad_maximum_fusion.18), channel_id=1, source_target_pairs={{0,6},{2,0},{4,2},{6,4},{1,7},{3,1},{5,3},{7,5},{8,14},{10,8},{12,... | collective-permute-start | bytes 1572872 | tf_op jit(solution)/shard_map/ppermute | solution.py:341
  147.8 54.5 %all-to-all-start.2 = ((bf16[8,32,1024]{2,1,0:T(8,128)(2,1)}), bf16[8,32,1024]{2,1,0:T(8,128)(2,1)S(1)}, u32[]{:S(2)}, u32[]{:S(2)}) async-start(bf16[8,32,1024]{2,1,0:T(8,128)(2,1)} %bitcast.37), calls=%async_computation.2 | async-start | bytes 1048576 | tf_op jit(solution)/shard_map/all_to_all | solution.py:493
  168.6 38.4 %collective-permute-start.19 = (bf16[256,1024]{1,0:T(8,128)(2,1)}, bf16[256,1024]{1,0:T(8,128)(2,1)S(1)}, u32[]{:S(2)}, u32[]{:S(2)}) collective-permute-start(bf16[256,1024]{1,0:T(8,128)(2,1)} %slice.866), channel_id=1, source_target_pairs={{0,1},{1,0},{2,3},{3,2},{4,5},{5,4},{6,7},{7,6},{8,9},{9,8},{10,11... | collective-permute-start | bytes 1572872 | tf_op jit(solution)/shard_map/ppermute | solution.py:334
  172.0 35.0 %collective-permute-start.18 = (bf16[256,1024]{1,0:T(8,128)(2,1)}, bf16[256,1024]{1,0:T(8,128)(2,1)}, u32[]{:S(2)}, u32[]{:S(2)}) collective-permute-start(bf16[256,1024]{1,0:T(8,128)(2,1)} %fusion.39), channel_id=1, source_target_pairs={{0,2},{2,0},{1,3},{3,1},{4,6},{6,4},{5,7},{7,5},{8,10},{10,8},{9,1... | collective-permute-start | bytes 1572872 | tf_op jit(solution)/shard_map/ppermute | solution.py:409
  232.4 97.9 %all-gather.5.cloned.1.call-start = ((), (), s32[]{:S(2)}) async-start(), calls=%async_computation.10 | async-start | bytes 10485760 | tf_op jit(solution)/shard_map/all_gather | solution.py:519
  243.3 292.6 %reduce-scatter.3.cloned.1.call-start = ((), (), s32[]{:S(2)}) async-start(), calls=%async_computation.11 | async-start | bytes 10485760 | tf_op jit(solution)/shard_map/reduce_scatter | solution.py:638
  414.1 44.6 %all-to-all-start.4 = ((bf16[4,256,256]{2,1,0:T(8,128)(2,1)}), bf16[4,256,256]{2,1,0:T(8,128)(2,1)}, u32[]{:S(2)}, u32[]{:S(2)}) async-start(bf16[4,256,256]{2,1,0:T(8,128)(2,1)} %bitcast.328), calls=%async_computation.4 | async-start | bytes 1048576 | tf_op jit(solution)/shard_map/all_to_all | solution.py:655
  418.4 195.4 %reduce-scatter.5.cloned.1.call-start = ((), (), s32[]{:S(2)}) async-start(), calls=%async_computation.12 | async-start | bytes 10485760 | tf_op jit(solution)/shard_map/reduce_scatter | solution.py:638
  457.2 22.8 %collective-permute-start.48 = (bf16[2,256,512]{2,1,0:T(8,128)(2,1)}, bf16[2,256,512]{2,1,0:T(8,128)(2,1)}, u32[]{:S(2)}, u32[]{:S(2)}) collective-permute-start(bf16[2,256,512]{2,1,0:T(8,128)(2,1)} %dynamic-slice_bitcast_fusion.8), channel_id=1, source_target_pairs={{0,16},{16,0},{1,17},{17,1},{2,18},{18,2},{3,19},{19,3},{4,20},{20... | collective-permute-start | bytes 1572872 | tf_op jit(solution)/shard_map/ppermute | solution.py:352
  538.7 34.5 %collective-permute-start.54 = (bf16[256,1024]{1,0:T(8,128)(2,1)}, bf16[256,1024]{1,0:T(8,128)(2,1)}, u32[]{:S(2)}, u32[]{:S(2)}) collective-permute-start(bf16[256,1024]{1,0:T(8,128)(2,1)} %get-tuple-element.238), channel_id=1, source_target_pairs={{0,2},{2,4},{4,6},{6,0},{1,3},{3,5},{5,7},{7,1},{8,10},{10,12},{12... | collective-permute-start | bytes 1572872 | tf_op jit(solution)/shard_map/ppermute | solution.py:352
  539.1 37.3 %collective-permute-start.55 = (bf16[256,1024]{1,0:T(8,128)(2,1)}, bf16[256,1024]{1,0:T(8,128)(2,1)}, u32[]{:S(2)}, u32[]{:S(2)}) collective-permute-start(bf16[256,1024]{1,0:T(8,128)(2,1)} %get-tuple-element.240), channel_id=1, source_target_pairs={{0,4},{2,6},{4,0},{6,2},{1,5},{3,7},{5,1},{7,3},{8,12},{10,14},{12... | collective-permute-start | bytes 1572872 | tf_op jit(solution)/shard_map/ppermute | solution.py:352
  541.5 34.9 %collective-permute-start.56 = (bf16[256,1024]{1,0:T(8,128)(2,1)}, bf16[256,1024]{1,0:T(8,128)(2,1)}, u32[]{:S(2)}, u32[]{:S(2)}) collective-permute-start(bf16[256,1024]{1,0:T(8,128)(2,1)} %get-tuple-element.239), channel_id=1, source_target_pairs={{0,6},{2,0},{4,2},{6,4},{1,7},{3,1},{5,3},{7,5},{8,14},{10,8},{12,... | collective-permute-start | bytes 1572872 | tf_op jit(solution)/shard_map/ppermute | solution.py:352
  545.8 46.1 %all-to-all-start.5 = ((bf16[4,256,256]{2,1,0:T(8,128)(2,1)}), bf16[4,256,256]{2,1,0:T(8,128)(2,1)}, u32[]{:S(2)}, u32[]{:S(2)}) async-start(bf16[4,256,256]{2,1,0:T(8,128)(2,1)} %bitcast.326), calls=%async_computation.6 | async-start | bytes 1048576 | tf_op jit(solution)/shard_map/all_to_all | solution.py:655
  581.8 25.5 %collective-permute-start.63 = (bf16[2,256,512]{2,1,0:T(8,128)(2,1)}, bf16[2,256,512]{2,1,0:T(8,128)(2,1)}, u32[]{:S(2)}, u32[]{:S(2)}) collective-permute-start(bf16[2,256,512]{2,1,0:T(8,128)(2,1)} %dynamic-slice_bitcast_fusion.4), channel_id=1, source_target_pairs={{0,16},{16,0},{1,17},{17,1},{2,18},{18,2},{3,19},{19,3},{4,20},{20... | collective-permute-start | bytes 1572872 | tf_op jit(solution)/shard_map/ppermute | solution.py:352
  596.9 79.3 %collective-permute-start.61 = (bf16[256,1024]{1,0:T(8,128)(2,1)}, bf16[256,1024]{1,0:T(8,128)(2,1)}, u32[]{:S(2)}, u32[]{:S(2)}) collective-permute-start(bf16[256,1024]{1,0:T(8,128)(2,1)} %slice.860), channel_id=1, source_target_pairs={{0,1},{1,0},{2,3},{3,2},{4,5},{5,4},{6,7},{7,6},{8,9},{9,8},{10,11... | collective-permute-start | bytes 1572872 | tf_op jit(solution)/shard_map/ppermute | solution.py:334
  615.3 24.3 %collective-permute-start.67 = (bf16[256,1024]{1,0:T(8,128)(2,1)S(1)}, bf16[256,1024]{1,0:T(8,128)(2,1)S(1)}, u32[]{:S(2)}, u32[]{:S(2)}) collective-permute-start(bf16[256,1024]{1,0:T(8,128)(2,1)S(1)} %get-tuple-element.235), channel_id=1, source_target_pairs={{0,2},{2,4},{4,6},{6,0},{1,3},{3,5},{5,7},{7,1},{8,10},{10,12},{12... | collective-permute-start | bytes 1572872 | tf_op jit(solution)/shard_map/ppermute | solution.py:352
  625.1 34.1 %collective-permute-start.68 = (bf16[256,1024]{1,0:T(8,128)(2,1)S(1)}, bf16[256,1024]{1,0:T(8,128)(2,1)S(1)}, u32[]{:S(2)}, u32[]{:S(2)}) collective-permute-start(bf16[256,1024]{1,0:T(8,128)(2,1)S(1)} %get-tuple-element.237), channel_id=1, source_target_pairs={{0,4},{2,6},{4,0},{6,2},{1,5},{3,7},{5,1},{7,3},{8,12},{10,14},{12... | collective-permute-start | bytes 1572872 | tf_op jit(solution)/shard_map/ppermute | solution.py:352
  627.2 32.9 %collective-permute-start.69 = (bf16[256,1024]{1,0:T(8,128)(2,1)S(1)}, bf16[256,1024]{1,0:T(8,128)(2,1)S(1)}, u32[]{:S(2)}, u32[]{:S(2)}) collective-permute-start(bf16[256,1024]{1,0:T(8,128)(2,1)S(1)} %get-tuple-element.236), channel_id=1, source_target_pairs={{0,6},{2,0},{4,2},{6,4},{1,7},{3,1},{5,3},{7,5},{8,14},{10,8},{12,... | collective-permute-start | bytes 1572872 | tf_op jit(solution)/shard_map/ppermute | solution.py:352
  628.4 47.7 %collective-permute-start.60 = (bf16[256,1024]{1,0:T(8,128)(2,1)}, bf16[256,1024]{1,0:T(8,128)(2,1)}, u32[]{:S(2)}, u32[]{:S(2)}) collective-permute-start(bf16[256,1024]{1,0:T(8,128)(2,1)} %fusion.30), channel_id=1, source_target_pairs={{0,2},{2,0},{1,3},{3,1},{4,6},{6,4},{5,7},{7,5},{8,10},{10,8},{9,1... | collective-permute-start | bytes 1572872 | tf_op jit(solution)/shard_map/ppermute | solution.py:409
  663.5 56.5 %all-to-all-start.6 = ((bf16[8,32,2176]{2,1,0:T(8,128)(2,1)}), bf16[8,32,2176]{2,1,0:T(8,128)(2,1)S(1)}, u32[]{:S(2)}, u32[]{:S(2)}) async-start(bf16[8,32,2176]{2,1,0:T(8,128)(2,1)} %pad_maximum_fusion.1), calls=%async_computation.8 | async-start | bytes 2228224 | tf_op jit(solution)/shard_map/all_to_all | solution.py:608
  680.3 36.4 %collective-permute-start.70 = (f32[2,2,32,1024]{3,1,2,0:T(2,128)S(1)}, f32[2,2,32,1024]{3,1,2,0:T(2,128)S(1)}, u32[]{:S(2)}, u32[]{:S(2)}) collective-permute-start(f32[2,2,32,1024]{3,1,2,0:T(2,128)S(1)} %get-tuple-element.243), channel_id=1, source_target_pairs={{0,1},{1,0},{2,3},{3,2},{4,5},{5,4},{6,7},{7,6},{8,9},{9,8},{10,11... | collective-permute-start | bytes 1572872 | tf_op jit(solution)/shard_map/ppermute | solution.py:334
  681.0 34.3 %collective-permute-start.62 = (bf16[128,1024]{1,0:T(8,128)(2,1)S(1)}, bf16[128,1024]{1,0:T(8,128)(2,1)S(1)}, u32[]{:S(2)}, u32[]{:S(2)}) collective-permute-start(bf16[128,1024]{1,0:T(8,128)(2,1)S(1)} %get-tuple-element.255), channel_id=1, source_target_pairs={{0,4},{4,0},{1,5},{5,1},{2,6},{6,2},{3,7},{7,3},{8,12},{12,8},{9,1... | collective-permute-start | bytes 786440 | tf_op jit(solution)/shard_map/ppermute | solution.py:463
  (129 other events, 1508.6 us)
Sparse Core Ops, SparseCore 0:
  110.2 101.3 all-gather.2
  243.5 86.7 all-gather.4
  383.8 94.9 reduce-scatter.2
  507.1 103.1 reduce-scatter.4

commit v3 on v2

--- a/solution.py
+++ b/solution.py
@@ -8,6 +8,9 @@
 HEAD = 64
 PAIR = 2 * HEAD
 BLOCK = 256
+SUB = 256
+FFN_TILE = 512
+FFN_BACK_TILE = 512
 WIDE = 1024
 EPSILON = 1e-05
 NEG_FILL = -1e30
@@ -30,7 +33,7 @@
 
 
 def params(*semantics):
-    return pltpu.CompilerParams(dimension_semantics=semantics, vmem_limit_bytes=VMEM_BYTES)
+    return pltpu.CompilerParams(dimension_semantics=semantics or None, vmem_limit_bytes=VMEM_BYTES)
 
 
 def one_head(value, lane, head):
@@ -165,34 +168,32 @@
     )(query_key, query_key, value, grad, docs[:, None], docs[None], logs)
 
 
-def join(ref, first, second):
-    half = first.shape[0]
-    ref[:half, :] = first[...]
-    ref[half:, :] = second[...]
-
-
 def ffn_forward_kernel(
-    x0_ref, x1_ref, w1_ref, w2_ref, b_ref, own_ref, give_ref, u_ref, x_ref, total_ref
+    x0_ref, x1_ref, w1_ref, w2_ref, b_ref, own_ref, give_ref, gt_ref, slope_ref, xt_ref, x_ref, total_ref
 ):
     step = pl.program_id(0)
     tile = b_ref.shape[1]
 
     @pl.when(step == 0)
     def _():
-        join(x_ref, x0_ref, x1_ref)
-
-    expanded = matmul(x_ref[...], w1_ref[...].reshape(WIDE, tile)) + b_ref[...]
-    u_ref[...] = expanded
-    active = (expanded * (0.5 + 0.5 * lax.erf(expanded * ROOT_HALF))).astype(BF)
-    part = matmul(active, w2_ref[...].reshape(tile, WIDE))
-
-    @pl.when(step == 0)
-    def _():
-        total_ref[...] = part
-
-    @pl.when(step > 0)
-    def _():
-        total_ref[...] += part
+        half = x0_ref.shape[0]
+        x_ref[:half, :] = x0_ref[...]
+        x_ref[half:, :] = x1_ref[...]
+        xt_ref[...] = x_ref[...].T
+        total_ref[...] = jnp.zeros_like(total_ref)
+
+    part = 0.0
+    for first in range(0, tile, SUB):
+        lanes = slice(first, first + SUB)
+        group = w2_ref.shape[0] * SUB // tile
+        chips = slice(first * w2_ref.shape[0] // tile, first * w2_ref.shape[0] // tile + group)
+        expanded = matmul(x_ref[...], w1_ref[:, :, lanes].reshape(WIDE, SUB)) + b_ref[:, lanes]
+        normal = 0.5 + 0.5 * lax.erf(expanded * ROOT_HALF)
+        slope_ref[:, lanes] = normal + expanded * (ROOT_TWO_PI * jnp.exp(-0.5 * expanded * expanded))
+        active = (expanded * normal).astype(BF)
+        gt_ref[lanes, :] = active.T
+        part = part + matmul(active, w2_ref[chips].reshape(SUB, WIDE))
+    total_ref[...] += part
 
     @pl.when(step == pl.num_programs(0) - 1)
     def _():
@@ -201,87 +202,81 @@
         give_ref[...] = total_ref[half:, :].astype(BF)
 
 
-def ffn_specs(packed, tile):
-    chips, rows = packed.shape[0], packed.shape[1]
+def ffn_specs(weights, tile):
+    chips = weights[0].shape[0]
+    rows = (2 * WIDE) // chips
     per_half = WIDE // tile
+    place = weights[1].shape[1] // rows - 1
     return [
-        pl.BlockSpec((chips, rows // 4, tile), lambda t: (0, t // per_half, t % per_half)),
-        pl.BlockSpec((tile * chips // (2 * WIDE), rows // 2, WIDE), lambda t: (t, 1, 0)),
+        pl.BlockSpec((chips, rows // 2, tile), lambda t: (0, t // per_half, t % per_half)),
+        pl.BlockSpec((tile // rows, rows, WIDE), lambda t: (t, place, 0)),
     ]
 
 
-def ffn_forward(rows_low, packed, bias):
-    tokens, tile = 2 * rows_low[0].shape[0], 512
+def ffn_forward(rows_low, weights, bias):
+    tokens, tile = 2 * rows_low[0].shape[0], FFN_TILE
     half = pl.BlockSpec((tokens // 2, WIDE), lambda t: (0, 0))
     return pl.pallas_call(
         ffn_forward_kernel,
         grid=(2 * WIDE // tile,),
         in_specs=[half, half]
-        + ffn_specs(packed, tile)
+        + ffn_specs(weights, tile)
         + [pl.BlockSpec((1, tile), lambda t: (0, t))],
         out_specs=[
-            pl.BlockSpec((tokens // 2, WIDE), lambda t: (0, 0)),
-            pl.BlockSpec((tokens // 2, WIDE), lambda t: (0, 0)),
+            half,
+            half,
+            pl.BlockSpec((tile, tokens), lambda t: (t, 0)),
             pl.BlockSpec((tokens, tile), lambda t: (0, t)),
+            pl.BlockSpec((WIDE, tokens), lambda t: (0, 0)),
         ],
         out_shape=[
             jax.ShapeDtypeStruct((tokens // 2, WIDE), F32),
             jax.ShapeDtypeStruct((tokens // 2, WIDE), BF),
+            jax.ShapeDtypeStruct((2 * WIDE, tokens), BF),
             jax.ShapeDtypeStruct((tokens, 2 * WIDE), F32),
+            jax.ShapeDtypeStruct((WIDE, tokens), BF),
         ],
         scratch_shapes=[pltpu.VMEM((tokens, WIDE), BF), pltpu.VMEM((tokens, WIDE), F32)],
         compiler_params=params("arbitrary"),
         cost_estimate=pl.CostEstimate(
             flops=8 * tokens * WIDE * WIDE,
             bytes_accessed=16 * WIDE * WIDE + 16 * tokens * WIDE,
-            transcendentals=2 * tokens * WIDE,
+            transcendentals=4 * tokens * WIDE,
         ),
-    )(*rows_low, packed, packed, bias[None])
+    )(*rows_low, *weights, bias[None])
 
 
 def ffn_backward_kernel(
     g0_ref,
     g1_ref,
-    x0_ref,
-    x1_ref,
-    u_ref,
+    xt_ref,
+    gt_ref,
+    slope_ref,
     w1_ref,
     w2_ref,
     own_ref,
     give_ref,
     db_ref,
-    dw_ref,
+    dw1_ref,
+    dw2_ref,
     g_ref,
-    xt_ref,
     total_ref,
 ):
     step = pl.program_id(0)
-    tile = u_ref.shape[1]
-    chips, rows = dw_ref.shape[0], dw_ref.shape[1]
-    quarter = rows // 4
-    per_half = WIDE // tile
-    group = tile * chips // (2 * WIDE)
+    tile = slope_ref.shape[1]
 
     @pl.when(step == 0)
     def _():
-        join(g_ref, g0_ref, g1_ref)
-        half = x0_ref.shape[0]
-        xt_ref[:, :half] = x0_ref[...].T
-        xt_ref[:, half:] = x1_ref[...].T
+        half = g0_ref.shape[0]
+        g_ref[:half, :] = g0_ref[...]
+        g_ref[half:, :] = g1_ref[...]
         total_ref[...] = jnp.zeros_like(total_ref)
 
     grad = g_ref[...]
-    expanded = u_ref[...]
-    normal = 0.5 + 0.5 * lax.erf(expanded * ROOT_HALF)
-    active = (expanded * normal).astype(BF)
-    slope = normal + expanded * (ROOT_TWO_PI * jnp.exp(-0.5 * expanded * expanded))
-    dw2 = matmul_tn(active, grad)
-    dw_ref[pl.ds(step * group, group), 2 * quarter :, :] = dw2.astype(BF).reshape(group, 2 * quarter, WIDE)
-    low = (matmul_nt(grad, w2_ref[...].reshape(tile, WIDE)) * slope).astype(BF)
+    low = (matmul_nt(grad, w2_ref[...].reshape(tile, WIDE)) * slope_ref[...]).astype(BF)
+    dw2_ref[...] = matmul(gt_ref[...], grad).astype(BF).reshape(dw2_ref.shape)
     db_ref[...] = jnp.sum(low.astype(F32), axis=0, keepdims=True)
-    dw1 = matmul(xt_ref[...], low).astype(BF).reshape(chips, quarter, tile)
-    dw_ref[:, pl.ds(pl.multiple_of((step // per_half) * quarter, quarter), quarter),
-           pl.ds(pl.multiple_of((step % per_half) * tile, tile), tile)] = dw1
+    dw1_ref[...] = matmul(xt_ref[...], low).astype(BF).reshape(dw1_ref.shape)
     total_ref[...] += matmul_nt(low, w1_ref[...].reshape(WIDE, tile))
 
     @pl.when(step == pl.num_programs(0) - 1)
@@ -291,39 +286,132 @@
         give_ref[...] = total_ref[half:, :].astype(BF)
 
 
-def ffn_backward(grad_low, rows_low, expanded, packed):
-    tokens, tile = 2 * rows_low[0].shape[0], 256
+def ffn_backward(grad_low, saved, weights):
+    tokens, tile = 2 * grad_low[0].shape[0], FFN_BACK_TILE
     half = pl.BlockSpec((tokens // 2, WIDE), lambda t: (0, 0))
+    active_t, slope, rows_t = saved
+    chips = weights[0].shape[0]
+    matrix = (chips, 2 * WIDE // chips, WIDE)
     return pl.pallas_call(
         ffn_backward_kernel,
         grid=(2 * WIDE // tile,),
-        in_specs=[half] * 4
-        + [pl.BlockSpec((tokens, tile), lambda t: (0, t))]
-        + ffn_specs(packed, tile),
+        in_specs=[
+            half,
+            half,
+            pl.BlockSpec((WIDE, tokens), lambda t: (0, 0)),
+            pl.BlockSpec((tile, tokens), lambda t: (t, 0)),
+            pl.BlockSpec((tokens, tile), lambda t: (0, t)),
+        ]
+        + ffn_specs(weights, tile),
         out_specs=[
-            pl.BlockSpec((tokens // 2, WIDE), lambda t: (0, 0)),
-            pl.BlockSpec((tokens // 2, WIDE), lambda t: (0, 0)),
+            half,
+            half,
             pl.BlockSpec((1, tile), lambda t: (0, t)),
-            pl.BlockSpec(packed.shape, lambda t: (0, 0, 0)),
-        ],
+        ]
+        + ffn_specs((jax.ShapeDtypeStruct(matrix, BF),) * 2, tile),
         out_shape=[
             jax.ShapeDtypeStruct((tokens // 2, WIDE), F32),
             jax.ShapeDtypeStruct((tokens // 2, WIDE), BF),
             jax.ShapeDtypeStruct((1, 2 * WIDE), F32),
-            jax.ShapeDtypeStruct(packed.shape, BF),
-        ],
-        scratch_shapes=[
-            pltpu.VMEM((tokens, WIDE), BF),
-            pltpu.VMEM((WIDE, tokens), BF),
-            pltpu.VMEM((tokens, WIDE), F32),
-        ],
+            jax.ShapeDtypeStruct(matrix, BF),
+            jax.ShapeDtypeStruct(matrix, BF),
+        ],
+        scratch_shapes=[pltpu.VMEM((tokens, WIDE), BF), pltpu.VMEM((tokens, WIDE), F32)],
         compiler_params=params("arbitrary"),
         cost_estimate=pl.CostEstimate(
             flops=16 * tokens * WIDE * WIDE,
-            bytes_accessed=16 * WIDE * WIDE + 20 * tokens * WIDE,
-            transcendentals=4 * tokens * WIDE,
+            bytes_accessed=32 * WIDE * WIDE + 20 * tokens * WIDE,
+            transcendentals=0,
         ),
-    )(*grad_low, *rows_low, expanded, packed, packed)
+    )(*grad_low, rows_t, active_t, slope, *weights)
+
+
+def project_forward_kernel(*refs):
+    *x_refs, qk_ref, v_ref, bqk_ref, scale_ref, bv_ref, qk_out, v_out = refs
+    for index, x_ref in enumerate(x_refs):
+        rows = x_ref[...]
+        at = slice(index * rows.shape[0], (index + 1) * rows.shape[0])
+        qk_out[at, :] = ((matmul(rows, qk_ref[...]) + bqk_ref[...]) * scale_ref[...]).astype(BF)
+        v_out[at, :] = (matmul(rows, v_ref[...]) + bv_ref[...]).astype(BF)
+
+
+def project_forward(pieces, qk_w, v_w, bias_qk, scale, bias_v):
+    tokens, width = len(pieces) * pieces[0].shape[0], v_w.shape[1]
+    return pl.pallas_call(
+        project_forward_kernel,
+        out_shape=[
+            jax.ShapeDtypeStruct((tokens, 2 * width), BF),
+            jax.ShapeDtypeStruct((tokens, width), BF),
+        ],
+        compiler_params=params(),
+        cost_estimate=pl.CostEstimate(
+            flops=6 * tokens * WIDE * width,
+            bytes_accessed=2 * tokens * (WIDE + 3 * width) + 6 * WIDE * width,
+            transcendentals=0,
+        ),
+    )(*pieces, qk_w, v_w, bias_qk[None], scale[None], bias_v[None])
+
+
+def project_backward_kernel(*refs):
+    *x_refs, dqk_ref, dv_ref, qk_ref, v_ref, gqk_ref, gv_ref, own_ref, give_ref, xt_ref = refs
+    rows = x_refs[0].shape[0]
+    for index, x_ref in enumerate(x_refs):
+        at = slice(index * rows, (index + 1) * rows)
+        xt_ref[:, at] = x_ref[...].T
+        found = matmul_nt(dqk_ref[at, :], qk_ref[...]) + matmul_nt(dv_ref[at, :], v_ref[...])
+        if index % 2 == 0:
+            own_ref[index // 2] = found
+        else:
+            give_ref[index // 2] = found.astype(BF)
+    gqk_ref[...] = matmul(xt_ref[...], dqk_ref[...]).astype(BF)
+    gv_ref[...] = matmul(xt_ref[...], dv_ref[...]).astype(BF)
+
+
+def project_backward(pieces, dqk, dv, qk_w, v_w):
+    count, rows, width = len(pieces), pieces[0].shape[0], dv.shape[1]
+    return pl.pallas_call(
+        project_backward_kernel,
+        out_shape=[
+            jax.ShapeDtypeStruct((WIDE, 2 * width), BF),
+            jax.ShapeDtypeStruct((WIDE, width), BF),
+            jax.ShapeDtypeStruct((count // 2, rows, WIDE), F32),
+            jax.ShapeDtypeStruct((count // 2, rows, WIDE), BF),
+        ],
+        scratch_shapes=[pltpu.VMEM((WIDE, count * rows), BF)],
+        compiler_params=params(),
+        cost_estimate=pl.CostEstimate(
+            flops=12 * count * rows * WIDE * width,
+            bytes_accessed=8 * count * rows * WIDE + 12 * WIDE * width,
+            transcendentals=0,
+        ),
+    )(*pieces, dqk, dv, qk_w, v_w)
+
+
+def output_backward_kernel(*refs):
+    *g_refs, context_ref, out_ref, gcontext_ref, gout_ref = refs
+    rows = g_refs[0].shape[0]
+    total = 0.0
+    for index, g_ref in enumerate(g_refs):
+        at = slice(index * rows, (index + 1) * rows)
+        gcontext_ref[at, :] = matmul_nt(g_ref[...], out_ref[...]).astype(BF)
+        total = total + matmul(context_ref[at, :].T, g_ref[...])
+    gout_ref[...] = total.astype(BF)
+
+
+def output_backward(grads, context, out_w):
+    return pl.pallas_call(
+        output_backward_kernel,
+        out_shape=[
+            jax.ShapeDtypeStruct(context.shape, BF),
+            jax.ShapeDtypeStruct(out_w.shape, BF),
+        ],
+        compiler_params=params(),
+        cost_estimate=pl.CostEstimate(
+            flops=4 * context.shape[0] * context.shape[1] * WIDE,
+            bytes_accessed=2 * context.shape[0] * WIDE + 8 * context.shape[1] * WIDE,
+            transcendentals=0,
+        ),
+    )(*grads, context, out_w)
 
 
 def shift_perm(count, step):
@@ -390,24 +478,26 @@
     pairs = width // PAIR
     extra = PAIR
 
-    def both_cores(value):
-        return jnp.concatenate([value, swap_core(value)], axis=0)
-
     def team_rows(value):
-        parts = [value] + [
-            lax.ppermute(value, "m", shift_perm(n_m, step)) for step in range(1, n_m)
-        ]
-        return [both_cores(part) for part in parts]
-
-    def team_sum(make):
-        total = 0.0
-        for step in reversed(range(n_m)):
+        pieces = []
+        for step in range(n_m):
+            part = lax.ppermute(value, "m", shift_perm(n_m, step)) if step else value
+            pieces += [part, swap_core(part)]
+        return pieces
+
+    def chip_sums(make):
+        sums = []
+        for step in range(n_m):
             part = make(step)
             half = part.shape[0] // 2
-            part = part[:half] + swap_core(part[half:].astype(BF)).astype(F32)
-            if step:
-                part = lax.ppermute(part.astype(BF), "m", shift_perm(n_m, -step)).astype(F32)
-            total = total + part
+            sums.append(part[:half] + swap_core(part[half:].astype(BF)).astype(F32))
+        return sums
+
+    def team_sum(sums):
+        total = sums[0]
+        for step in range(1, n_m):
+            part = lax.ppermute(sums[step].astype(BF), "m", shift_perm(n_m, -step))
+            total = total + part.astype(F32)
         return total
 
     def pair_up(first, second):
@@ -434,6 +524,7 @@
         core, half = lax.axis_index("c"), lax.axis_index("h")
         rank = lax.axis_index(("m", "c"))
         layers = attend_weight.shape[0]
+        own_rows = 2 * layer_input.shape[1]
         tokens = layer_input.shape[1]
         rows0 = attend_weight.shape[2]
         rows1 = 2 * rows0
@@ -477,16 +568,18 @@
             )
 
         small = jnp.concatenate([small_lanes(layer) for layer in range(layers)], axis=0)
-        small = jnp.pad(small.astype(BF).T, ((0, 0), (0, extra - layers * lanes_of)))
-
-        def attn_shard(layer):
-            wa = attend_weight[layer].astype(BF).reshape(3, rows0, team, width)
-            wo = output_weight[layer].astype(BF).reshape(rows0, team, width)
-            packed = jnp.concatenate([pair_up(wa[0], wa[1]), wa[2], wo], axis=-1)
-            packed = jnp.swapaxes(packed, 0, 1)
-            if layer == 0:
-                more = jnp.broadcast_to(small[None], (team,) + small.shape)
-                packed = jnp.concatenate([packed, more], axis=-1)
+        small = together(small)[0].astype(BF).T
+        small = jnp.pad(small, ((0, 0), (0, extra - layers * lanes_of)))
+
+        def attn_shard():
+            wa = attend_weight.astype(BF).reshape(layers, 3, rows0, team, width)
+            wo = output_weight.astype(BF).reshape(layers, rows0, team, width)
+            packed = []
+            for layer in range(layers):
+                packed += [pair_up(wa[layer, 0], wa[layer, 1]), wa[layer, 2], wo[layer]]
+                if layer == 0:
+                    packed.append(jnp.broadcast_to(small[:, None], (rows0, team, extra)))
+            packed = jnp.swapaxes(jnp.concatenate(packed, axis=-1), 0, 1)
             return jnp.broadcast_to(packed[None], (n_h,) + packed.shape).reshape((n_s,) + packed.shape[1:])
 
         def column_attn(shard):
@@ -509,8 +602,7 @@
             give = jnp.where(core == 0, w1[:, :, 1], w1[:, :, 0]).reshape(rows0, 2, WIDE)
             own, give = jnp.swapaxes(own, 0, 1), jnp.swapaxes(give, 0, 1)
             w1 = by_core(own, swap_core(give), 1).reshape(2 * rows1, WIDE)
-            shard = jnp.concatenate([w1, reduce_weight[layer].astype(BF)], axis=0)
-            return shard
+            return w1, reduce_weight[layer].astype(BF)
 
         def column_ffn(shard):
             return gather_shift(shard, ("h", "m"), n_z, 0)
@@ -519,12 +611,13 @@
             return lax.all_gather(column, ("fa", "fb"), axis=0, tiled=True)
 
         attn_w, ffn_w = [None] * layers, [None] * layers
-        attn_column = column_attn(attn_shard(0))
         rows_low = to_halves(layer_input)
         parts = team_rows(rows_low)
-        parts, attn_column, ffn_part = together(parts, attn_column, ffn_shard(0))
-        ffn_column = column_ffn(ffn_part)
-        attn_w[0], small_all = gather_attn(attn_column)
+        column = column_attn(attn_shard())
+        column, parts, (first, second) = together(column, parts, ffn_shard(0))
+        first, second = together(column_ffn(first), second)
+        second = column_ffn(second)
+        attn_w[0], small_all = gather_attn(column[:, : 4 * width + extra])
 
         small_all = small_all.T.astype(F32)
 
@@ -552,43 +645,44 @@
             bias_v = own_width(bv)
             if layer:
                 parts = team_rows(rows_low)
-            qk = jnp.concatenate([((matmul(p, qk_w) + bias_qk) * scale).astype(BF) for p in parts])
-            value = jnp.concatenate([(matmul(p, v_w) + bias_v).astype(BF) for p in parts])
+            qk, value = project_forward(parts, qk_w, v_w, bias_qk, scale, bias_v)
             if layer == 0:
-                qk, value, ffn_column = together(qk, value, ffn_column)
-                ffn_w[0] = gather_ffn(ffn_column)
-                qk, out_w, attn_part, ffn_part, cotangent = together(
-                    qk, out_w, attn_shard(1), ffn_shard(1), cotangent
-                )
-                attn_w[1] = gather_attn(column_attn(attn_part))[0]
-                ffn_column = column_ffn(ffn_part)
-                grad_rows = to_halves(cotangent).astype(F32)
+                later = column[:, 4 * width + extra :]
+                qk, value, second, ffn_part, later = together(qk, value, second, ffn_shard(1), later)
+                attn_w[1], _ = gather_attn(later)
+                ffn_w[0] = gather_ffn(first), gather_ffn(second)
+                ffn_part = column_ffn(jnp.concatenate(ffn_part, axis=0))
             context, logs = attend_forward(qk, value, docs)
-            chip_rows = parts[0].shape[0]
-            first_sum = rows_in + bo + team_sum(
+            chip_rows = 2 * own_rows
+            sums = chip_sums(
                 lambda step: matmul(context[step * chip_rows : (step + 1) * chip_rows], out_w)
             )
+            first_sum = rows_in + bo + team_sum(sums)
             first_norm = layer_norm(first_sum, gain0, shift0)
             norm_low = first_norm.astype(BF)
+            if layer == 0:
+                norm_low, ffn_part = together(norm_low, ffn_part)
+                ffn_part = gather_ffn(ffn_part)
+                ffn_w[1] = (ffn_part, ffn_part)
             chip_norm = (norm_low, swap_core(norm_low))
-            if layer == 0:
-                chip_norm, attn_w[1], ffn_column = together(chip_norm, attn_w[1], ffn_column)
-                ffn_w[1] = gather_ffn(ffn_column)
-            reduced, give, expanded = ffn_forward(chip_norm, ffn_w[layer], bias1)
+            reduced, give, *saved = ffn_forward(chip_norm, ffn_w[layer], bias1)
             second_sum = first_norm + (reduced + swap_core(give).astype(F32) + bias2)
             rows_in = layer_norm(second_sum, gain1, shift1)
-            kept.append((parts, qk, value, context, logs, first_sum, chip_norm, expanded, second_sum))
+            kept.append((parts, qk, value, context, logs, first_sum, saved, second_sum))
             rows_low = rows_in.astype(BF)
+            if layer == 0:
+                rows_low, cotangent = together(rows_low, cotangent)
+                grad_rows = to_halves(cotangent).astype(F32)
         layer_output = from_halves(rows_low)
 
-        def own_ffn(mine):
-            w1 = mine[:, : 2 * rows1].reshape(layers, 2, rows1, WIDE)
+        def own_first(mine):
+            w1 = mine.reshape(layers, 2, rows1, WIDE)
             keep = jnp.where(core == 0, w1[:, :, :rows0], w1[:, :, rows0:])
             give = jnp.where(core == 0, w1[:, :, rows0:], w1[:, :, :rows0])
             got = swap_core(give)
             keep = jnp.swapaxes(keep, 1, 2).reshape(layers, rows0, -1, 1, units)
             got = jnp.swapaxes(got, 1, 2).reshape(layers, rows0, -1, 1, units)
-            return by_core(keep, got, 3).reshape(layers, rows0, -1), mine[:, 2 * rows1 :]
+            return by_core(keep, got, 3).reshape(layers, rows0, -1)
 
         def scatter_attn(first, second):
             first = first.reshape(n_fa, n_fb, n_s * rows0, -1)
@@ -604,25 +698,25 @@
             return column.reshape(n_s, rows0, -1)
 
         def own_attn(columns):
-            column = jnp.concatenate(columns, axis=-1)
-            pieces = lax.all_to_all(column, ("h", "m", "c"), 0, 0, tiled=True)
+            pieces = lax.all_to_all(jnp.concatenate(columns, axis=-1), ("h", "m", "c"), 0, 0, tiled=True)
             pieces = jnp.sum(pieces.reshape((n_h, team, rows0, -1)).astype(F32), axis=0)
-            fours = pieces[..., : 4 * width * layers].reshape(team, rows0, layers, 4 * width)
-            qk = fours[..., : 2 * width].reshape(team, rows0, layers, pairs, 2, PAIR)
-            query = qk[..., 0, :].reshape(team, rows0, layers, width)
-            key = qk[..., 1, :].reshape(team, rows0, layers, width)
-            value, out = fours[..., 2 * width : 3 * width], fours[..., 3 * width :]
-
-            def whole(four):
-                return jnp.transpose(four, (2, 1, 0, 3)).reshape(layers, rows0, WIDE)
-
-            wa = jnp.stack([whole(query), whole(key), whole(value)], axis=1)
-            return wa, whole(out), jnp.sum(pieces[..., 4 * width * layers :], axis=0)
+
+            def whole(first, count):
+                return jnp.swapaxes(pieces[..., first : first + count], 0, 1).reshape(rows0, team * count)
+
+            def matrices(first):
+                qk = whole(first, 2 * width).reshape(rows0, team * pairs, 2, PAIR)
+                query, key = qk[:, :, 0].reshape(rows0, WIDE), qk[:, :, 1].reshape(rows0, WIDE)
+                first = first + 2 * width
+                return jnp.stack([query, key, whole(first, width)]), whole(first + width, width)
+
+            both = [matrices(4 * width * index) for index in range(layers)]
+            return both, jnp.sum(pieces[..., 4 * width * layers :], axis=0)
 
         attn_columns, ffn_mine = [None] * layers, [None] * layers
         small_grads = [None] * layers
         for layer in reversed(range(layers)):
-            parts, qk, value, context, logs, first_sum, chip_norm, expanded, second_sum = kept[layer]
+            parts, qk, value, context, logs, first_sum, saved, second_sum = kept[layer]
             (qk_w, v_w, out_w), ffn = attn_w[layer], ffn_w[layer]
             gain0, gain1 = vectors[layer][3], vectors[layer][4]
             grad_second, dgain1, dshift1 = layer_norm_back(grad_rows, second_sum, gain1)
@@ -631,11 +725,13 @@
             chip_low = (grad_low, swap_core(grad_low))
             if layer + 1 < layers:
                 chip_low, attn_half = together(chip_low, attn_half)
-            reduced, give, dbias1, packed = ffn_backward(chip_low, chip_norm, expanded, ffn)
+            reduced, give, dbias1, dw1, dw2 = ffn_backward(chip_low, saved, ffn)
             if layer + 1 < layers:
                 attn_columns[layer + 1] = finish_attn(*attn_half)
-                ffn_last = ffn_column
-            ffn_column = lax.psum_scatter(packed, ("fa", "fb"), scatter_dimension=0, tiled=True)
+                ffn_last = jnp.concatenate(ffn_columns, axis=1)
+            ffn_columns = [
+                lax.psum_scatter(dw, ("fa", "fb"), scatter_dimension=0, tiled=True) for dw in (dw1, dw2)
+            ]
             grad_first = grad_second + (reduced + swap_core(give).astype(F32))
             grad_sum, dgain0, dshift0 = layer_norm_back(grad_first, first_sum, gain0)
             grad_low = grad_sum.astype(BF)
@@ -644,28 +740,19 @@
             if layer + 1 < layers:
                 grads, ffn_last = together(grads, ffn_last)
                 ffn_mine[layer + 1] = scatter_shift(ffn_last, ("h", "m"), n_z, 0)
-            grad_context = jnp.concatenate([matmul_nt(g, out_w).astype(BF) for g in grads])
-            chip_rows = grads[0].shape[0]
-
-            def piece(rows, step):
-                return rows[step * chip_rows : (step + 1) * chip_rows]
-
-            grad_out = sum(matmul_tn(piece(context, step), g) for step, g in enumerate(grads))
-            grad_out = jnp.swapaxes(grad_out.astype(BF).reshape(width, team, width), 0, 1)
+            grad_context, grad_out = output_backward(grads, context, out_w)
+            grad_out = jnp.swapaxes(grad_out.reshape(width, team, width), 0, 1)
             grad_out = lax.all_to_all(grad_out, ("m", "c"), 0, 0, tiled=True).reshape(WIDE, width)
             if layer + 1 == layers:
                 grad_context, layer_output = together(grad_context, layer_output)
             dqk, dv = attend_backward(grad_context, qk, value, logs, docs)
+            grad_qk, grad_v, own, give = project_backward(parts, dqk, dv, qk_w, v_w)
             if layer + 1 < layers:
-                dqk, ffn_mine[layer + 1], attn_columns[layer + 1] = together(
-                    dqk, ffn_mine[layer + 1], attn_columns[layer + 1]
+                grad_qk, own, give, ffn_mine[layer + 1], attn_columns[layer + 1] = together(
+                    grad_qk, own, give, ffn_mine[layer + 1], attn_columns[layer + 1]
                 )
-            grad_qk = sum(matmul_tn(p, piece(dqk, step)) for step, p in enumerate(parts)).astype(BF)
-            grad_v = sum(matmul_tn(p, piece(dv, step)) for step, p in enumerate(parts)).astype(BF)
-            dqk, dv, grad_qk, grad_v = together(dqk, dv, grad_qk, grad_v)
-            grad_rows = grad_sum + team_sum(
-                lambda step: matmul_nt(piece(dqk, step), qk_w) + matmul_nt(piece(dv, step), v_w)
-            )
+            sums = [own[step] + swap_core(give[step]).astype(F32) for step in range(n_m)]
+            grad_rows = grad_sum + team_sum(sums)
             dbq = jnp.sum(dqk.reshape(-1, pairs, 2, PAIR)[:, :, 0], axis=0, dtype=F32)
             dbv = jnp.sum(dv, axis=0, dtype=F32)
 
@@ -689,20 +776,22 @@
                 lanes = jnp.concatenate(small_grads, axis=0).T.astype(BF)
                 second.append(jnp.pad(lanes, ((0, 0), (0, extra - layers * lanes_of))))
             attn_half = scatter_attn(grad_qk, jnp.concatenate(second, axis=1))
-        ffn_mine[0] = scatter_shift(ffn_column, ("h", "m"), n_z, 0)
-        attn_columns[0] = finish_attn(*attn_half)
-        attn_columns[0], ffn_mine[0] = together(attn_columns[0], ffn_mine[0])
-        wa_out, wo_out, more = own_attn(attn_columns[::-1])
-        w1_out, w2_out = own_ffn(jnp.stack(ffn_mine))
         input_gradient = from_halves(grad_rows.astype(BF)).astype(F32)
+        first = scatter_shift(ffn_columns[0], ("h", "m"), n_z, 0)
+        attn_half, first = together(attn_half, first)
+        second = scatter_shift(ffn_columns[1], ("h", "m"), n_z, 0)
+        column, second, input_gradient = together(finish_attn(*attn_half), second, input_gradient)
+        w1_out = own_first(jnp.stack([first, ffn_mine[1][: 2 * rows1]]))
+        w2_out = jnp.stack([second, ffn_mine[1][2 * rows1 :]])
+        both, more = own_attn([attn_columns[1], column])
 
         more = more[:, : layers * lanes_of].T.reshape(layers, lanes_of, rows0)
         return (
             layer_output,
             input_gradient,
-            wa_out[::-1],
+            jnp.stack([both[1][0], both[0][0]]),
             more[:, :2],
-            wo_out[::-1],
+            jnp.stack([both[1][1], both[0][1]]),
             more[:, 2],
             more[:, 3:5],
             more[:, 5:7],

time: 742 us -> 704 us (0.949)
  matrix products: 35.1 us -> 3.89 us
  Pallas kernels: 127 us -> 151 us
  other arithmetic: 71.6 us -> 59.1 us
  starting transfers between devices: 126 us -> 114 us
    pallas_call x0 -> x6, Pallas kernels: none -> 36 us  [the longest x2 16.5 us: project_backward(): pl.pallas_call(project_backward_kernel, out_shape=[jax.ShapeDtypeStruct((...]
    dot_general x24 -> x0, matrix products: 24.1 us -> none  [the longest x12 12.7 us: matmul_nt(): lax.dot_general(left, right, (((1,), (1,)), ((), ())), preferred_element_...]
    ppermute x14 -> x17, waiting for transfers between devices: 34 us -> 55.9 us  [gather_shift(): lax.ppermute(value, axis, shift_perm(count, step))]
    ppermute x2, waiting for transfers between devices: 45.5 us -> 24.6 us  [from_halves(): got = lax.ppermute(give, 'h', [(0, 1), (1, 0)])]
    all_to_all x2 -> x1, waiting for transfers between devices: 19.2 us -> 0.01 us  [column_attn(): column = lax.all_to_all(shard, ('h', 'm', 'c'), 0, 0, tiled=True)]
    all_to_all x1, waiting for transfers between devices: 0.01 us -> 18.4 us  [own_attn(): lax.all_to_all(jnp.concatenate(columns, axis=-1), ('h', 'm', 'c'), 0, 0,...]
    pallas_call x2, Pallas kernels: 44.6 us -> 30.1 us  [ffn_backward(): pl.pallas_call(ffn_backward_kernel, grid=(2 * WIDE // tile,), in_specs=[h...]
    ppermute x14 -> x17, waiting for transfers between devices: 55.8 us -> 46.2 us  [scatter_shift(): lax.ppermute(piece(step), axis, shift_perm(count, step))]
  transfers between devices with their start and end apart: 82 -> 90, of which waited for: 37 -> 40; matrix products, arithmetic and copies ran while one was open for 22% -> 19% of each run, Pallas kernels for 13% -> 18%
where the time goes in v3:
time: 704 us; the launch traced here: 696 us
  waiting for transfers between devices  261 us (37%)
  Pallas kernels  151 us (21%)
  starting transfers between devices  114 us (16%)
  local copies, waits for them, and re-layouts  89.5 us (13%)
  other arithmetic  59.1 us (8%)
  between operations  16.9 us (2%)
    ppermute x17, waiting for transfers between devices, gather_shift(): lax.ppermute(value, axis, shift_perm(count, step))  55.9 us
    ppermute x17, waiting for transfers between devices, scatter_shift(): lax.ppermute(piece(step), axis, shift_perm(count, step))  46.2 us
    ppermute x5, waiting for transfers between devices, team_rows(): part = lax.ppermute(value, 'm', shift_perm(n_m, step)) if step else value  43.2 us
    pallas_call x2, Pallas kernels, attend_backward(): pl.pallas_call(attend_backward_kernel, grid=(pairs,), in_specs=pair_specs...  36.8 us
    ppermute x4, waiting for transfers between devices, team_sum(): part = lax.ppermute(sums[step].astype(BF), 'm', shift_perm(n_m, -step))  30.2 us
    pallas_call x2, Pallas kernels, ffn_backward(): pl.pallas_call(ffn_backward_kernel, grid=(2 * WIDE // tile,), in_specs=[h...  30.1 us
    ppermute x17, starting transfers between devices, gather_shift(): lax.ppermute(value, axis, shift_perm(count, step))  26.4 us
    ppermute x2, waiting for transfers between devices, from_halves(): got = lax.ppermute(give, 'h', [(0, 1), (1, 0)])  24.6 us
  transfers between devices with their start and end apart: 90, of which 40 were waited for; matrix products, arithmetic and copies ran while one was open for 19% of the time, Pallas kernels for 18%

profile of v3, /device:TPU:0, one launch (start us, length us, event | category | flops | bytes accessed | tf_op | source)
XLA Modules:
  0.0 695.7 jit_solution(2853908526384795390)
XLA Ops:
  31.2 22.4 %collective-permute-done.2.refs_2_ = bf16[256,1024]{1,0:T(8,128)(2,1)} collective-permute-done((bf16[256,1024]{1,0:T(8,128)(2,1)S(1)}, bf16[256,1024]{1,0:T(8,128)(2,1)}, u32[]{:S(2)}, u32[]{:S(2)}) %collective-permute-start.2) | collective-permute-done | bytes 524320 | tf_op jit(solution)/shard_map/ppermute | solution.py:484
  69.1 10.5 %collective-permute-done.10 = bf16[128,1024]{1,0:T(8,128)(2,1)S(1)} collective-permute-done((bf16[128,1024]{1,0:T(8,128)(2,1)S(1)}, bf16[128,1024]{1,0:T(8,128)(2,1)S(1)}, u32[]{:S(2)}, u32[]{:S(2)}) %collective-permute-start.10) | collective-permute-done | bytes 262176 | tf_op jit(solution)/shard_map/ppermute | solution.py:429
  90.5 6.1 collective-permute-start.12
  105.9 9.0 %collective-permute-done.13 = bf16[128,1024]{1,0:T(8,128)(2,1)S(1)} collective-permute-done((bf16[128,1024]{1,0:T(8,128)(2,1)}, bf16[128,1024]{1,0:T(8,128)(2,1)S(1)}, u32[]{:S(2)}, u32[]{:S(2)}) %collective-permute-start.13) | collective-permute-done | bytes 262176 | tf_op jit(solution)/shard_map/ppermute | solution.py:429
  155.0 12.3 %shard_map.221 = (bf16[1024,256]{1,0:T(8,128)(2,1)}, f32[16,1024]{1,0:T(8,128)}) custom-call(bf16[1024,512]{1,0:T(8,128)(2,1)} %get-tuple-element.107.q_ref.k_ref, bf16[1024,512]{1,0:T(8,128)(2,1)} %get-tuple-element.107.q_ref.k_ref, bf16[1024,256]{1,0:T(8,128)(2,1)} %get-tuple-element.108.v_ref, s32[1024,1]{1,0:T(8,128)} %copy.191.col_ref, s32[1,1024]{1,0:T(1,128)} %bitcast.408), custom_call_target="tpu_custom_call" | custom-call | flops 4294967296 | bytes 2621440 | tf_op jit(solution)/shard_map/pallas_call | solution.py:85
  183.2 7.5 %collective-permute-done.24 = bf16[256,1024]{1,0:T(8,128)(2,1)} collective-permute-done((bf16[256,1024]{1,0:T(8,128)(2,1)S(1)}, bf16[256,1024]{1,0:T(8,128)(2,1)}, u32[]{:S(2)}, u32[]{:S(2)}) %collective-permute-start.24) | collective-permute-done | bytes 524320 | tf_op jit(solution)/shard_map/ppermute | solution.py:429
  194.5 8.7 %collective-permute-done.22 = bf16[256,1024]{1,0:T(8,128)(2,1)S(1)} collective-permute-done((bf16[256,1024]{1,0:T(8,128)(2,1)}, bf16[256,1024]{1,0:T(8,128)(2,1)S(1)}, u32[]{:S(2)}, u32[]{:S(2)}) %collective-permute-start.22) | collective-permute-done | bytes 524320 | tf_op jit(solution)/shard_map/ppermute | solution.py:499
  217.2 12.2 %shard_map.222 = (f32[256,1024]{1,0:T(8,128)}, bf16[256,1024]{1,0:T(8,128)(2,1)}, bf16[2048,512]{1,0:T(8,128)(2,1)}, f32[512,2048]{1,0:T(8,128)}, bf16[1024,512]{1,0:T(8,128)(2,1)}) custom-call(bf16[256,1024]{1,0:T(8,128)(2,1)} %copy-done.45, bf16[256,1024]{1,0:T(8,128)(2,1)} %collective-permute-done.26.x1_ref, ...), custom_call_target="tpu_custom_call" | custom-call | flops 4294967296 | bytes 25165824 | tf_op jit(solution)/shard_map/pallas_call | solution.py:219
  230.4 8.9 %collective-permute-done.34 = bf16[2,256,512]{2,1,0:T(8,128)(2,1)} collective-permute-done((bf16[2,256,512]{2,1,0:T(8,128)(2,1)S(1)}, bf16[2,256,512]{2,1,0:T(8,128)(2,1)}, u32[]{:S(2)}, u32[]{:S(2)}) %collective-permute-start.34) | collective-permute-done | bytes 524320 | tf_op jit(solution)/shard_map/ppermute | solution.py:429
  263.5 6.2 shard_map.223
  269.7 12.1 %shard_map.224 = (bf16[1024,256]{1,0:T(8,128)(2,1)}, f32[16,1024]{1,0:T(8,128)}) custom-call(bf16[1024,512]{1,0:T(8,128)(2,1)} %get-tuple-element.119.q_ref.k_ref, bf16[1024,512]{1,0:T(8,128)(2,1)} %get-tuple-element.119.q_ref.k_ref, bf16[1024,256]{1,0:T(8,128)(2,1)} %get-tuple-element.120.v_ref, s32[1024,1]{1,0:T(8,128)} %copy.191.col_ref, s32[1,1024]{1,0:T(1,128)} %bitcast.409), custom_call_target="tpu_custom_call" | custom-call | flops 4294967296 | bytes 2621440 | tf_op jit(solution)/shard_map/pallas_call | solution.py:85
  287.2 12.4 %collective-permute-done.37 = bf16[256,1024]{1,0:T(8,128)(2,1)S(1)} collective-permute-done((bf16[256,1024]{1,0:T(8,128)(2,1)S(1)}, bf16[256,1024]{1,0:T(8,128)(2,1)S(1)}, u32[]{:S(2)}, u32[]{:S(2)}) %collective-permute-start.37) | collective-permute-done | bytes 524320 | tf_op jit(solution)/shard_map/ppermute | solution.py:499
  303.7 8.1 %all-gather.8.cloned.1.call-done.w1_ref.w2_ref = bf16[16,256,1024]{2,1,0:T(8,128)(2,1)} async-done(((bf16[4,256,1024]{2,1,0:T(8,128)(2,1)}), bf16[16,256,1024]{2,1,0:T(8,128)(2,1)}) %all-gather.8.cloned.1.call-update) | async-done | bytes 8388624 | tf_op jit(solution)/shard_map/all_gather | solution.py:611
  311.8 11.6 %shard_map.225 = (f32[256,1024]{1,0:T(8,128)}, bf16[256,1024]{1,0:T(8,128)(2,1)}, bf16[2048,512]{1,0:T(8,128)(2,1)}, f32[512,2048]{1,0:T(8,128)}, bf16[1024,512]{1,0:T(8,128)(2,1)}) custom-call(bf16[256,1024]{1,0:T(8,128)(2,1)} %fusion.30.x0_ref, bf16[256,1024]{1,0:T(8,128)(2,1)} %collective-permute-done.38.x1_ref, ...), custom_call_target="tpu_custom_call" | custom-call | flops 4294967296 | bytes 25165824 | tf_op jit(solution)/shard_map/pallas_call | solution.py:219
  327.1 12.5 %collective-permute-done.40 = bf16[128,1024]{1,0:T(8,128)(2,1)S(1)} collective-permute-done((bf16[128,1024]{1,0:T(8,128)(2,1)S(1)}, bf16[128,1024]{1,0:T(8,128)(2,1)S(1)}, u32[]{:S(2)}, u32[]{:S(2)}) %collective-permute-start.40) | collective-permute-done | bytes 262176 | tf_op jit(solution)/shard_map/ppermute | solution.py:545
  345.1 15.0 %shard_map.226 = (f32[256,1024]{1,0:T(8,128)}, bf16[256,1024]{1,0:T(8,128)(2,1)}, f32[1,2048]{1,0:T(1,128)}, bf16[16,128,1024]{2,1,0:T(8,128)(2,1)}, bf16[16,128,1024]{2,1,0:T(8,128)(2,1)}) custom-call(bf16[256,1024]{1,0:T(8,128)(2,1)} %copy-done.42, bf16[256,1024]{1,0:T(8,128)(2,1)} %copy-done.65, bf16[1024,512]{1,0:T(8,128)(2,1)} %get-tuple-element.126.xt_ref, ...), custom_call_target="tpu_custom_call" | custom-call | flops 8589934592 | bytes 44040192 | tf_op jit(solution)/shard_map/pallas_call | solution.py:295
  367.7 13.2 %collective-permute-done.44.refs_2_ = bf16[256,1024]{1,0:T(8,128)(2,1)S(1)} collective-permute-done((bf16[256,1024]{1,0:T(8,128)(2,1)S(1)}, bf16[256,1024]{1,0:T(8,128)(2,1)S(1)}, u32[]{:S(2)}, u32[]{:S(2)}) %collective-permute-start.44) | collective-permute-done | bytes 524320 | tf_op jit(solution)/shard_map/ppermute | solution.py:484
  383.4 12.9 %collective-permute-done.46 = bf16[128,1024]{1,0:T(8,128)(2,1)S(1)} collective-permute-done((bf16[128,1024]{1,0:T(8,128)(2,1)S(1)}, bf16[128,1024]{1,0:T(8,128)(2,1)S(1)}, u32[]{:S(2)}, u32[]{:S(2)}) %collective-permute-start.46) | collective-permute-done | bytes 262176 | tf_op jit(solution)/shard_map/ppermute | solution.py:554
  403.0 18.4 %shard_map.228 = (bf16[1024,512]{1,0:T(8,128)(2,1)}, bf16[1024,256]{1,0:T(8,128)(2,1)}) custom-call(bf16[1024,512]{1,0:T(8,128)(2,1)} %get-tuple-element.119.q_ref.k_ref, bf16[1024,512]{1,0:T(8,128)(2,1)} %get-tuple-element.119.q_ref.k_ref, bf16[1024,256]{1,0:T(8,128)(2,1)} %get-tuple-element.120.v_ref, bf16[1024,256]{1,0:T(8,128)(2,1)} %get-tuple-element.133.g_ref, ...), custom_call_target="tpu_custom_call" | custom-call | flops 10737418240 | bytes 4718592 | tf_op jit(solution)/shard_map/pallas_call | solution.py:142
  421.4 8.2 %shard_map.229 = (bf16[1024,512]{1,0:T(8,128)(2,1)}, bf16[1024,256]{1,0:T(8,128)(2,1)}, f32[2,256,1024]{2,1,0:T(8,128)}, bf16[2,256,1024]{2,1,0:T(8,128)(2,1)}) custom-call(bf16[256,1024]{1,0:T(8,128)(2,1)} %fusion.29.refs_0_, bf16[256,1024]{1,0:T(8,128)(2,1)} %collective-permute-done.28.refs_1_, bf16[256,1024]{1,0:T(8,128)(2,1)} %collective-permute-done.29.refs_2_, ...), custom_call_target="tpu_custom_call" | custom-call | flops 3221225472 | bytes 11534336 | tf_op jit(solution)/shard_map/pallas_call | solution.py:372
  447.6 9.1 %collective-permute-done.49 = bf16[256,1024]{1,0:T(8,128)(2,1)} collective-permute-done((bf16[256,1024]{1,0:T(8,128)(2,1)}, bf16[256,1024]{1,0:T(8,128)(2,1)}, u32[]{:S(2)}, u32[]{:S(2)}) %collective-permute-start.49) | collective-permute-done | bytes 524320 | tf_op jit(solution)/shard_map/ppermute | solution.py:499
  464.7 15.1 %shard_map.230 = (f32[256,1024]{1,0:T(8,128)}, bf16[256,1024]{1,0:T(8,128)(2,1)}, f32[1,2048]{1,0:T(1,128)}, bf16[16,128,1024]{2,1,0:T(8,128)(2,1)}, bf16[16,128,1024]{2,1,0:T(8,128)(2,1)}) custom-call(bf16[256,1024]{1,0:T(8,128)(2,1)} %copy-done.40, bf16[256,1024]{1,0:T(8,128)(2,1)} %copy-done.63, bf16[1024,512]{1,0:T(8,128)(2,1)} %get-tuple-element.144.xt_ref, ...), custom_call_target="tpu_custom_call" | custom-call | flops 8589934592 | bytes 44040192 | tf_op jit(solution)/shard_map/pallas_call | solution.py:295
  493.2 9.0 %collective-permute-done.60 = bf16[256,512]{1,0:T(8,128)(2,1)} collective-permute-done((bf16[256,512]{1,0:T(8,128)(2,1)S(1)}, bf16[256,512]{1,0:T(8,128)(2,1)}, u32[]{:S(2)}, u32[]{:S(2)}) %collective-permute-start.60) | collective-permute-done | bytes 262176 | tf_op jit(solution)/shard_map/ppermute | solution.py:440
  518.5 18.4 %shard_map.232 = (bf16[1024,512]{1,0:T(8,128)(2,1)}, bf16[1024,256]{1,0:T(8,128)(2,1)}) custom-call(bf16[1024,512]{1,0:T(8,128)(2,1)} %get-tuple-element.107.q_ref.k_ref, bf16[1024,512]{1,0:T(8,128)(2,1)} %get-tuple-element.107.q_ref.k_ref, bf16[1024,256]{1,0:T(8,128)(2,1)} %get-tuple-element.108.v_ref, bf16[1024,256]{1,0:T(8,128)(2,1)} %get-tuple-element.155.g_ref, ...), custom_call_target="tpu_custom_call" | custom-call | flops 10737418240 | bytes 4718592 | tf_op jit(solution)/shard_map/pallas_call | solution.py:142
  545.1 8.3 %shard_map.233 = (bf16[1024,512]{1,0:T(8,128)(2,1)}, bf16[1024,256]{1,0:T(8,128)(2,1)}, f32[2,256,1024]{2,1,0:T(8,128)}, bf16[2,256,1024]{2,1,0:T(8,128)(2,1)}) custom-call(bf16[256,1024]{1,0:T(8,128)(2,1)} %copy-done.43, bf16[256,1024]{1,0:T(8,128)(2,1)} %collective-permute-done.1.refs_1_, bf16[256,1024]{1,0:T(8,128)(2,1)} %collective-permute-done.2.refs_2_, ...), custom_call_target="tpu_custom_call" | custom-call | flops 3221225472 | bytes 11534336 | tf_op jit(solution)/shard_map/pallas_call | solution.py:372
  573.9 9.1 %collective-permute-done.62 = bf16[2,256,512]{2,1,0:T(8,128)(2,1)} collective-permute-done((bf16[2,256,512]{2,1,0:T(8,128)(2,1)}, bf16[2,256,512]{2,1,0:T(8,128)(2,1)}, u32[]{:S(2)}, u32[]{:S(2)}) %collective-permute-start.62) | collective-permute-done | bytes 524320 | tf_op jit(solution)/shard_map/ppermute | solution.py:440
  589.0 7.5 %collective-permute-done.63 = bf16[2,256,640]{2,1,0:T(8,128)(2,1)S(1)} collective-permute-done((bf16[2,256,640]{2,1,0:T(8,128)(2,1)S(1)}, bf16[2,256,640]{2,1,0:T(8,128)(2,1)S(1)}, u32[]{:S(2)}, u32[]{:S(2)}) %collective-permute-start.63) | collective-permute-done | bytes 655392 | tf_op jit(solution)/shard_map/ppermute | solution.py:440
  601.8 11.7 %collective-permute-done.75 = bf16[128,1024]{1,0:T(8,128)(2,1)S(1)} collective-permute-done((bf16[128,1024]{1,0:T(8,128)(2,1)S(1)}, bf16[128,1024]{1,0:T(8,128)(2,1)S(1)}, u32[]{:S(2)}, u32[]{:S(2)}) %collective-permute-start.75) | collective-permute-done | bytes 262176 | tf_op jit(solution)/shard_map/ppermute | solution.py:554
  619.6 10.8 %collective-permute-done.65 = bf16[128,1024]{1,0:T(8,128)(2,1)S(1)} collective-permute-done((bf16[128,1024]{1,0:T(8,128)(2,1)S(1)}, bf16[128,1024]{1,0:T(8,128)(2,1)S(1)}, u32[]{:S(2)}, u32[]{:S(2)}) %collective-permute-start.65) | collective-permute-done | bytes 262176 | tf_op jit(solution)/shard_map/ppermute | solution.py:440
  632.4 9.3 %collective-permute-done.70 = bf16[128,1024]{1,0:T(8,128)(2,1)S(1)} collective-permute-done((bf16[128,1024]{1,0:T(8,128)(2,1)S(1)}, bf16[128,1024]{1,0:T(8,128)(2,1)S(1)}, u32[]{:S(2)}, u32[]{:S(2)}) %collective-permute-start.70) | collective-permute-done | bytes 262176 | tf_op jit(solution)/shard_map/ppermute | solution.py:440
  644.2 9.4 %all-to-all-start.5 = ((bf16[8,32,2176]{2,1,0:T(8,128)(2,1)}), bf16[8,32,2176]{2,1,0:T(8,128)(2,1)S(1)}, u32[]{:S(2)}, u32[]{:S(2)}) async-start(bf16[8,32,2176]{2,1,0:T(8,128)(2,1)} %pad_maximum_fusion.2), calls=%async_computation.9 | async-start | bytes 2228224 | tf_op jit(solution)/shard_map/all_to_all | solution.py:701
  663.1 18.4 %all-to-all-done.5 = bf16[8,32,2176]{2,1,0:T(8,128)(2,1)S(1)} async-done(((bf16[8,32,2176]{2,1,0:T(8,128)(2,1)}), bf16[8,32,2176]{2,1,0:T(8,128)(2,1)S(1)}, u32[]{:S(2)}, u32[]{:S(2)}) %all-to-all-start.5) | async-done | bytes 1114144 | tf_op jit(solution)/shard_map/all_to_all | solution.py:701
  (603 shorter events, 314.4 us)
Async XLA Ops:
  17.3 40.6 %all-to-all-start = ((bf16[8,32,2176]{2,1,0:T(8,128)(2,1)}), bf16[8,32,2176]{2,1,0:T(8,128)(2,1)S(1)}, u32[]{:S(2)}, u32[]{:S(2)}) async-start(bf16[8,32,2176]{2,1,0:T(8,128)(2,1)} %bitcast.12), calls=%async_computation | async-start | bytes 2228224 | tf_op jit(solution)/shard_map/all_to_all | solution.py:586
  21.0 196.2 %all-gather.4.cloned.1.call-start = ((), (), s32[]{:S(2)}) async-start(), calls=%async_computation.10 | async-start | bytes 5242880 | tf_op jit(solution)/shard_map/all_gather | solution.py:611
  25.1 28.4 %collective-permute-start.2 = (bf16[256,1024]{1,0:T(8,128)(2,1)S(1)}, bf16[256,1024]{1,0:T(8,128)(2,1)}, u32[]{:S(2)}, u32[]{:S(2)}) collective-permute-start(bf16[256,1024]{1,0:T(8,128)(2,1)S(1)} %pad_maximum_fusion.6.refs_0_), channel_id=1, source_target_pairs={{0,2},{2,0},{1,3},{3,1},{4,6},{6,4},{5,7},{7,5},{8,10},{10,8},{9,1... | collective-permute-start | bytes 1572872 | tf_op jit(solution)/shard_map/ppermute | solution.py:484
  31.1 26.8 %collective-permute-start.1 = (bf16[256,1024]{1,0:T(8,128)(2,1)S(1)}, bf16[256,1024]{1,0:T(8,128)(2,1)}, u32[]{:S(2)}, u32[]{:S(2)}) collective-permute-start(bf16[256,1024]{1,0:T(8,128)(2,1)S(1)} %pad_maximum_fusion.6.refs_0_), channel_id=1, source_target_pairs={{0,1},{1,0},{2,3},{3,2},{4,5},{5,4},{6,7},{7,6},{8,9},{9,8},{10,11... | collective-permute-start | bytes 1572872 | tf_op jit(solution)/shard_map/ppermute | solution.py:422
  58.3 21.3 %collective-permute-start.10 = (bf16[128,1024]{1,0:T(8,128)(2,1)S(1)}, bf16[128,1024]{1,0:T(8,128)(2,1)S(1)}, u32[]{:S(2)}, u32[]{:S(2)}) collective-permute-start(bf16[128,1024]{1,0:T(8,128)(2,1)S(1)} %bitcast.380), channel_id=1, source_target_pairs={{0,4},{2,6},{4,0},{6,2},{1,5},{3,7},{5,1},{7,3},{8,12},{10,14},{12... | collective-permute-start | bytes 786440 | tf_op jit(solution)/shard_map/ppermute | solution.py:429
  80.7 136.5 %all-gather.6.cloned.1.call-start = ((), (), s32[]{:S(2)}) async-start(), calls=%async_computation.11 | async-start | bytes 5242880 | tf_op jit(solution)/shard_map/all_gather | solution.py:611
  145.6 27.3 %all-to-all-start.1 = ((bf16[4,256,256]{2,1,0:T(8,128)(2,1)}), bf16[4,256,256]{2,1,0:T(8,128)(2,1)S(1)}, u32[]{:S(2)}, u32[]{:S(2)}) async-start(bf16[4,256,256]{2,1,0:T(8,128)(2,1)} %bitcast.47), calls=%async_computation.1 | async-start | bytes 1048576 | tf_op jit(solution)/shard_map/all_to_all | solution.py:595
  149.1 162.7 %all-gather.8.cloned.1.call-start = ((), (), s32[]{:S(2)}) async-start(), calls=%async_computation.12 | async-start | bytes 10485760 | tf_op jit(solution)/shard_map/all_gather | solution.py:611
  150.3 31.0 %collective-permute-start.23 = (bf16[256,1024]{1,0:T(8,128)(2,1)S(1)}, bf16[256,1024]{1,0:T(8,128)(2,1)}, u32[]{:S(2)}, u32[]{:S(2)}) collective-permute-start(bf16[256,1024]{1,0:T(8,128)(2,1)S(1)} %constant_dynamic-update-slice_fusion.4), channel_id=1, source_target_pairs={{0,2},{2,4},{4,6},{6,0},{1,3},{3,5},{5,7},{7,1},{8,10},{10,12},{12... | collective-permute-start | bytes 1572872 | tf_op jit(solution)/shard_map/ppermute | solution.py:429
  152.4 38.3 %collective-permute-start.24 = (bf16[256,1024]{1,0:T(8,128)(2,1)S(1)}, bf16[256,1024]{1,0:T(8,128)(2,1)}, u32[]{:S(2)}, u32[]{:S(2)}) collective-permute-start(bf16[256,1024]{1,0:T(8,128)(2,1)S(1)} %constant_dynamic-update-slice_fusion.4), channel_id=1, source_target_pairs={{0,4},{2,6},{4,0},{6,2},{1,5},{3,7},{5,1},{7,3},{8,12},{10,14},{12... | collective-permute-start | bytes 1572872 | tf_op jit(solution)/shard_map/ppermute | solution.py:429
  153.9 38.7 %collective-permute-start.25 = (bf16[256,1024]{1,0:T(8,128)(2,1)S(1)}, bf16[256,1024]{1,0:T(8,128)(2,1)}, u32[]{:S(2)}, u32[]{:S(2)}) collective-permute-start(bf16[256,1024]{1,0:T(8,128)(2,1)S(1)} %constant_dynamic-update-slice_fusion.4), channel_id=1, source_target_pairs={{0,6},{2,0},{4,2},{6,4},{1,7},{3,1},{5,3},{7,5},{8,14},{10,8},{12,... | collective-permute-start | bytes 1572872 | tf_op jit(solution)/shard_map/ppermute | solution.py:429
  181.3 21.9 %collective-permute-start.22 = (bf16[256,1024]{1,0:T(8,128)(2,1)}, bf16[256,1024]{1,0:T(8,128)(2,1)S(1)}, u32[]{:S(2)}, u32[]{:S(2)}) collective-permute-start(bf16[256,1024]{1,0:T(8,128)(2,1)} %fusion.13), channel_id=1, source_target_pairs={{0,2},{2,0},{1,3},{3,1},{4,6},{6,4},{5,7},{7,5},{8,10},{10,8},{9,1... | collective-permute-start | bytes 1572872 | tf_op jit(solution)/shard_map/ppermute | solution.py:499
  215.7 23.6 %collective-permute-start.34 = (bf16[2,256,512]{2,1,0:T(8,128)(2,1)S(1)}, bf16[2,256,512]{2,1,0:T(8,128)(2,1)}, u32[]{:S(2)}, u32[]{:S(2)}) collective-permute-start(bf16[2,256,512]{2,1,0:T(8,128)(2,1)S(1)} %bitcast_dynamic-update-slice_fusion.14), channel_id=1, source_target_pairs={{0,8},{8,0},{1,9},{9,1},{2,10},{10,2},{3,11},{11,3},{4,12},{12,4},... | collective-permute-start | bytes 1572872 | tf_op jit(solution)/shard_map/ppermute | solution.py:429
  243.3 20.1 %all-to-all-start.2 = ((bf16[4,256,256]{2,1,0:T(8,128)(2,1)}), bf16[4,256,256]{2,1,0:T(8,128)(2,1)S(1)}, u32[]{:S(2)}, u32[]{:S(2)}) async-start(bf16[4,256,256]{2,1,0:T(8,128)(2,1)} %bitcast.374), calls=%async_computation.2 | async-start | bytes 1048576 | tf_op jit(solution)/shard_map/all_to_all | solution.py:595
  246.8 259.8 %reduce-scatter.5.cloned.1.call-start = ((), (), s32[]{:S(2)}) async-start(), calls=%async_computation.13 | async-start | bytes 5242880 | tf_op jit(solution)/shard_map/reduce_scatter | solution.py:733
  360.1 146.4 %reduce-scatter.7.cloned.1.call-start = ((), (), s32[]{:S(2)}) async-start(), calls=%async_computation.14 | async-start | bytes 5242880 | tf_op jit(solution)/shard_map/reduce_scatter | solution.py:733
  367.7 29.5 %collective-permute-start.43 = (bf16[256,1024]{1,0:T(8,128)(2,1)S(1)}, bf16[256,1024]{1,0:T(8,128)(2,1)S(1)}, u32[]{:S(2)}, u32[]{:S(2)}) collective-permute-start(bf16[256,1024]{1,0:T(8,128)(2,1)S(1)} %get-tuple-element.222.refs_0_), channel_id=1, source_target_pairs={{0,1},{1,0},{2,3},{3,2},{4,5},{5,4},{6,7},{7,6},{8,9},{9,8},{10,11... | collective-permute-start | bytes 1572872 | tf_op jit(solution)/shard_map/ppermute | solution.py:422
  436.5 160.2 %reduce-scatter.9.cloned.1.call-start = ((), (), s32[]{:S(2)}) async-start(), calls=%async_computation.15 | async-start | bytes 5242880 | tf_op jit(solution)/shard_map/reduce_scatter | solution.py:733
  479.8 134.8 %reduce-scatter.11.cloned.1.call-start = ((), (), s32[]{:S(2)}) async-start(), calls=%async_computation.16 | async-start | bytes 5242880 | tf_op jit(solution)/shard_map/reduce_scatter | solution.py:733
  509.5 43.8 %collective-permute-start.57 = (bf16[256,1024]{1,0:T(8,128)(2,1)}, bf16[256,1024]{1,0:T(8,128)(2,1)}, u32[]{:S(2)}, u32[]{:S(2)}) collective-permute-start(bf16[256,1024]{1,0:T(8,128)(2,1)} %get-tuple-element.245), channel_id=1, source_target_pairs={{0,2},{2,4},{4,6},{6,0},{1,3},{3,5},{5,7},{7,1},{8,10},{10,12},{12... | collective-permute-start | bytes 1572872 | tf_op jit(solution)/shard_map/ppermute | solution.py:440
  511.5 41.9 %collective-permute-start.58 = (bf16[256,1024]{1,0:T(8,128)(2,1)}, bf16[256,1024]{1,0:T(8,128)(2,1)}, u32[]{:S(2)}, u32[]{:S(2)}) collective-permute-start(bf16[256,1024]{1,0:T(8,128)(2,1)} %get-tuple-element.247), channel_id=1, source_target_pairs={{0,4},{2,6},{4,0},{6,2},{1,5},{3,7},{5,1},{7,3},{8,12},{10,14},{12... | collective-permute-start | bytes 1572872 | tf_op jit(solution)/shard_map/ppermute | solution.py:440
  513.2 40.2 %collective-permute-start.59 = (bf16[256,1024]{1,0:T(8,128)(2,1)}, bf16[256,1024]{1,0:T(8,128)(2,1)}, u32[]{:S(2)}, u32[]{:S(2)}) collective-permute-start(bf16[256,1024]{1,0:T(8,128)(2,1)} %get-tuple-element.246), channel_id=1, source_target_pairs={{0,6},{2,0},{4,2},{6,4},{1,7},{3,1},{5,3},{7,5},{8,14},{10,8},{12,... | collective-permute-start | bytes 1572872 | tf_op jit(solution)/shard_map/ppermute | solution.py:440
  541.0 30.9 %all-to-all-start.4 = ((bf16[4,256,256]{2,1,0:T(8,128)(2,1)}), bf16[4,256,256]{2,1,0:T(8,128)(2,1)}, u32[]{:S(2)}, u32[]{:S(2)}) async-start(bf16[4,256,256]{2,1,0:T(8,128)(2,1)} %bitcast.367), calls=%async_computation.6 | async-start | bytes 1048576 | tf_op jit(solution)/shard_map/all_to_all | solution.py:745
  561.2 23.8 %collective-permute-start.72 = (bf16[256,1024]{1,0:T(8,128)(2,1)}, bf16[256,1024]{1,0:T(8,128)(2,1)}, u32[]{:S(2)}, u32[]{:S(2)}) collective-permute-start(bf16[256,1024]{1,0:T(8,128)(2,1)} %get-tuple-element.261), channel_id=1, source_target_pairs={{0,1},{1,0},{2,3},{3,2},{4,5},{5,4},{6,7},{7,6},{8,9},{9,8},{10,11... | collective-permute-start | bytes 1572872 | tf_op jit(solution)/shard_map/ppermute | solution.py:422
  573.4 23.1 %collective-permute-start.63 = (bf16[2,256,640]{2,1,0:T(8,128)(2,1)S(1)}, bf16[2,256,640]{2,1,0:T(8,128)(2,1)S(1)}, u32[]{:S(2)}, u32[]{:S(2)}) collective-permute-start(bf16[2,256,640]{2,1,0:T(8,128)(2,1)S(1)} %dynamic-slice_bitcast_fusion), channel_id=1, source_target_pairs={{0,8},{8,0},{1,9},{9,1},{2,10},{10,2},{3,11},{11,3},{4,12},{12,4},... | collective-permute-start | bytes 1966088 | tf_op jit(solution)/shard_map/ppermute | solution.py:440
  586.6 27.0 %collective-permute-start.75 = (bf16[128,1024]{1,0:T(8,128)(2,1)S(1)}, bf16[128,1024]{1,0:T(8,128)(2,1)S(1)}, u32[]{:S(2)}, u32[]{:S(2)}) collective-permute-start(bf16[128,1024]{1,0:T(8,128)(2,1)S(1)} %get-tuple-element.278), channel_id=1, source_target_pairs={{0,4},{4,0},{1,5},{5,1},{2,6},{6,2},{3,7},{7,3},{8,12},{12,8},{9,1... | collective-permute-start | bytes 786440 | tf_op jit(solution)/shard_map/ppermute | solution.py:554
  597.9 20.9 %collective-permute-start.64 = (bf16[128,1024]{1,0:T(8,128)(2,1)S(1)}, bf16[128,1024]{1,0:T(8,128)(2,1)S(1)}, u32[]{:S(2)}, u32[]{:S(2)}) collective-permute-start(bf16[128,1024]{1,0:T(8,128)(2,1)S(1)} %get-tuple-element.266), channel_id=1, source_target_pairs={{0,2},{2,4},{4,6},{6,0},{1,3},{3,5},{5,7},{7,1},{8,10},{10,12},{12... | collective-permute-start | bytes 786440 | tf_op jit(solution)/shard_map/ppermute | solution.py:440
  598.0 32.5 %collective-permute-start.65 = (bf16[128,1024]{1,0:T(8,128)(2,1)S(1)}, bf16[128,1024]{1,0:T(8,128)(2,1)S(1)}, u32[]{:S(2)}, u32[]{:S(2)}) collective-permute-start(bf16[128,1024]{1,0:T(8,128)(2,1)S(1)} %get-tuple-element.268), channel_id=1, source_target_pairs={{0,4},{2,6},{4,0},{6,2},{1,5},{3,7},{5,1},{7,3},{8,12},{10,14},{12... | collective-permute-start | bytes 786440 | tf_op jit(solution)/shard_map/ppermute | solution.py:440
  598.5 31.9 %collective-permute-start.66 = (bf16[128,1024]{1,0:T(8,128)(2,1)S(1)}, bf16[128,1024]{1,0:T(8,128)(2,1)S(1)}, u32[]{:S(2)}, u32[]{:S(2)}) collective-permute-start(bf16[128,1024]{1,0:T(8,128)(2,1)S(1)} %get-tuple-element.267), channel_id=1, source_target_pairs={{0,6},{2,0},{4,2},{6,4},{1,7},{3,1},{5,3},{7,5},{8,14},{10,8},{12,... | collective-permute-start | bytes 786440 | tf_op jit(solution)/shard_map/ppermute | solution.py:440
  615.8 25.8 %collective-permute-start.70 = (bf16[128,1024]{1,0:T(8,128)(2,1)S(1)}, bf16[128,1024]{1,0:T(8,128)(2,1)S(1)}, u32[]{:S(2)}, u32[]{:S(2)}) collective-permute-start(bf16[128,1024]{1,0:T(8,128)(2,1)S(1)} %get-tuple-element.265), channel_id=1, source_target_pairs={{0,4},{2,6},{4,0},{6,2},{1,5},{3,7},{5,1},{7,3},{8,12},{10,14},{12... | collective-permute-start | bytes 786440 | tf_op jit(solution)/shard_map/ppermute | solution.py:440
  618.8 22.9 %collective-permute-start.71 = (bf16[128,1024]{1,0:T(8,128)(2,1)S(1)}, bf16[128,1024]{1,0:T(8,128)(2,1)S(1)}, u32[]{:S(2)}, u32[]{:S(2)}) collective-permute-start(bf16[128,1024]{1,0:T(8,128)(2,1)S(1)} %get-tuple-element.264), channel_id=1, source_target_pairs={{0,6},{2,0},{4,2},{6,4},{1,7},{3,1},{5,3},{7,5},{8,14},{10,8},{12,... | collective-permute-start | bytes 786440 | tf_op jit(solution)/shard_map/ppermute | solution.py:440
  644.2 37.4 %all-to-all-start.5 = ((bf16[8,32,2176]{2,1,0:T(8,128)(2,1)}), bf16[8,32,2176]{2,1,0:T(8,128)(2,1)S(1)}, u32[]{:S(2)}, u32[]{:S(2)}) async-start(bf16[8,32,2176]{2,1,0:T(8,128)(2,1)} %pad_maximum_fusion.2), calls=%async_computation.9 | async-start | bytes 2228224 | tf_op jit(solution)/shard_map/all_to_all | solution.py:701
  (124 other events, 1115.6 us)
Sparse Core Ops, SparseCore 0:
  80.8 66.7 all-gather.3
  149.4 52.6 all-gather.5
  206.5 105.2 all-gather.7
  360.3 53.5 reduce-scatter.4
  416.9 55.6 reduce-scatter.6
  479.9 57.4 reduce-scatter.8
  540.6 61.5 reduce-scatter.10

commit v4 on v3

--- a/solution.py
+++ b/solution.py
@@ -422,13 +422,21 @@
     return lax.ppermute(value, "c", [(0, 1), (1, 0)])
 
 
-def gather_shift(value, axis, count, dim):
+def pieces_shift(value, axis, count):
+    return [value] + [lax.ppermute(value, axis, shift_perm(count, step)) for step in range(1, count)]
+
+
+def place_shift(pieces, axis, dim):
+    value, count = pieces[0], len(pieces)
     place = lax.axis_index(axis)
     out = jnp.zeros(value.shape[:dim] + (count,) + value.shape[dim:], value.dtype)
-    for step in range(count):
-        piece = lax.ppermute(value, axis, shift_perm(count, step)) if step else value
+    for step, piece in enumerate(pieces):
         out = lax.dynamic_update_index_in_dim(out, piece, (place - step) % count, dim)
     return out
+
+
+def gather_shift(value, axis, count, dim):
+    return place_shift(pieces_shift(value, axis, count), axis, dim)
 
 
 def scatter_shift(value, axis, count, dim):
@@ -547,11 +555,12 @@
             last = jnp.where(half == 0, got, keep)
             return jnp.concatenate([first, last], axis=0)
 
-        def from_halves(rows):
-            first, last = rows[:tokens], rows[tokens:]
-            keep = jnp.where(half == 0, first, last)
-            give = jnp.where(half == 0, last, first)
-            got = lax.ppermute(give, "h", [(0, 1), (1, 0)])
+        def give_halves(rows):
+            give = jnp.where(half == 0, rows[tokens:], rows[:tokens])
+            return lax.ppermute(give, "h", [(0, 1), (1, 0)])
+
+        def from_halves(rows, got):
+            keep = jnp.where(half == 0, rows[:tokens], rows[tokens:])
             return jnp.where(half == 0, jnp.stack([keep, got]), jnp.stack([got, keep]))
 
         def small_lanes(layer):
@@ -586,10 +595,16 @@
             column = lax.all_to_all(shard, ("h", "m", "c"), 0, 0, tiled=True)
             return column.reshape(n_s * rows0, -1)
 
-        def gather_attn(column):
+        def half_attn(column):
             first, second = column[:, : 2 * width], column[:, 2 * width :]
-            first = gather_shift(gather_shift(first, "fb", n_fb, 0), "fa", n_fa, 0)
-            second = gather_shift(gather_shift(second, "fa", n_fa, 0), "fb", n_fb, 1)
+            return gather_shift(first, "fb", n_fb, 0), gather_shift(second, "fa", n_fa, 0)
+
+        def pieces_attn(first, second):
+            return pieces_shift(first, "fa", n_fa), pieces_shift(second, "fb", n_fb)
+
+        def gather_attn(first, second):
+            first = place_shift(first, "fa", 0)
+            second = place_shift(second, "fb", 1)
             first, second = first.reshape(WIDE, -1), second.reshape(WIDE, -1)
             out = second[:, width : 2 * width].reshape(team, width, width)
             out = lax.all_to_all(out, ("m", "c"), 0, 0, tiled=True)
@@ -614,10 +629,12 @@
         rows_low = to_halves(layer_input)
         parts = team_rows(rows_low)
         column = column_attn(attn_shard())
-        column, parts, (first, second) = together(column, parts, ffn_shard(0))
-        first, second = together(column_ffn(first), second)
+        docs = team_rows(to_halves(documents))
+        column, parts, docs, (first, second) = together(column, parts, docs, ffn_shard(0))
+        halves = half_attn(column[:, : 4 * width + extra])
+        first, second, halves = together(column_ffn(first), second, halves)
         second = column_ffn(second)
-        attn_w[0], small_all = gather_attn(column[:, : 4 * width + extra])
+        attn_w[0], small_all = gather_attn(*pieces_attn(*halves))
 
         small_all = small_all.T.astype(F32)
 
@@ -633,7 +650,7 @@
         def own_width(vector):
             return lax.dynamic_slice_in_dim(vector, rank * width, width)
 
-        docs = jnp.concatenate(team_rows(to_halves(documents)))
+        docs = jnp.concatenate(docs)
         scale = pair_up(jnp.full((width,), HEAD ** (-0.5), F32), jnp.ones((width,), F32))
 
         kept = []
@@ -649,7 +666,7 @@
             if layer == 0:
                 later = column[:, 4 * width + extra :]
                 qk, value, second, ffn_part, later = together(qk, value, second, ffn_shard(1), later)
-                attn_w[1], _ = gather_attn(later)
+                attn_w[1], _ = gather_attn(*pieces_attn(*half_attn(later)))
                 ffn_w[0] = gather_ffn(first), gather_ffn(second)
                 ffn_part = column_ffn(jnp.concatenate(ffn_part, axis=0))
             context, logs = attend_forward(qk, value, docs)
@@ -665,6 +682,8 @@
                 ffn_part = gather_ffn(ffn_part)
                 ffn_w[1] = (ffn_part, ffn_part)
             chip_norm = (norm_low, swap_core(norm_low))
+            if layer:
+                chip_norm, grad_rows = together(chip_norm, grad_rows)
             reduced, give, *saved = ffn_forward(chip_norm, ffn_w[layer], bias1)
             second_sum = first_norm + (reduced + swap_core(give).astype(F32) + bias2)
             rows_in = layer_norm(second_sum, gain1, shift1)
@@ -673,7 +692,7 @@
             if layer == 0:
                 rows_low, cotangent = together(rows_low, cotangent)
                 grad_rows = to_halves(cotangent).astype(F32)
-        layer_output = from_halves(rows_low)
+        output_got = give_halves(rows_low)
 
         def own_first(mine):
             w1 = mine.reshape(layers, 2, rows1, WIDE)
@@ -713,7 +732,7 @@
             both = [matrices(4 * width * index) for index in range(layers)]
             return both, jnp.sum(pieces[..., 4 * width * layers :], axis=0)
 
-        attn_columns, ffn_mine = [None] * layers, [None] * layers
+        attn_columns = [None] * layers
         small_grads = [None] * layers
         for layer in reversed(range(layers)):
             parts, qk, value, context, logs, first_sum, saved, second_sum = kept[layer]
@@ -739,18 +758,18 @@
             grads = team_rows(grad_low)
             if layer + 1 < layers:
                 grads, ffn_last = together(grads, ffn_last)
-                ffn_mine[layer + 1] = scatter_shift(ffn_last, ("h", "m"), n_z, 0)
+                ffn_mine = scatter_shift(ffn_last, ("h", "m"), n_z, 0)
             grad_context, grad_out = output_backward(grads, context, out_w)
             grad_out = jnp.swapaxes(grad_out.reshape(width, team, width), 0, 1)
             grad_out = lax.all_to_all(grad_out, ("m", "c"), 0, 0, tiled=True).reshape(WIDE, width)
-            if layer + 1 == layers:
-                grad_context, layer_output = together(grad_context, layer_output)
             dqk, dv = attend_backward(grad_context, qk, value, logs, docs)
             grad_qk, grad_v, own, give = project_backward(parts, dqk, dv, qk_w, v_w)
             if layer + 1 < layers:
-                grad_qk, own, give, ffn_mine[layer + 1], attn_columns[layer + 1] = together(
-                    grad_qk, own, give, ffn_mine[layer + 1], attn_columns[layer + 1]
+                grad_qk, own, give, ffn_mine, attn_columns[layer + 1] = together(
+                    grad_qk, own, give, ffn_mine, attn_columns[layer + 1]
                 )
+            else:
+                own, give, output_got = together(own, give, output_got)
             sums = [own[step] + swap_core(give[step]).astype(F32) for step in range(n_m)]
             grad_rows = grad_sum + team_sum(sums)
             dbq = jnp.sum(dqk.reshape(-1, pairs, 2, PAIR)[:, :, 0], axis=0, dtype=F32)
@@ -776,13 +795,16 @@
                 lanes = jnp.concatenate(small_grads, axis=0).T.astype(BF)
                 second.append(jnp.pad(lanes, ((0, 0), (0, extra - layers * lanes_of))))
             attn_half = scatter_attn(grad_qk, jnp.concatenate(second, axis=1))
-        input_gradient = from_halves(grad_rows.astype(BF)).astype(F32)
+        grad_low = grad_rows.astype(BF)
+        input_got = give_halves(grad_low)
         first = scatter_shift(ffn_columns[0], ("h", "m"), n_z, 0)
         attn_half, first = together(attn_half, first)
         second = scatter_shift(ffn_columns[1], ("h", "m"), n_z, 0)
-        column, second, input_gradient = together(finish_attn(*attn_half), second, input_gradient)
-        w1_out = own_first(jnp.stack([first, ffn_mine[1][: 2 * rows1]]))
-        w2_out = jnp.stack([second, ffn_mine[1][2 * rows1 :]])
+        column, second, input_got = together(finish_attn(*attn_half), second, input_got)
+        input_gradient = from_halves(grad_low, input_got).astype(F32)
+        layer_output = from_halves(rows_low, output_got)
+        w1_out = own_first(jnp.stack([first, ffn_mine[: 2 * rows1]]))
+        w2_out = jnp.stack([second, ffn_mine[2 * rows1 :]])
         both, more = own_attn([attn_columns[1], column])
 
         more = more[:, : layers * lanes_of].T.reshape(layers, lanes_of, rows0)

time: 704 us -> 686 us (0.974)
  waiting for transfers between devices: 261 us -> 231 us
  starting transfers between devices: 114 us -> 129 us
    ppermute x17, starting transfers between devices: 19.5 us -> 44.8 us  [scatter_shift(): lax.ppermute(piece(step), axis, shift_perm(count, step))]
    ppermute x19, waiting for transfers between devices: 80.6 us -> 58.6 us  [the longest x17 58.6 us: pieces_shift(): lax.ppermute(value, axis, shift_perm(count, step))]
    ppermute x3, waiting for transfers between devices: 17.2 us -> 0.74 us  [to_halves(): got = lax.ppermute(give, 'h', [(0, 1), (1, 0)])]
    ppermute x5, waiting for transfers between devices: 43.2 us -> 56.4 us  [team_rows(): part = lax.ppermute(value, 'm', shift_perm(n_m, step)) if step else value]
    reduce_scatter x4, waiting for transfers between devices: 0.06 us -> 10.4 us  [body(): lax.psum_scatter(dw, ('fa', 'fb'), scatter_dimension=0, tiled=True)]
    all_gather x3, waiting for transfers between devices: 8.07 us -> 0.02 us  [gather_ffn(): return lax.all_gather(column, ('fa', 'fb'), axis=0, tiled=True)]
  transfers between devices with their start and end apart: 90 -> 90, of which waited for: 40 -> 36; matrix products, arithmetic and copies ran while one was open for 19% -> 19% of each run, Pallas kernels for 18% -> 18%
where the time goes in v4:
time: 686 us; the launch traced here: 678 us
  waiting for transfers between devices  231 us (34%)
  Pallas kernels  149 us (22%)
  starting transfers between devices  129 us (19%)
  local copies, waits for them, and re-layouts  84.3 us (12%)
  other arithmetic  65.1 us (9%)
  between operations  16.5 us (2%)
    ppermute x17, waiting for transfers between devices, pieces_shift(): lax.ppermute(value, axis, shift_perm(count, step))  58.6 us
    ppermute x5, waiting for transfers between devices, team_rows(): part = lax.ppermute(value, 'm', shift_perm(n_m, step)) if step else value  56.4 us
    ppermute x17, starting transfers between devices, scatter_shift(): lax.ppermute(piece(step), axis, shift_perm(count, step))  44.8 us
    ppermute x17, waiting for transfers between devices, scatter_shift(): lax.ppermute(piece(step), axis, shift_perm(count, step))  40.6 us
    pallas_call x2, Pallas kernels, attend_backward(): pl.pallas_call(attend_backward_kernel, grid=(pairs,), in_specs=pair_specs...  36.8 us
    ppermute x4, waiting for transfers between devices, team_sum(): part = lax.ppermute(sums[step].astype(BF), 'm', shift_perm(n_m, -step))  32.5 us
    pallas_call x2, Pallas kernels, ffn_backward(): pl.pallas_call(ffn_backward_kernel, grid=(2 * WIDE // tile,), in_specs=[h...  30.4 us
    ppermute x17, starting transfers between devices, pieces_shift(): lax.ppermute(value, axis, shift_perm(count, step))  27.4 us
  transfers between devices with their start and end apart: 90, of which 36 were waited for; matrix products, arithmetic and copies ran while one was open for 19% of the time, Pallas kernels for 18%

profile of v4, /device:TPU:0, one launch (start us, length us, event | category | flops | bytes accessed | tf_op | source)
XLA Modules:
  0.0 678.1 jit_solution(12357110254209931074)
XLA Ops:
  27.9 28.0 %collective-permute-done.2.refs_2_ = bf16[256,1024]{1,0:T(8,128)(2,1)} collective-permute-done((bf16[256,1024]{1,0:T(8,128)(2,1)S(1)}, bf16[256,1024]{1,0:T(8,128)(2,1)}, u32[]{:S(2)}, u32[]{:S(2)}) %collective-permute-start.2) | collective-permute-done | bytes 524320 | tf_op jit(solution)/shard_map/ppermute | solution.py:492
  76.6 6.7 collective-permute-done.10
  102.8 10.4 %collective-permute-done.17 = bf16[128,1024]{1,0:T(8,128)(2,1)S(1)} collective-permute-done((bf16[128,1024]{1,0:T(8,128)(2,1)}, bf16[128,1024]{1,0:T(8,128)(2,1)S(1)}, u32[]{:S(2)}, u32[]{:S(2)}) %collective-permute-start.17) | collective-permute-done | bytes 262176 | tf_op jit(solution)/shard_map/ppermute | solution.py:426
  113.3 6.9 %collective-permute-done.15 = bf16[2,256,512]{2,1,0:T(8,128)(2,1)S(1)} collective-permute-done((bf16[2,256,512]{2,1,0:T(8,128)(2,1)}, bf16[2,256,512]{2,1,0:T(8,128)(2,1)S(1)}, u32[]{:S(2)}, u32[]{:S(2)}) %collective-permute-start.15) | collective-permute-done | bytes 524320 | tf_op jit(solution)/shard_map/ppermute | solution.py:426
  148.5 12.2 %shard_map.221 = (bf16[1024,256]{1,0:T(8,128)(2,1)}, f32[16,1024]{1,0:T(8,128)}) custom-call(bf16[1024,512]{1,0:T(8,128)(2,1)} %get-tuple-element.119.q_ref.k_ref, bf16[1024,512]{1,0:T(8,128)(2,1)} %get-tuple-element.119.q_ref.k_ref, bf16[1024,256]{1,0:T(8,128)(2,1)} %get-tuple-element.120.v_ref, s32[1024,1]{1,0:T(8,128)} %copy.191.col_ref, s32[1,1024]{1,0:T(1,128)} %bitcast.403), custom_call_target="tpu_custom_call" | custom-call | flops 4294967296 | bytes 2621440 | tf_op jit(solution)/shard_map/pallas_call | solution.py:85
  160.7 5.6 all-to-all-done.1
  176.6 7.5 %collective-permute-done.24 = bf16[256,1024]{1,0:T(8,128)(2,1)} collective-permute-done((bf16[256,1024]{1,0:T(8,128)(2,1)S(1)}, bf16[256,1024]{1,0:T(8,128)(2,1)}, u32[]{:S(2)}, u32[]{:S(2)}) %collective-permute-start.24) | collective-permute-done | bytes 524320 | tf_op jit(solution)/shard_map/ppermute | solution.py:426
  187.9 8.5 %collective-permute-done.22 = bf16[256,1024]{1,0:T(8,128)(2,1)S(1)} collective-permute-done((bf16[256,1024]{1,0:T(8,128)(2,1)}, bf16[256,1024]{1,0:T(8,128)(2,1)S(1)}, u32[]{:S(2)}, u32[]{:S(2)}) %collective-permute-start.22) | collective-permute-done | bytes 524320 | tf_op jit(solution)/shard_map/ppermute | solution.py:507
  203.0 9.1 %collective-permute-done.33 = bf16[256,512]{1,0:T(8,128)(2,1)S(1)} collective-permute-done((bf16[256,512]{1,0:T(8,128)(2,1)}, bf16[256,512]{1,0:T(8,128)(2,1)S(1)}, u32[]{:S(2)}, u32[]{:S(2)}) %collective-permute-start.33) | collective-permute-done | bytes 262176 | tf_op jit(solution)/shard_map/ppermute | solution.py:426
  213.6 11.9 %shard_map.222 = (f32[256,1024]{1,0:T(8,128)}, bf16[256,1024]{1,0:T(8,128)(2,1)}, bf16[2048,512]{1,0:T(8,128)(2,1)}, f32[512,2048]{1,0:T(8,128)}, bf16[1024,512]{1,0:T(8,128)(2,1)}) custom-call(bf16[256,1024]{1,0:T(8,128)(2,1)} %copy-done.43, bf16[256,1024]{1,0:T(8,128)(2,1)} %collective-permute-done.26.x1_ref, ...), custom_call_target="tpu_custom_call" | custom-call | flops 4294967296 | bytes 25165824 | tf_op jit(solution)/shard_map/pallas_call | solution.py:219
  251.1 6.9 %collective-permute-done.32 = bf16[2,256,512]{2,1,0:T(8,128)(2,1)} collective-permute-done((bf16[2,256,512]{2,1,0:T(8,128)(2,1)S(1)}, bf16[2,256,512]{2,1,0:T(8,128)(2,1)}, u32[]{:S(2)}, u32[]{:S(2)}) %collective-permute-start.32) | collective-permute-done | bytes 524320 | tf_op jit(solution)/shard_map/ppermute | solution.py:426
  260.2 5.4 shard_map.223
  265.5 12.1 %shard_map.224 = (bf16[1024,256]{1,0:T(8,128)(2,1)}, f32[16,1024]{1,0:T(8,128)}) custom-call(bf16[1024,512]{1,0:T(8,128)(2,1)} %get-tuple-element.135.q_ref.k_ref, bf16[1024,512]{1,0:T(8,128)(2,1)} %get-tuple-element.135.q_ref.k_ref, bf16[1024,256]{1,0:T(8,128)(2,1)} %get-tuple-element.136.v_ref, s32[1024,1]{1,0:T(8,128)} %copy.191.col_ref, s32[1,1024]{1,0:T(1,128)} %bitcast.404), custom_call_target="tpu_custom_call" | custom-call | flops 4294967296 | bytes 2621440 | tf_op jit(solution)/shard_map/pallas_call | solution.py:85
  286.2 14.8 %collective-permute-done.37 = bf16[256,1024]{1,0:T(8,128)(2,1)S(1)} collective-permute-done((bf16[256,1024]{1,0:T(8,128)(2,1)S(1)}, bf16[256,1024]{1,0:T(8,128)(2,1)S(1)}, u32[]{:S(2)}, u32[]{:S(2)}) %collective-permute-start.37) | collective-permute-done | bytes 524320 | tf_op jit(solution)/shard_map/ppermute | solution.py:507
  306.0 11.6 %shard_map.225 = (f32[256,1024]{1,0:T(8,128)}, bf16[256,1024]{1,0:T(8,128)(2,1)}, bf16[2048,512]{1,0:T(8,128)(2,1)}, f32[512,2048]{1,0:T(8,128)}, bf16[1024,512]{1,0:T(8,128)(2,1)}) custom-call(bf16[256,1024]{1,0:T(8,128)(2,1)} %fusion.23.x0_ref, bf16[256,1024]{1,0:T(8,128)(2,1)} %collective-permute-done.38.x1_ref, ...), custom_call_target="tpu_custom_call" | custom-call | flops 4294967296 | bytes 25165824 | tf_op jit(solution)/shard_map/pallas_call | solution.py:219
  327.5 15.1 %shard_map.226 = (f32[256,1024]{1,0:T(8,128)}, bf16[256,1024]{1,0:T(8,128)(2,1)}, f32[1,2048]{1,0:T(1,128)}, bf16[16,128,1024]{2,1,0:T(8,128)(2,1)}, bf16[16,128,1024]{2,1,0:T(8,128)(2,1)}) custom-call(bf16[256,1024]{1,0:T(8,128)(2,1)} %copy-done.41, bf16[256,1024]{1,0:T(8,128)(2,1)} %copy-done.66, bf16[1024,512]{1,0:T(8,128)(2,1)} %get-tuple-element.145.xt_ref, ...), custom_call_target="tpu_custom_call" | custom-call | flops 8589934592 | bytes 44040192 | tf_op jit(solution)/shard_map/pallas_call | solution.py:295
  350.3 12.9 %collective-permute-done.44.refs_2_ = bf16[256,1024]{1,0:T(8,128)(2,1)S(1)} collective-permute-done((bf16[256,1024]{1,0:T(8,128)(2,1)S(1)}, bf16[256,1024]{1,0:T(8,128)(2,1)S(1)}, u32[]{:S(2)}, u32[]{:S(2)}) %collective-permute-start.44) | collective-permute-done | bytes 524320 | tf_op jit(solution)/shard_map/ppermute | solution.py:492
  371.9 18.4 %shard_map.228 = (bf16[1024,512]{1,0:T(8,128)(2,1)}, bf16[1024,256]{1,0:T(8,128)(2,1)}) custom-call(bf16[1024,512]{1,0:T(8,128)(2,1)} %get-tuple-element.135.q_ref.k_ref, bf16[1024,512]{1,0:T(8,128)(2,1)} %get-tuple-element.135.q_ref.k_ref, bf16[1024,256]{1,0:T(8,128)(2,1)} %get-tuple-element.136.v_ref, bf16[1024,256]{1,0:T(8,128)(2,1)} %get-tuple-element.150.g_ref, ...), custom_call_target="tpu_custom_call" | custom-call | flops 10737418240 | bytes 4718592 | tf_op jit(solution)/shard_map/pallas_call | solution.py:142
  390.3 7.8 %shard_map.229 = (bf16[1024,512]{1,0:T(8,128)(2,1)}, bf16[1024,256]{1,0:T(8,128)(2,1)}, f32[2,256,1024]{2,1,0:T(8,128)}, bf16[2,256,1024]{2,1,0:T(8,128)(2,1)}) custom-call(bf16[256,1024]{1,0:T(8,128)(2,1)} %fusion.22.refs_0_, bf16[256,1024]{1,0:T(8,128)(2,1)} %collective-permute-done.28.refs_1_, bf16[256,1024]{1,0:T(8,128)(2,1)} %collective-permute-done.29.refs_2_, ...), custom_call_target="tpu_custom_call" | custom-call | flops 3221225472 | bytes 11534336 | tf_op jit(solution)/shard_map/pallas_call | solution.py:372
  416.0 9.3 %collective-permute-done.49 = bf16[256,1024]{1,0:T(8,128)(2,1)} collective-permute-done((bf16[256,1024]{1,0:T(8,128)(2,1)}, bf16[256,1024]{1,0:T(8,128)(2,1)}, u32[]{:S(2)}, u32[]{:S(2)}) %collective-permute-start.49) | collective-permute-done | bytes 524320 | tf_op jit(solution)/shard_map/ppermute | solution.py:507
  428.9 8.8 %collective-permute-done.51 = bf16[2,256,512]{2,1,0:T(8,128)(2,1)} collective-permute-done((bf16[2,256,512]{2,1,0:T(8,128)(2,1)}, bf16[2,256,512]{2,1,0:T(8,128)(2,1)}, u32[]{:S(2)}, u32[]{:S(2)}) %collective-permute-start.51) | collective-permute-done | bytes 524320 | tf_op jit(solution)/shard_map/ppermute | solution.py:448
  441.7 15.3 %shard_map.230 = (f32[256,1024]{1,0:T(8,128)}, bf16[256,1024]{1,0:T(8,128)(2,1)}, f32[1,2048]{1,0:T(1,128)}, bf16[16,128,1024]{2,1,0:T(8,128)(2,1)}, bf16[16,128,1024]{2,1,0:T(8,128)(2,1)}) custom-call(bf16[256,1024]{1,0:T(8,128)(2,1)} %copy-done.39, bf16[256,1024]{1,0:T(8,128)(2,1)} %copy-done.63, bf16[1024,512]{1,0:T(8,128)(2,1)} %get-tuple-element.164.xt_ref, ...), custom_call_target="tpu_custom_call" | custom-call | flops 8589934592 | bytes 44040192 | tf_op jit(solution)/shard_map/pallas_call | solution.py:295
  474.3 8.0 %collective-permute-done.55.refs_2_ = bf16[256,1024]{1,0:T(8,128)(2,1)} collective-permute-done((bf16[256,1024]{1,0:T(8,128)(2,1)}, bf16[256,1024]{1,0:T(8,128)(2,1)}, u32[]{:S(2)}, u32[]{:S(2)}) %collective-permute-start.55) | collective-permute-done | bytes 524320 | tf_op jit(solution)/shard_map/ppermute | solution.py:492
  494.2 18.4 %shard_map.232 = (bf16[1024,512]{1,0:T(8,128)(2,1)}, bf16[1024,256]{1,0:T(8,128)(2,1)}) custom-call(bf16[1024,512]{1,0:T(8,128)(2,1)} %get-tuple-element.119.q_ref.k_ref, bf16[1024,512]{1,0:T(8,128)(2,1)} %get-tuple-element.119.q_ref.k_ref, bf16[1024,256]{1,0:T(8,128)(2,1)} %get-tuple-element.120.v_ref, bf16[1024,256]{1,0:T(8,128)(2,1)} %get-tuple-element.175.g_ref, ...), custom_call_target="tpu_custom_call" | custom-call | flops 10737418240 | bytes 4718592 | tf_op jit(solution)/shard_map/pallas_call | solution.py:142
  524.6 7.8 %shard_map.233 = (bf16[1024,512]{1,0:T(8,128)(2,1)}, bf16[1024,256]{1,0:T(8,128)(2,1)}, f32[2,256,1024]{2,1,0:T(8,128)}, bf16[2,256,1024]{2,1,0:T(8,128)(2,1)}) custom-call(bf16[256,1024]{1,0:T(8,128)(2,1)} %copy-done.42, bf16[256,1024]{1,0:T(8,128)(2,1)} %copy-done.61, bf16[256,1024]{1,0:T(8,128)(2,1)} %collective-permute-done.2.refs_2_, ...), custom_call_target="tpu_custom_call" | custom-call | flops 3221225472 | bytes 11534336 | tf_op jit(solution)/shard_map/pallas_call | solution.py:372
  546.5 17.5 %collective-permute-done.65 = bf16[2,256,512]{2,1,0:T(8,128)(2,1)} collective-permute-done((bf16[2,256,512]{2,1,0:T(8,128)(2,1)}, bf16[2,256,512]{2,1,0:T(8,128)(2,1)}, u32[]{:S(2)}, u32[]{:S(2)}) %collective-permute-start.65) | collective-permute-done | bytes 524320 | tf_op jit(solution)/shard_map/ppermute | solution.py:448
  575.7 10.4 %reduce-scatter.11.cloned.1.call-done = bf16[4,128,1024]{2,1,0:T(8,128)(2,1)} async-done(((bf16[16,128,1024]{2,1,0:T(8,128)(2,1)}), bf16[4,128,1024]{2,1,0:T(8,128)(2,1)}) %reduce-scatter.11.cloned.1.call-update) | async-done | bytes 1048592 | tf_op jit(solution)/shard_map/reduce_scatter | solution.py:752
  588.8 8.8 %collective-permute-start.73 = (bf16[128,1024]{1,0:T(8,128)(2,1)S(1)}, bf16[128,1024]{1,0:T(8,128)(2,1)S(1)}, u32[]{:S(2)}, u32[]{:S(2)}) collective-permute-start(bf16[128,1024]{1,0:T(8,128)(2,1)S(1)} %get-tuple-element.279), channel_id=1, source_target_pairs={{0,4},{2,6},{4,0},{6,2},{1,5},{3,7},{5,1},{7,3},{8,12},{10,14},{12... | collective-permute-start | bytes 786440 | tf_op jit(solution)/shard_map/ppermute | solution.py:448
  597.6 15.0 %collective-permute-start.74 = (bf16[128,1024]{1,0:T(8,128)(2,1)S(1)}, bf16[128,1024]{1,0:T(8,128)(2,1)S(1)}, u32[]{:S(2)}, u32[]{:S(2)}) collective-permute-start(bf16[128,1024]{1,0:T(8,128)(2,1)S(1)} %get-tuple-element.278), channel_id=1, source_target_pairs={{0,6},{2,0},{4,2},{6,4},{1,7},{3,1},{5,3},{7,5},{8,14},{10,8},{12,... | collective-permute-start | bytes 786440 | tf_op jit(solution)/shard_map/ppermute | solution.py:448
  616.3 7.7 %collective-permute-done.73 = bf16[128,1024]{1,0:T(8,128)(2,1)S(1)} collective-permute-done((bf16[128,1024]{1,0:T(8,128)(2,1)S(1)}, bf16[128,1024]{1,0:T(8,128)(2,1)S(1)}, u32[]{:S(2)}, u32[]{:S(2)}) %collective-permute-start.73) | collective-permute-done | bytes 262176 | tf_op jit(solution)/shard_map/ppermute | solution.py:448
  627.9 8.3 %all-to-all-start.5 = ((bf16[8,32,2176]{2,1,0:T(8,128)(2,1)}), bf16[8,32,2176]{2,1,0:T(8,128)(2,1)S(1)}, u32[]{:S(2)}, u32[]{:S(2)}) async-start(bf16[8,32,2176]{2,1,0:T(8,128)(2,1)} %pad_maximum_fusion.2), calls=%async_computation.9 | async-start | bytes 2228224 | tf_op jit(solution)/shard_map/all_to_all | solution.py:720
  648.3 15.9 %all-to-all-done.5 = bf16[8,32,2176]{2,1,0:T(8,128)(2,1)S(1)} async-done(((bf16[8,32,2176]{2,1,0:T(8,128)(2,1)}), bf16[8,32,2176]{2,1,0:T(8,128)(2,1)S(1)}, u32[]{:S(2)}, u32[]{:S(2)}) %all-to-all-start.5) | async-done | bytes 1114144 | tf_op jit(solution)/shard_map/all_to_all | solution.py:720
  (605 shorter events, 298.5 us)
Async XLA Ops:
  13.1 43.6 %collective-permute-start.4 = (s32[128]{0:T(128)S(1)}, s32[128]{0:T(128)S(1)}, u32[]{:S(2)}, u32[]{:S(2)}) collective-permute-start(s32[128]{0:T(128)S(1)} %fusion.46), channel_id=1, source_target_pairs={{0,4},{4,0},{1,5},{5,1},{2,6},{6,2},{3,7},{7,3},{8,12},{12,8},{9,1... | collective-permute-start | bytes 1544 | tf_op jit(solution)/shard_map/ppermute | solution.py:553
  18.2 43.4 %all-to-all-start = ((bf16[8,32,2176]{2,1,0:T(8,128)(2,1)}), bf16[8,32,2176]{2,1,0:T(8,128)(2,1)S(1)}, u32[]{:S(2)}, u32[]{:S(2)}) async-start(bf16[8,32,2176]{2,1,0:T(8,128)(2,1)} %bitcast.12), calls=%async_computation | async-start | bytes 2228224 | tf_op jit(solution)/shard_map/all_to_all | solution.py:595
  23.4 190.2 %all-gather.4.cloned.1.call-start = ((), (), s32[]{:S(2)}) async-start(), calls=%async_computation.10 | async-start | bytes 5242880 | tf_op jit(solution)/shard_map/all_gather | solution.py:626
  25.1 30.8 %collective-permute-start.2 = (bf16[256,1024]{1,0:T(8,128)(2,1)S(1)}, bf16[256,1024]{1,0:T(8,128)(2,1)}, u32[]{:S(2)}, u32[]{:S(2)}) collective-permute-start(bf16[256,1024]{1,0:T(8,128)(2,1)S(1)} %pad_maximum_fusion.6.refs_0_), channel_id=1, source_target_pairs={{0,2},{2,0},{1,3},{3,1},{4,6},{6,4},{5,7},{7,5},{8,10},{10,8},{9,1... | collective-permute-start | bytes 1572872 | tf_op jit(solution)/shard_map/ppermute | solution.py:492
  27.1 33.3 %collective-permute-start.8 = (bf16[2,32,1024]{2,0,1:T(2,128)(2,1)S(1)}, bf16[2,32,1024]{2,0,1:T(2,128)(2,1)S(1)}, u32[]{:S(2)}, u32[]{:S(2)}) collective-permute-start(bf16[2,32,1024]{2,0,1:T(2,128)(2,1)S(1)} %bitcast.399), channel_id=1, source_target_pairs={{0,1},{1,0},{2,3},{3,2},{4,5},{5,4},{6,7},{7,6},{8,9},{9,8},{10,11... | collective-permute-start | bytes 393224 | tf_op jit(solution)/shard_map/ppermute | solution.py:422
  27.3 34.2 %collective-permute-start.1 = (bf16[256,1024]{1,0:T(8,128)(2,1)S(1)}, bf16[256,1024]{1,0:T(8,128)(2,1)S(1)}, u32[]{:S(2)}, u32[]{:S(2)}) collective-permute-start(bf16[256,1024]{1,0:T(8,128)(2,1)S(1)} %pad_maximum_fusion.6.refs_0_), channel_id=1, source_target_pairs={{0,1},{1,0},{2,3},{3,2},{4,5},{5,4},{6,7},{7,6},{8,9},{9,8},{10,11... | collective-permute-start | bytes 1572872 | tf_op jit(solution)/shard_map/ppermute | solution.py:422
  84.4 129.2 %all-gather.6.cloned.1.call-start = ((), (), s32[]{:S(2)}) async-start(), calls=%async_computation.11 | async-start | bytes 5242880 | tf_op jit(solution)/shard_map/all_gather | solution.py:626
  97.4 27.5 %collective-permute-start.14 = (bf16[2,256,640]{2,1,0:T(8,128)(2,1)}, bf16[2,256,640]{2,1,0:T(8,128)(2,1)}, u32[]{:S(2)}, u32[]{:S(2)}) collective-permute-start(bf16[2,256,640]{2,1,0:T(8,128)(2,1)} %bitcast_dynamic-update-slice_fusion.12), channel_id=1, source_target_pairs={{0,8},{8,0},{1,9},{9,1},{2,10},{10,2},{3,11},{11,3},{4,12},{12,4},... | collective-permute-start | bytes 1966088 | tf_op jit(solution)/shard_map/ppermute | solution.py:426
  139.0 27.3 %all-to-all-start.1 = ((bf16[4,256,256]{2,1,0:T(8,128)(2,1)}), bf16[4,256,256]{2,1,0:T(8,128)(2,1)S(1)}, u32[]{:S(2)}, u32[]{:S(2)}) async-start(bf16[4,256,256]{2,1,0:T(8,128)(2,1)} %bitcast.47), calls=%async_computation.1 | async-start | bytes 1048576 | tf_op jit(solution)/shard_map/all_to_all | solution.py:610
  142.6 163.4 %all-gather.8.cloned.1.call-start = ((), (), s32[]{:S(2)}) async-start(), calls=%async_computation.12 | async-start | bytes 10485760 | tf_op jit(solution)/shard_map/all_gather | solution.py:626
  143.8 30.9 %collective-permute-start.23 = (bf16[256,1024]{1,0:T(8,128)(2,1)S(1)}, bf16[256,1024]{1,0:T(8,128)(2,1)}, u32[]{:S(2)}, u32[]{:S(2)}) collective-permute-start(bf16[256,1024]{1,0:T(8,128)(2,1)S(1)} %constant_dynamic-update-slice_fusion.4), channel_id=1, source_target_pairs={{0,2},{2,4},{4,6},{6,0},{1,3},{3,5},{5,7},{7,1},{8,10},{10,12},{12... | collective-permute-start | bytes 1572872 | tf_op jit(solution)/shard_map/ppermute | solution.py:426
  145.8 38.3 %collective-permute-start.24 = (bf16[256,1024]{1,0:T(8,128)(2,1)S(1)}, bf16[256,1024]{1,0:T(8,128)(2,1)}, u32[]{:S(2)}, u32[]{:S(2)}) collective-permute-start(bf16[256,1024]{1,0:T(8,128)(2,1)S(1)} %constant_dynamic-update-slice_fusion.4), channel_id=1, source_target_pairs={{0,4},{2,6},{4,0},{6,2},{1,5},{3,7},{5,1},{7,3},{8,12},{10,14},{12... | collective-permute-start | bytes 1572872 | tf_op jit(solution)/shard_map/ppermute | solution.py:426
  147.2 38.8 %collective-permute-start.25 = (bf16[256,1024]{1,0:T(8,128)(2,1)S(1)}, bf16[256,1024]{1,0:T(8,128)(2,1)}, u32[]{:S(2)}, u32[]{:S(2)}) collective-permute-start(bf16[256,1024]{1,0:T(8,128)(2,1)S(1)} %constant_dynamic-update-slice_fusion.4), channel_id=1, source_target_pairs={{0,6},{2,0},{4,2},{6,4},{1,7},{3,1},{5,3},{7,5},{8,14},{10,8},{12,... | collective-permute-start | bytes 1572872 | tf_op jit(solution)/shard_map/ppermute | solution.py:426
  238.4 245.0 %reduce-scatter.5.cloned.1.call-start = ((), (), s32[]{:S(2)}) async-start(), calls=%async_computation.13 | async-start | bytes 5242880 | tf_op jit(solution)/shard_map/reduce_scatter | solution.py:752
  342.6 140.7 %reduce-scatter.7.cloned.1.call-start = ((), (), s32[]{:S(2)}) async-start(), calls=%async_computation.14 | async-start | bytes 5242880 | tf_op jit(solution)/shard_map/reduce_scatter | solution.py:752
  364.0 34.1 %collective-permute-start.46 = (bf16[128,1024]{1,0:T(8,128)(2,1)S(1)}, bf16[128,1024]{1,0:T(8,128)(2,1)S(1)}, u32[]{:S(2)}, u32[]{:S(2)}) collective-permute-start(bf16[128,1024]{1,0:T(8,128)(2,1)S(1)} %get-tuple-element.294), channel_id=1, source_target_pairs={{0,4},{4,0},{1,5},{5,1},{2,6},{6,2},{3,7},{7,3},{8,12},{12,8},{9,1... | collective-permute-start | bytes 786440 | tf_op jit(solution)/shard_map/ppermute | solution.py:560
  405.1 162.7 %reduce-scatter.9.cloned.1.call-start = ((), (), s32[]{:S(2)}) async-start(), calls=%async_computation.15 | async-start | bytes 5242880 | tf_op jit(solution)/shard_map/reduce_scatter | solution.py:752
  411.8 26.0 %collective-permute-start.51 = (bf16[2,256,512]{2,1,0:T(8,128)(2,1)}, bf16[2,256,512]{2,1,0:T(8,128)(2,1)}, u32[]{:S(2)}, u32[]{:S(2)}) collective-permute-start(bf16[2,256,512]{2,1,0:T(8,128)(2,1)} %dynamic-slice_bitcast_fusion.5), channel_id=1, source_target_pairs={{0,16},{16,0},{1,17},{17,1},{2,18},{18,2},{3,19},{19,3},{4,20},{20... | collective-permute-start | bytes 1572872 | tf_op jit(solution)/shard_map/ppermute | solution.py:448
  457.1 129.0 %reduce-scatter.11.cloned.1.call-start = ((), (), s32[]{:S(2)}) async-start(), calls=%async_computation.16 | async-start | bytes 5242880 | tf_op jit(solution)/shard_map/reduce_scatter | solution.py:752
  486.4 46.0 %collective-permute-start.57 = (bf16[256,1024]{1,0:T(8,128)(2,1)}, bf16[256,1024]{1,0:T(8,128)(2,1)}, u32[]{:S(2)}, u32[]{:S(2)}) collective-permute-start(bf16[256,1024]{1,0:T(8,128)(2,1)} %get-tuple-element.259), channel_id=1, source_target_pairs={{0,2},{2,4},{4,6},{6,0},{1,3},{3,5},{5,7},{7,1},{8,10},{10,12},{12... | collective-permute-start | bytes 1572872 | tf_op jit(solution)/shard_map/ppermute | solution.py:448
  486.6 45.8 %collective-permute-start.58 = (bf16[256,1024]{1,0:T(8,128)(2,1)}, bf16[256,1024]{1,0:T(8,128)(2,1)}, u32[]{:S(2)}, u32[]{:S(2)}) collective-permute-start(bf16[256,1024]{1,0:T(8,128)(2,1)} %get-tuple-element.261), channel_id=1, source_target_pairs={{0,4},{2,6},{4,0},{6,2},{1,5},{3,7},{5,1},{7,3},{8,12},{10,14},{12... | collective-permute-start | bytes 1572872 | tf_op jit(solution)/shard_map/ppermute | solution.py:448
  487.7 44.7 %collective-permute-start.59 = (bf16[256,1024]{1,0:T(8,128)(2,1)}, bf16[256,1024]{1,0:T(8,128)(2,1)}, u32[]{:S(2)}, u32[]{:S(2)}) collective-permute-start(bf16[256,1024]{1,0:T(8,128)(2,1)} %get-tuple-element.260), channel_id=1, source_target_pairs={{0,6},{2,0},{4,2},{6,4},{1,7},{3,1},{5,3},{7,5},{8,14},{10,8},{12,... | collective-permute-start | bytes 1572872 | tf_op jit(solution)/shard_map/ppermute | solution.py:448
  537.9 26.0 %collective-permute-start.65 = (bf16[2,256,512]{2,1,0:T(8,128)(2,1)}, bf16[2,256,512]{2,1,0:T(8,128)(2,1)}, u32[]{:S(2)}, u32[]{:S(2)}) collective-permute-start(bf16[2,256,512]{2,1,0:T(8,128)(2,1)} %dynamic-slice_bitcast_fusion.1), channel_id=1, source_target_pairs={{0,16},{16,0},{1,17},{17,1},{2,18},{18,2},{3,19},{19,3},{4,20},{20... | collective-permute-start | bytes 1572872 | tf_op jit(solution)/shard_map/ppermute | solution.py:448
  540.7 26.6 %collective-permute-start.66 = (bf16[2,256,640]{2,1,0:T(8,128)(2,1)S(1)}, bf16[2,256,640]{2,1,0:T(8,128)(2,1)S(1)}, u32[]{:S(2)}, u32[]{:S(2)}) collective-permute-start(bf16[2,256,640]{2,1,0:T(8,128)(2,1)S(1)} %dynamic-slice_bitcast_fusion), channel_id=1, source_target_pairs={{0,8},{8,0},{1,9},{9,1},{2,10},{10,2},{3,11},{11,3},{4,12},{12,4},... | collective-permute-start | bytes 1966088 | tf_op jit(solution)/shard_map/ppermute | solution.py:448
  541.5 26.0 %collective-permute-start.62 = (bf16[256,1024]{1,0:T(8,128)(2,1)S(1)}, bf16[256,1024]{1,0:T(8,128)(2,1)S(1)}, u32[]{:S(2)}, u32[]{:S(2)}) collective-permute-start(bf16[256,1024]{1,0:T(8,128)(2,1)S(1)} %copy-done.45), channel_id=1, source_target_pairs={{0,1},{1,0},{2,3},{3,2},{4,5},{5,4},{6,7},{7,6},{8,9},{9,8},{10,11... | collective-permute-start | bytes 1572872 | tf_op jit(solution)/shard_map/ppermute | solution.py:422
  570.6 27.0 %collective-permute-start.68 = (bf16[128,1024]{1,0:T(8,128)(2,1)S(1)}, bf16[128,1024]{1,0:T(8,128)(2,1)}, u32[]{:S(2)}, u32[]{:S(2)}) collective-permute-start(bf16[128,1024]{1,0:T(8,128)(2,1)S(1)} %get-tuple-element.282), channel_id=1, source_target_pairs={{0,4},{2,6},{4,0},{6,2},{1,5},{3,7},{5,1},{7,3},{8,12},{10,14},{12... | collective-permute-start | bytes 786440 | tf_op jit(solution)/shard_map/ppermute | solution.py:448
  573.0 39.7 %collective-permute-start.69 = (bf16[128,1024]{1,0:T(8,128)(2,1)S(1)}, bf16[128,1024]{1,0:T(8,128)(2,1)}, u32[]{:S(2)}, u32[]{:S(2)}) collective-permute-start(bf16[128,1024]{1,0:T(8,128)(2,1)S(1)} %get-tuple-element.281), channel_id=1, source_target_pairs={{0,6},{2,0},{4,2},{6,4},{1,7},{3,1},{5,3},{7,5},{8,14},{10,8},{12,... | collective-permute-start | bytes 786440 | tf_op jit(solution)/shard_map/ppermute | solution.py:448
  575.2 51.5 %collective-permute-start.75 = (bf16[128,1024]{1,0:T(8,128)(2,1)}, bf16[128,1024]{1,0:T(8,128)(2,1)}, u32[]{:S(2)}, u32[]{:S(2)}) collective-permute-start(bf16[128,1024]{1,0:T(8,128)(2,1)} %get-tuple-element.292), channel_id=1, source_target_pairs={{0,4},{4,0},{1,5},{5,1},{2,6},{6,2},{3,7},{7,3},{8,12},{12,8},{9,1... | collective-permute-start | bytes 786440 | tf_op jit(solution)/shard_map/ppermute | solution.py:560
  587.2 27.5 %collective-permute-start.72 = (bf16[128,1024]{1,0:T(8,128)(2,1)S(1)}, bf16[128,1024]{1,0:T(8,128)(2,1)S(1)}, u32[]{:S(2)}, u32[]{:S(2)}) collective-permute-start(bf16[128,1024]{1,0:T(8,128)(2,1)S(1)} %get-tuple-element.277), channel_id=1, source_target_pairs={{0,2},{2,4},{4,6},{6,0},{1,3},{3,5},{5,7},{7,1},{8,10},{10,12},{12... | collective-permute-start | bytes 786440 | tf_op jit(solution)/shard_map/ppermute | solution.py:448
  588.8 35.2 %collective-permute-start.73 = (bf16[128,1024]{1,0:T(8,128)(2,1)S(1)}, bf16[128,1024]{1,0:T(8,128)(2,1)S(1)}, u32[]{:S(2)}, u32[]{:S(2)}) collective-permute-start(bf16[128,1024]{1,0:T(8,128)(2,1)S(1)} %get-tuple-element.279), channel_id=1, source_target_pairs={{0,4},{2,6},{4,0},{6,2},{1,5},{3,7},{5,1},{7,3},{8,12},{10,14},{12... | collective-permute-start | bytes 786440 | tf_op jit(solution)/shard_map/ppermute | solution.py:448
  597.6 27.7 %collective-permute-start.74 = (bf16[128,1024]{1,0:T(8,128)(2,1)S(1)}, bf16[128,1024]{1,0:T(8,128)(2,1)S(1)}, u32[]{:S(2)}, u32[]{:S(2)}) collective-permute-start(bf16[128,1024]{1,0:T(8,128)(2,1)S(1)} %get-tuple-element.278), channel_id=1, source_target_pairs={{0,6},{2,0},{4,2},{6,4},{1,7},{3,1},{5,3},{7,5},{8,14},{10,8},{12,... | collective-permute-start | bytes 786440 | tf_op jit(solution)/shard_map/ppermute | solution.py:448
  627.9 36.3 %all-to-all-start.5 = ((bf16[8,32,2176]{2,1,0:T(8,128)(2,1)}), bf16[8,32,2176]{2,1,0:T(8,128)(2,1)S(1)}, u32[]{:S(2)}, u32[]{:S(2)}) async-start(bf16[8,32,2176]{2,1,0:T(8,128)(2,1)} %pad_maximum_fusion.2), calls=%async_computation.9 | async-start | bytes 2228224 | tf_op jit(solution)/shard_map/all_to_all | solution.py:720
  (125 other events, 1135.0 us)
Sparse Core Ops, SparseCore 0:
  84.6 67.5 all-gather.3
  154.0 56.0 all-gather.5
  212.0 94.0 all-gather.7
  342.7 53.3 reduce-scatter.4
  399.3 63.8 reduce-scatter.6
  466.0 52.9 reduce-scatter.8
  522.2 63.8 reduce-scatter.10

commit v5 on v4

--- a/solution.py
+++ b/solution.py
@@ -798,9 +798,8 @@
         grad_low = grad_rows.astype(BF)
         input_got = give_halves(grad_low)
         first = scatter_shift(ffn_columns[0], ("h", "m"), n_z, 0)
-        attn_half, first = together(attn_half, first)
         second = scatter_shift(ffn_columns[1], ("h", "m"), n_z, 0)
-        column, second, input_got = together(finish_attn(*attn_half), second, input_got)
+        column, first, second, input_got = together(finish_attn(*attn_half), first, second, input_got)
         input_gradient = from_halves(grad_low, input_got).astype(F32)
         layer_output = from_halves(rows_low, output_got)
         w1_out = own_first(jnp.stack([first, ffn_mine[: 2 * rows1]]))

time: 686 us -> 699 us (1.019)
  waiting for transfers between devices: 231 us -> 269 us
  starting transfers between devices: 129 us -> 100 us
    ppermute x17, waiting for transfers between devices: 40.6 us -> 70.5 us  [scatter_shift(): lax.ppermute(piece(step), axis, shift_perm(count, step))]
    ppermute x17, starting transfers between devices: 44.8 us -> 22.9 us  [scatter_shift(): lax.ppermute(piece(step), axis, shift_perm(count, step))]
    ppermute x2, waiting for transfers between devices: 0.01 us -> 12.9 us  [give_halves(): return lax.ppermute(give, 'h', [(0, 1), (1, 0)])]
    reduce_scatter x4, waiting for transfers between devices: 10.4 us -> 0.04 us  [body(): lax.psum_scatter(dw, ('fa', 'fb'), scatter_dimension=0, tiled=True)]
  transfers between devices with their start and end apart: 90 -> 90, of which waited for: 36 -> 40; matrix products, arithmetic and copies ran while one was open for 19% -> 20% of each run, Pallas kernels for 18% -> 18%
where the time goes in v5:
time: 699 us; the launch traced here: 691 us
  waiting for transfers between devices  269 us (38%)
  Pallas kernels  149 us (21%)
  starting transfers between devices  100 us (14%)
  local copies, waits for them, and re-layouts  86 us (12%)
  other arithmetic  66.1 us (9%)
  between operations  16.4 us (2%)
    ppermute x17, waiting for transfers between devices, scatter_shift(): lax.ppermute(piece(step), axis, shift_perm(count, step))  70.5 us
    ppermute x17, waiting for transfers between devices, pieces_shift(): lax.ppermute(value, axis, shift_perm(count, step))  58.6 us
    ppermute x5, waiting for transfers between devices, team_rows(): part = lax.ppermute(value, 'm', shift_perm(n_m, step)) if step else value  56.4 us
    ppermute x4, waiting for transfers between devices, team_sum(): part = lax.ppermute(sums[step].astype(BF), 'm', shift_perm(n_m, -step))  38.4 us
    pallas_call x2, Pallas kernels, attend_backward(): pl.pallas_call(attend_backward_kernel, grid=(pairs,), in_specs=pair_specs...  36.9 us
    pallas_call x2, Pallas kernels, ffn_backward(): pl.pallas_call(ffn_backward_kernel, grid=(2 * WIDE // tile,), in_specs=[h...  30.5 us
    ppermute x17, starting transfers between devices, pieces_shift(): lax.ppermute(value, axis, shift_perm(count, step))  27.4 us
    pallas_call x2, Pallas kernels, attend_forward(): pl.pallas_call(attend_forward_kernel, grid=(pairs,), in_specs=pair_specs(...  24.3 us
  transfers between devices with their start and end apart: 90, of which 40 were waited for; matrix products, arithmetic and copies ran while one was open for 20% of the time, Pallas kernels for 18%

profile of v5, /device:TPU:0, one launch (start us, length us, event | category | flops | bytes accessed | tf_op | source)
XLA Modules:
  0.0 690.5 jit_solution(2000077925295305954)
XLA Ops:
  27.9 28.0 %collective-permute-done.2.refs_2_ = bf16[256,1024]{1,0:T(8,128)(2,1)} collective-permute-done((bf16[256,1024]{1,0:T(8,128)(2,1)S(1)}, bf16[256,1024]{1,0:T(8,128)(2,1)}, u32[]{:S(2)}, u32[]{:S(2)}) %collective-permute-start.2) | collective-permute-done | bytes 524320 | tf_op jit(solution)/shard_map/ppermute | solution.py:492
  76.6 6.7 collective-permute-done.10
  87.9 5.3 collective-permute-start.16
  102.8 10.4 %collective-permute-done.17 = bf16[128,1024]{1,0:T(8,128)(2,1)S(1)} collective-permute-done((bf16[128,1024]{1,0:T(8,128)(2,1)}, bf16[128,1024]{1,0:T(8,128)(2,1)S(1)}, u32[]{:S(2)}, u32[]{:S(2)}) %collective-permute-start.17) | collective-permute-done | bytes 262176 | tf_op jit(solution)/shard_map/ppermute | solution.py:426
  113.3 6.9 %collective-permute-done.15 = bf16[2,256,512]{2,1,0:T(8,128)(2,1)S(1)} collective-permute-done((bf16[2,256,512]{2,1,0:T(8,128)(2,1)}, bf16[2,256,512]{2,1,0:T(8,128)(2,1)S(1)}, u32[]{:S(2)}, u32[]{:S(2)}) %collective-permute-start.15) | collective-permute-done | bytes 524320 | tf_op jit(solution)/shard_map/ppermute | solution.py:426
  148.5 12.2 %shard_map.221 = (bf16[1024,256]{1,0:T(8,128)(2,1)}, f32[16,1024]{1,0:T(8,128)}) custom-call(bf16[1024,512]{1,0:T(8,128)(2,1)} %get-tuple-element.117.q_ref.k_ref, bf16[1024,512]{1,0:T(8,128)(2,1)} %get-tuple-element.117.q_ref.k_ref, bf16[1024,256]{1,0:T(8,128)(2,1)} %get-tuple-element.118.v_ref, s32[1024,1]{1,0:T(8,128)} %copy.191.col_ref, s32[1,1024]{1,0:T(1,128)} %bitcast.403), custom_call_target="tpu_custom_call" | custom-call | flops 4294967296 | bytes 2621440 | tf_op jit(solution)/shard_map/pallas_call | solution.py:85
  160.7 5.6 all-to-all-done.1
  176.6 7.5 %collective-permute-done.24 = bf16[256,1024]{1,0:T(8,128)(2,1)} collective-permute-done((bf16[256,1024]{1,0:T(8,128)(2,1)S(1)}, bf16[256,1024]{1,0:T(8,128)(2,1)}, u32[]{:S(2)}, u32[]{:S(2)}) %collective-permute-start.24) | collective-permute-done | bytes 524320 | tf_op jit(solution)/shard_map/ppermute | solution.py:426
  187.9 8.5 %collective-permute-done.22 = bf16[256,1024]{1,0:T(8,128)(2,1)S(1)} collective-permute-done((bf16[256,1024]{1,0:T(8,128)(2,1)}, bf16[256,1024]{1,0:T(8,128)(2,1)S(1)}, u32[]{:S(2)}, u32[]{:S(2)}) %collective-permute-start.22) | collective-permute-done | bytes 524320 | tf_op jit(solution)/shard_map/ppermute | solution.py:507
  203.0 9.1 %collective-permute-done.33 = bf16[256,512]{1,0:T(8,128)(2,1)S(1)} collective-permute-done((bf16[256,512]{1,0:T(8,128)(2,1)}, bf16[256,512]{1,0:T(8,128)(2,1)S(1)}, u32[]{:S(2)}, u32[]{:S(2)}) %collective-permute-start.33) | collective-permute-done | bytes 262176 | tf_op jit(solution)/shard_map/ppermute | solution.py:426
  213.6 11.9 %shard_map.222 = (f32[256,1024]{1,0:T(8,128)}, bf16[256,1024]{1,0:T(8,128)(2,1)}, bf16[2048,512]{1,0:T(8,128)(2,1)}, f32[512,2048]{1,0:T(8,128)}, bf16[1024,512]{1,0:T(8,128)(2,1)}) custom-call(bf16[256,1024]{1,0:T(8,128)(2,1)} %copy-done.43, bf16[256,1024]{1,0:T(8,128)(2,1)} %collective-permute-done.26.x1_ref, ...), custom_call_target="tpu_custom_call" | custom-call | flops 4294967296 | bytes 25165824 | tf_op jit(solution)/shard_map/pallas_call | solution.py:219
  251.1 6.9 %collective-permute-done.32 = bf16[2,256,512]{2,1,0:T(8,128)(2,1)} collective-permute-done((bf16[2,256,512]{2,1,0:T(8,128)(2,1)S(1)}, bf16[2,256,512]{2,1,0:T(8,128)(2,1)}, u32[]{:S(2)}, u32[]{:S(2)}) %collective-permute-start.32) | collective-permute-done | bytes 524320 | tf_op jit(solution)/shard_map/ppermute | solution.py:426
  260.2 5.4 shard_map.223
  265.5 12.1 %shard_map.224 = (bf16[1024,256]{1,0:T(8,128)(2,1)}, f32[16,1024]{1,0:T(8,128)}) custom-call(bf16[1024,512]{1,0:T(8,128)(2,1)} %get-tuple-element.133.q_ref.k_ref, bf16[1024,512]{1,0:T(8,128)(2,1)} %get-tuple-element.133.q_ref.k_ref, bf16[1024,256]{1,0:T(8,128)(2,1)} %get-tuple-element.134.v_ref, s32[1024,1]{1,0:T(8,128)} %copy.191.col_ref, s32[1,1024]{1,0:T(1,128)} %bitcast.404), custom_call_target="tpu_custom_call" | custom-call | flops 4294967296 | bytes 2621440 | tf_op jit(solution)/shard_map/pallas_call | solution.py:85
  286.2 14.8 %collective-permute-done.37 = bf16[256,1024]{1,0:T(8,128)(2,1)S(1)} collective-permute-done((bf16[256,1024]{1,0:T(8,128)(2,1)S(1)}, bf16[256,1024]{1,0:T(8,128)(2,1)S(1)}, u32[]{:S(2)}, u32[]{:S(2)}) %collective-permute-start.37) | collective-permute-done | bytes 524320 | tf_op jit(solution)/shard_map/ppermute | solution.py:507
  306.0 11.6 %shard_map.225 = (f32[256,1024]{1,0:T(8,128)}, bf16[256,1024]{1,0:T(8,128)(2,1)}, bf16[2048,512]{1,0:T(8,128)(2,1)}, f32[512,2048]{1,0:T(8,128)}, bf16[1024,512]{1,0:T(8,128)(2,1)}) custom-call(bf16[256,1024]{1,0:T(8,128)(2,1)} %fusion.23.x0_ref, bf16[256,1024]{1,0:T(8,128)(2,1)} %collective-permute-done.38.x1_ref, ...), custom_call_target="tpu_custom_call" | custom-call | flops 4294967296 | bytes 25165824 | tf_op jit(solution)/shard_map/pallas_call | solution.py:219
  327.5 15.1 %shard_map.226 = (f32[256,1024]{1,0:T(8,128)}, bf16[256,1024]{1,0:T(8,128)(2,1)}, f32[1,2048]{1,0:T(1,128)}, bf16[16,128,1024]{2,1,0:T(8,128)(2,1)}, bf16[16,128,1024]{2,1,0:T(8,128)(2,1)}) custom-call(bf16[256,1024]{1,0:T(8,128)(2,1)} %copy-done.41, bf16[256,1024]{1,0:T(8,128)(2,1)} %copy-done.66, bf16[1024,512]{1,0:T(8,128)(2,1)} %get-tuple-element.143.xt_ref, ...), custom_call_target="tpu_custom_call" | custom-call | flops 8589934592 | bytes 44040192 | tf_op jit(solution)/shard_map/pallas_call | solution.py:295
  350.3 12.9 %collective-permute-done.44.refs_2_ = bf16[256,1024]{1,0:T(8,128)(2,1)S(1)} collective-permute-done((bf16[256,1024]{1,0:T(8,128)(2,1)S(1)}, bf16[256,1024]{1,0:T(8,128)(2,1)S(1)}, u32[]{:S(2)}, u32[]{:S(2)}) %collective-permute-start.44) | collective-permute-done | bytes 524320 | tf_op jit(solution)/shard_map/ppermute | solution.py:492
  371.9 18.4 %shard_map.228 = (bf16[1024,512]{1,0:T(8,128)(2,1)}, bf16[1024,256]{1,0:T(8,128)(2,1)}) custom-call(bf16[1024,512]{1,0:T(8,128)(2,1)} %get-tuple-element.133.q_ref.k_ref, bf16[1024,512]{1,0:T(8,128)(2,1)} %get-tuple-element.133.q_ref.k_ref, bf16[1024,256]{1,0:T(8,128)(2,1)} %get-tuple-element.134.v_ref, bf16[1024,256]{1,0:T(8,128)(2,1)} %get-tuple-element.148.g_ref, ...), custom_call_target="tpu_custom_call" | custom-call | flops 10737418240 | bytes 4718592 | tf_op jit(solution)/shard_map/pallas_call | solution.py:142
  390.3 7.8 %shard_map.229 = (bf16[1024,512]{1,0:T(8,128)(2,1)}, bf16[1024,256]{1,0:T(8,128)(2,1)}, f32[2,256,1024]{2,1,0:T(8,128)}, bf16[2,256,1024]{2,1,0:T(8,128)(2,1)}) custom-call(bf16[256,1024]{1,0:T(8,128)(2,1)} %fusion.22.refs_0_, bf16[256,1024]{1,0:T(8,128)(2,1)} %collective-permute-done.28.refs_1_, bf16[256,1024]{1,0:T(8,128)(2,1)} %collective-permute-done.29.refs_2_, ...), custom_call_target="tpu_custom_call" | custom-call | flops 3221225472 | bytes 11534336 | tf_op jit(solution)/shard_map/pallas_call | solution.py:372
  416.0 9.3 %collective-permute-done.49 = bf16[256,1024]{1,0:T(8,128)(2,1)} collective-permute-done((bf16[256,1024]{1,0:T(8,128)(2,1)}, bf16[256,1024]{1,0:T(8,128)(2,1)}, u32[]{:S(2)}, u32[]{:S(2)}) %collective-permute-start.49) | collective-permute-done | bytes 524320 | tf_op jit(solution)/shard_map/ppermute | solution.py:507
  428.9 8.8 %collective-permute-done.51 = bf16[2,256,512]{2,1,0:T(8,128)(2,1)} collective-permute-done((bf16[2,256,512]{2,1,0:T(8,128)(2,1)}, bf16[2,256,512]{2,1,0:T(8,128)(2,1)}, u32[]{:S(2)}, u32[]{:S(2)}) %collective-permute-start.51) | collective-permute-done | bytes 524320 | tf_op jit(solution)/shard_map/ppermute | solution.py:448
  441.7 15.5 %shard_map.230 = (f32[256,1024]{1,0:T(8,128)}, bf16[256,1024]{1,0:T(8,128)(2,1)}, f32[1,2048]{1,0:T(1,128)}, bf16[16,128,1024]{2,1,0:T(8,128)(2,1)}, bf16[16,128,1024]{2,1,0:T(8,128)(2,1)}) custom-call(bf16[256,1024]{1,0:T(8,128)(2,1)} %copy-done.39, bf16[256,1024]{1,0:T(8,128)(2,1)} %copy-done.63, bf16[1024,512]{1,0:T(8,128)(2,1)} %get-tuple-element.162.xt_ref, ...), custom_call_target="tpu_custom_call" | custom-call | flops 8589934592 | bytes 44040192 | tf_op jit(solution)/shard_map/pallas_call | solution.py:295
  474.4 8.0 %collective-permute-done.55.refs_2_ = bf16[256,1024]{1,0:T(8,128)(2,1)} collective-permute-done((bf16[256,1024]{1,0:T(8,128)(2,1)}, bf16[256,1024]{1,0:T(8,128)(2,1)}, u32[]{:S(2)}, u32[]{:S(2)}) %collective-permute-start.55) | collective-permute-done | bytes 524320 | tf_op jit(solution)/shard_map/ppermute | solution.py:492
  494.3 18.5 %shard_map.232 = (bf16[1024,512]{1,0:T(8,128)(2,1)}, bf16[1024,256]{1,0:T(8,128)(2,1)}) custom-call(bf16[1024,512]{1,0:T(8,128)(2,1)} %get-tuple-element.117.q_ref.k_ref, bf16[1024,512]{1,0:T(8,128)(2,1)} %get-tuple-element.117.q_ref.k_ref, bf16[1024,256]{1,0:T(8,128)(2,1)} %get-tuple-element.118.v_ref, bf16[1024,256]{1,0:T(8,128)(2,1)} %get-tuple-element.173.g_ref, ...), custom_call_target="tpu_custom_call" | custom-call | flops 10737418240 | bytes 4718592 | tf_op jit(solution)/shard_map/pallas_call | solution.py:142
  524.8 7.8 %shard_map.233 = (bf16[1024,512]{1,0:T(8,128)(2,1)}, bf16[1024,256]{1,0:T(8,128)(2,1)}, f32[2,256,1024]{2,1,0:T(8,128)}, bf16[2,256,1024]{2,1,0:T(8,128)(2,1)}) custom-call(bf16[256,1024]{1,0:T(8,128)(2,1)} %copy-done.42, bf16[256,1024]{1,0:T(8,128)(2,1)} %copy-done.61, bf16[256,1024]{1,0:T(8,128)(2,1)} %collective-permute-done.2.refs_2_, ...), custom_call_target="tpu_custom_call" | custom-call | flops 3221225472 | bytes 11534336 | tf_op jit(solution)/shard_map/pallas_call | solution.py:372
  543.4 21.1 %collective-permute-done.65 = bf16[2,256,512]{2,1,0:T(8,128)(2,1)} collective-permute-done((bf16[2,256,512]{2,1,0:T(8,128)(2,1)}, bf16[2,256,512]{2,1,0:T(8,128)(2,1)}, u32[]{:S(2)}, u32[]{:S(2)}) %collective-permute-start.65) | collective-permute-done | bytes 524320 | tf_op jit(solution)/shard_map/ppermute | solution.py:448
  574.9 5.9 collective-permute-done.64
  600.0 7.6 %collective-permute-done.73 = bf16[128,1024]{1,0:T(8,128)(2,1)S(1)} collective-permute-done((bf16[128,1024]{1,0:T(8,128)(2,1)S(1)}, bf16[128,1024]{1,0:T(8,128)(2,1)S(1)}, u32[]{:S(2)}, u32[]{:S(2)}) %collective-permute-start.73) | collective-permute-done | bytes 262176 | tf_op jit(solution)/shard_map/ppermute | solution.py:448
  613.4 16.2 %collective-permute-done.70 = bf16[128,1024]{1,0:T(8,128)(2,1)S(1)} collective-permute-done((bf16[128,1024]{1,0:T(8,128)(2,1)S(1)}, bf16[128,1024]{1,0:T(8,128)(2,1)S(1)}, u32[]{:S(2)}, u32[]{:S(2)}) %collective-permute-start.70) | collective-permute-done | bytes 262176 | tf_op jit(solution)/shard_map/ppermute | solution.py:448
  630.7 12.9 %collective-permute-done.75 = bf16[128,1024]{1,0:T(8,128)(2,1)} collective-permute-done((bf16[128,1024]{1,0:T(8,128)(2,1)}, bf16[128,1024]{1,0:T(8,128)(2,1)}, u32[]{:S(2)}, u32[]{:S(2)}) %collective-permute-start.75) | collective-permute-done | bytes 262176 | tf_op jit(solution)/shard_map/ppermute | solution.py:560
  660.7 15.9 %all-to-all-done.5 = bf16[8,32,2176]{2,1,0:T(8,128)(2,1)S(1)} async-done(((bf16[8,32,2176]{2,1,0:T(8,128)(2,1)}), bf16[8,32,2176]{2,1,0:T(8,128)(2,1)S(1)}, u32[]{:S(2)}, u32[]{:S(2)}) %all-to-all-start.5) | async-done | bytes 1114144 | tf_op jit(solution)/shard_map/all_to_all | solution.py:720
  (605 shorter events, 309.7 us)
Async XLA Ops:
  13.1 43.6 %collective-permute-start.4 = (s32[128]{0:T(128)S(1)}, s32[128]{0:T(128)S(1)}, u32[]{:S(2)}, u32[]{:S(2)}) collective-permute-start(s32[128]{0:T(128)S(1)} %fusion.46), channel_id=1, source_target_pairs={{0,4},{4,0},{1,5},{5,1},{2,6},{6,2},{3,7},{7,3},{8,12},{12,8},{9,1... | collective-permute-start | bytes 1544 | tf_op jit(solution)/shard_map/ppermute | solution.py:553
  18.2 43.4 %all-to-all-start = ((bf16[8,32,2176]{2,1,0:T(8,128)(2,1)}), bf16[8,32,2176]{2,1,0:T(8,128)(2,1)S(1)}, u32[]{:S(2)}, u32[]{:S(2)}) async-start(bf16[8,32,2176]{2,1,0:T(8,128)(2,1)} %bitcast.12), calls=%async_computation | async-start | bytes 2228224 | tf_op jit(solution)/shard_map/all_to_all | solution.py:595
  23.4 190.2 %all-gather.4.cloned.1.call-start = ((), (), s32[]{:S(2)}) async-start(), calls=%async_computation.10 | async-start | bytes 5242880 | tf_op jit(solution)/shard_map/all_gather | solution.py:626
  25.1 30.8 %collective-permute-start.2 = (bf16[256,1024]{1,0:T(8,128)(2,1)S(1)}, bf16[256,1024]{1,0:T(8,128)(2,1)}, u32[]{:S(2)}, u32[]{:S(2)}) collective-permute-start(bf16[256,1024]{1,0:T(8,128)(2,1)S(1)} %pad_maximum_fusion.6.refs_0_), channel_id=1, source_target_pairs={{0,2},{2,0},{1,3},{3,1},{4,6},{6,4},{5,7},{7,5},{8,10},{10,8},{9,1... | collective-permute-start | bytes 1572872 | tf_op jit(solution)/shard_map/ppermute | solution.py:492
  27.1 33.3 %collective-permute-start.8 = (bf16[2,32,1024]{2,0,1:T(2,128)(2,1)S(1)}, bf16[2,32,1024]{2,0,1:T(2,128)(2,1)S(1)}, u32[]{:S(2)}, u32[]{:S(2)}) collective-permute-start(bf16[2,32,1024]{2,0,1:T(2,128)(2,1)S(1)} %bitcast.399), channel_id=1, source_target_pairs={{0,1},{1,0},{2,3},{3,2},{4,5},{5,4},{6,7},{7,6},{8,9},{9,8},{10,11... | collective-permute-start | bytes 393224 | tf_op jit(solution)/shard_map/ppermute | solution.py:422
  27.3 34.2 %collective-permute-start.1 = (bf16[256,1024]{1,0:T(8,128)(2,1)S(1)}, bf16[256,1024]{1,0:T(8,128)(2,1)S(1)}, u32[]{:S(2)}, u32[]{:S(2)}) collective-permute-start(bf16[256,1024]{1,0:T(8,128)(2,1)S(1)} %pad_maximum_fusion.6.refs_0_), channel_id=1, source_target_pairs={{0,1},{1,0},{2,3},{3,2},{4,5},{5,4},{6,7},{7,6},{8,9},{9,8},{10,11... | collective-permute-start | bytes 1572872 | tf_op jit(solution)/shard_map/ppermute | solution.py:422
  84.4 129.2 %all-gather.6.cloned.1.call-start = ((), (), s32[]{:S(2)}) async-start(), calls=%async_computation.11 | async-start | bytes 5242880 | tf_op jit(solution)/shard_map/all_gather | solution.py:626
  97.4 27.5 %collective-permute-start.14 = (bf16[2,256,640]{2,1,0:T(8,128)(2,1)}, bf16[2,256,640]{2,1,0:T(8,128)(2,1)}, u32[]{:S(2)}, u32[]{:S(2)}) collective-permute-start(bf16[2,256,640]{2,1,0:T(8,128)(2,1)} %bitcast_dynamic-update-slice_fusion.12), channel_id=1, source_target_pairs={{0,8},{8,0},{1,9},{9,1},{2,10},{10,2},{3,11},{11,3},{4,12},{12,4},... | collective-permute-start | bytes 1966088 | tf_op jit(solution)/shard_map/ppermute | solution.py:426
  139.0 27.3 %all-to-all-start.1 = ((bf16[4,256,256]{2,1,0:T(8,128)(2,1)}), bf16[4,256,256]{2,1,0:T(8,128)(2,1)S(1)}, u32[]{:S(2)}, u32[]{:S(2)}) async-start(bf16[4,256,256]{2,1,0:T(8,128)(2,1)} %bitcast.47), calls=%async_computation.1 | async-start | bytes 1048576 | tf_op jit(solution)/shard_map/all_to_all | solution.py:610
  142.6 163.4 %all-gather.8.cloned.1.call-start = ((), (), s32[]{:S(2)}) async-start(), calls=%async_computation.12 | async-start | bytes 10485760 | tf_op jit(solution)/shard_map/all_gather | solution.py:626
  143.8 30.9 %collective-permute-start.23 = (bf16[256,1024]{1,0:T(8,128)(2,1)S(1)}, bf16[256,1024]{1,0:T(8,128)(2,1)}, u32[]{:S(2)}, u32[]{:S(2)}) collective-permute-start(bf16[256,1024]{1,0:T(8,128)(2,1)S(1)} %constant_dynamic-update-slice_fusion.4), channel_id=1, source_target_pairs={{0,2},{2,4},{4,6},{6,0},{1,3},{3,5},{5,7},{7,1},{8,10},{10,12},{12... | collective-permute-start | bytes 1572872 | tf_op jit(solution)/shard_map/ppermute | solution.py:426
  145.8 38.3 %collective-permute-start.24 = (bf16[256,1024]{1,0:T(8,128)(2,1)S(1)}, bf16[256,1024]{1,0:T(8,128)(2,1)}, u32[]{:S(2)}, u32[]{:S(2)}) collective-permute-start(bf16[256,1024]{1,0:T(8,128)(2,1)S(1)} %constant_dynamic-update-slice_fusion.4), channel_id=1, source_target_pairs={{0,4},{2,6},{4,0},{6,2},{1,5},{3,7},{5,1},{7,3},{8,12},{10,14},{12... | collective-permute-start | bytes 1572872 | tf_op jit(solution)/shard_map/ppermute | solution.py:426
  147.2 38.8 %collective-permute-start.25 = (bf16[256,1024]{1,0:T(8,128)(2,1)S(1)}, bf16[256,1024]{1,0:T(8,128)(2,1)}, u32[]{:S(2)}, u32[]{:S(2)}) collective-permute-start(bf16[256,1024]{1,0:T(8,128)(2,1)S(1)} %constant_dynamic-update-slice_fusion.4), channel_id=1, source_target_pairs={{0,6},{2,0},{4,2},{6,4},{1,7},{3,1},{5,3},{7,5},{8,14},{10,8},{12,... | collective-permute-start | bytes 1572872 | tf_op jit(solution)/shard_map/ppermute | solution.py:426
  234.9 25.2 %all-to-all-start.2 = ((bf16[4,256,256]{2,1,0:T(8,128)(2,1)}), bf16[4,256,256]{2,1,0:T(8,128)(2,1)S(1)}, u32[]{:S(2)}, u32[]{:S(2)}) async-start(bf16[4,256,256]{2,1,0:T(8,128)(2,1)} %bitcast.370), calls=%async_computation.2 | async-start | bytes 1048576 | tf_op jit(solution)/shard_map/all_to_all | solution.py:610
  238.4 245.1 %reduce-scatter.5.cloned.1.call-start = ((), (), s32[]{:S(2)}) async-start(), calls=%async_computation.13 | async-start | bytes 5242880 | tf_op jit(solution)/shard_map/reduce_scatter | solution.py:752
  342.6 140.9 %reduce-scatter.7.cloned.1.call-start = ((), (), s32[]{:S(2)}) async-start(), calls=%async_computation.14 | async-start | bytes 5242880 | tf_op jit(solution)/shard_map/reduce_scatter | solution.py:752
  364.0 34.1 %collective-permute-start.46 = (bf16[128,1024]{1,0:T(8,128)(2,1)S(1)}, bf16[128,1024]{1,0:T(8,128)(2,1)S(1)}, u32[]{:S(2)}, u32[]{:S(2)}) collective-permute-start(bf16[128,1024]{1,0:T(8,128)(2,1)S(1)} %get-tuple-element.290), channel_id=1, source_target_pairs={{0,4},{4,0},{1,5},{5,1},{2,6},{6,2},{3,7},{7,3},{8,12},{12,8},{9,1... | collective-permute-start | bytes 786440 | tf_op jit(solution)/shard_map/ppermute | solution.py:560
  405.1 177.7 %reduce-scatter.11.cloned.1.call-start = ((), (), s32[]{:S(2)}) async-start(), calls=%async_computation.16 | async-start | bytes 5242880 | tf_op jit(solution)/shard_map/reduce_scatter | solution.py:752
  411.8 26.0 %collective-permute-start.51 = (bf16[2,256,512]{2,1,0:T(8,128)(2,1)}, bf16[2,256,512]{2,1,0:T(8,128)(2,1)}, u32[]{:S(2)}, u32[]{:S(2)}) collective-permute-start(bf16[2,256,512]{2,1,0:T(8,128)(2,1)} %dynamic-slice_bitcast_fusion.5), channel_id=1, source_target_pairs={{0,16},{16,0},{1,17},{17,1},{2,18},{18,2},{3,19},{19,3},{4,20},{20... | collective-permute-start | bytes 1572872 | tf_op jit(solution)/shard_map/ppermute | solution.py:448
  414.5 25.5 %collective-permute-start.52 = (bf16[2,256,512]{2,1,0:T(8,128)(2,1)S(1)}, bf16[2,256,512]{2,1,0:T(8,128)(2,1)S(1)}, u32[]{:S(2)}, u32[]{:S(2)}) collective-permute-start(bf16[2,256,512]{2,1,0:T(8,128)(2,1)S(1)} %fusion.26), channel_id=1, source_target_pairs={{0,8},{8,0},{1,9},{9,1},{2,10},{10,2},{3,11},{11,3},{4,12},{12,4},... | collective-permute-start | bytes 1572872 | tf_op jit(solution)/shard_map/ppermute | solution.py:448
  457.2 137.7 %reduce-scatter.9.cloned.1.call-start = ((), (), s32[]{:S(2)}) async-start(), calls=%async_computation.15 | async-start | bytes 5242880 | tf_op jit(solution)/shard_map/reduce_scatter | solution.py:752
  486.5 48.2 %collective-permute-start.57 = (bf16[256,1024]{1,0:T(8,128)(2,1)}, bf16[256,1024]{1,0:T(8,128)(2,1)}, u32[]{:S(2)}, u32[]{:S(2)}) collective-permute-start(bf16[256,1024]{1,0:T(8,128)(2,1)} %get-tuple-element.255), channel_id=1, source_target_pairs={{0,2},{2,4},{4,6},{6,0},{1,3},{3,5},{5,7},{7,1},{8,10},{10,12},{12... | collective-permute-start | bytes 1572872 | tf_op jit(solution)/shard_map/ppermute | solution.py:448
  486.7 48.0 %collective-permute-start.58 = (bf16[256,1024]{1,0:T(8,128)(2,1)}, bf16[256,1024]{1,0:T(8,128)(2,1)}, u32[]{:S(2)}, u32[]{:S(2)}) collective-permute-start(bf16[256,1024]{1,0:T(8,128)(2,1)} %get-tuple-element.257), channel_id=1, source_target_pairs={{0,4},{2,6},{4,0},{6,2},{1,5},{3,7},{5,1},{7,3},{8,12},{10,14},{12... | collective-permute-start | bytes 1572872 | tf_op jit(solution)/shard_map/ppermute | solution.py:448
  487.9 46.8 %collective-permute-start.59 = (bf16[256,1024]{1,0:T(8,128)(2,1)}, bf16[256,1024]{1,0:T(8,128)(2,1)}, u32[]{:S(2)}, u32[]{:S(2)}) collective-permute-start(bf16[256,1024]{1,0:T(8,128)(2,1)} %get-tuple-element.256), channel_id=1, source_target_pairs={{0,6},{2,0},{4,2},{6,4},{1,7},{3,1},{5,3},{7,5},{8,14},{10,8},{12,... | collective-permute-start | bytes 1572872 | tf_op jit(solution)/shard_map/ppermute | solution.py:448
  538.5 26.1 %collective-permute-start.65 = (bf16[2,256,512]{2,1,0:T(8,128)(2,1)}, bf16[2,256,512]{2,1,0:T(8,128)(2,1)}, u32[]{:S(2)}, u32[]{:S(2)}) collective-permute-start(bf16[2,256,512]{2,1,0:T(8,128)(2,1)} %dynamic-slice_bitcast_fusion.1), channel_id=1, source_target_pairs={{0,16},{16,0},{1,17},{17,1},{2,18},{18,2},{3,19},{19,3},{4,20},{20... | collective-permute-start | bytes 1572872 | tf_op jit(solution)/shard_map/ppermute | solution.py:448
  540.8 25.3 %collective-permute-start.63 = (bf16[256,1024]{1,0:T(8,128)(2,1)}, bf16[256,1024]{1,0:T(8,128)(2,1)}, u32[]{:S(2)}, u32[]{:S(2)}) collective-permute-start(bf16[256,1024]{1,0:T(8,128)(2,1)} %get-tuple-element.272), channel_id=1, source_target_pairs={{0,1},{1,0},{2,3},{3,2},{4,5},{5,4},{6,7},{7,6},{8,9},{9,8},{10,11... | collective-permute-start | bytes 1572872 | tf_op jit(solution)/shard_map/ppermute | solution.py:422
  540.8 34.1 %collective-permute-start.62 = (bf16[256,1024]{1,0:T(8,128)(2,1)}, bf16[256,1024]{1,0:T(8,128)(2,1)}, u32[]{:S(2)}, u32[]{:S(2)}) collective-permute-start(bf16[256,1024]{1,0:T(8,128)(2,1)} %get-tuple-element.271), channel_id=1, source_target_pairs={{0,1},{1,0},{2,3},{3,2},{4,5},{5,4},{6,7},{7,6},{8,9},{9,8},{10,11... | collective-permute-start | bytes 1572872 | tf_op jit(solution)/shard_map/ppermute | solution.py:422
  542.5 31.1 %collective-permute-start.67 = (bf16[2,256,640]{2,1,0:T(8,128)(2,1)S(1)}, bf16[2,256,640]{2,1,0:T(8,128)(2,1)S(1)}, u32[]{:S(2)}, u32[]{:S(2)}) collective-permute-start(bf16[2,256,640]{2,1,0:T(8,128)(2,1)S(1)} %dynamic-slice_bitcast_fusion), channel_id=1, source_target_pairs={{0,8},{8,0},{1,9},{9,1},{2,10},{10,2},{3,11},{11,3},{4,12},{12,4},... | collective-permute-start | bytes 1966088 | tf_op jit(solution)/shard_map/ppermute | solution.py:448
  596.1 33.4 %collective-permute-start.70 = (bf16[128,1024]{1,0:T(8,128)(2,1)S(1)}, bf16[128,1024]{1,0:T(8,128)(2,1)S(1)}, u32[]{:S(2)}, u32[]{:S(2)}) collective-permute-start(bf16[128,1024]{1,0:T(8,128)(2,1)S(1)} %get-tuple-element.278), channel_id=1, source_target_pairs={{0,4},{2,6},{4,0},{6,2},{1,5},{3,7},{5,1},{7,3},{8,12},{10,14},{12... | collective-permute-start | bytes 786440 | tf_op jit(solution)/shard_map/ppermute | solution.py:448
  598.2 31.3 %collective-permute-start.71 = (bf16[128,1024]{1,0:T(8,128)(2,1)S(1)}, bf16[128,1024]{1,0:T(8,128)(2,1)S(1)}, u32[]{:S(2)}, u32[]{:S(2)}) collective-permute-start(bf16[128,1024]{1,0:T(8,128)(2,1)S(1)} %get-tuple-element.277), channel_id=1, source_target_pairs={{0,6},{2,0},{4,2},{6,4},{1,7},{3,1},{5,3},{7,5},{8,14},{10,8},{12,... | collective-permute-start | bytes 786440 | tf_op jit(solution)/shard_map/ppermute | solution.py:448
  607.7 35.9 %collective-permute-start.75 = (bf16[128,1024]{1,0:T(8,128)(2,1)}, bf16[128,1024]{1,0:T(8,128)(2,1)}, u32[]{:S(2)}, u32[]{:S(2)}) collective-permute-start(bf16[128,1024]{1,0:T(8,128)(2,1)} %get-tuple-element.288), channel_id=1, source_target_pairs={{0,4},{4,0},{1,5},{5,1},{2,6},{6,2},{3,7},{7,3},{8,12},{12,8},{9,1... | collective-permute-start | bytes 786440 | tf_op jit(solution)/shard_map/ppermute | solution.py:560
  644.7 31.9 %all-to-all-start.5 = ((bf16[8,32,2176]{2,1,0:T(8,128)(2,1)}), bf16[8,32,2176]{2,1,0:T(8,128)(2,1)S(1)}, u32[]{:S(2)}, u32[]{:S(2)}) async-start(bf16[8,32,2176]{2,1,0:T(8,128)(2,1)} %pad_maximum_fusion.2), calls=%async_computation.9 | async-start | bytes 2228224 | tf_op jit(solution)/shard_map/all_to_all | solution.py:720
  (125 other events, 1164.5 us)
Sparse Core Ops, SparseCore 0:
  84.6 67.5 all-gather.3
  154.0 56.0 all-gather.5
  212.0 94.0 all-gather.7
  342.7 53.3 reduce-scatter.4
  399.3 63.8 reduce-scatter.6
  466.0 53.0 reduce-scatter.10
  522.3 70.7 reduce-scatter.8
